TPU v7x, 32 devices: a whole 2x2x4 slice. The times are simulated.
32 devices in a mesh: section: 2 (over core), tok: 4 (over z), head: 4 (over y, x).
Axes of the slice: x: 2, y: 2, z: 4, core: 2. Of those that a mesh axis runs over, the one named last changes fastest.
Arguments:
- block_input: bfloat16 [2, 1024, 2048], P(None, 'tok'), may hold values from -6 to 6
- out_grad: bfloat16 [2, 1024, 2048], P(None, 'tok'), may hold values from -6 to 6
- lengths: int32 [2, 4], replicated, may hold values from 1 to 1021, as said below
- norm_gain: float32 [2, 2048], P('section'), may hold values from 0.5 to 1.5
- gate_weight: bfloat16 [2, 2048, 4096], P('section', None, 'head'), may hold values from -0.125 to 0.125
- value_weight: bfloat16 [2, 2048, 4096], P('section', None, 'head'), may hold values from -0.125 to 0.125
- select_weight: bfloat16 [2, 2048, 256], P('section'), may hold values from -0.125 to 0.125
- step_weight: bfloat16 [2, 2048, 64], P('section', None, 'head'), may hold values from -0.25 to 0.25
- conv_value: float32 [2, 4, 64, 64], P('section', None, 'head'), may hold values from -3 to 3
- conv_value_bias: float32 [2, 64, 64], P('section', 'head'), may hold values from -2 to 2
- conv_select: float32 [2, 4, 256], P('section'), may hold values from -3 to 3
- conv_select_bias: float32 [2, 256], P('section'), may hold values from -2 to 2
- step_bias: float32 [2, 64], P('section', 'head'), may hold values from -6 to -2
- log_rate: float32 [2, 64], P('section', 'head'), may hold values from -8 to 1.5
- skip_gain: float32 [2, 64], P('section', 'head'), may hold values from 0.5 to 1.5
- gate_gain: float32 [2, 64, 64], P('section', 'head'), may hold values from 0.5 to 1.5
- output_weight: bfloat16 [2, 4096, 2048], P('section', 'head'), may hold values from -0.09375 to 0.09375
Outputs:
- layer_out: float32 [2, 2, 1024, 2048], P('section', None, 'tok')
- input_grad: float32 [2, 2, 1024, 2048], P('section', None, 'tok')
- norm_gain_grad: float32 [2, 2048], P('section', 'tok')
- gate_weight_grad: float32 [2, 2048, 4096], P('section', 'tok', 'head')
- value_weight_grad: float32 [2, 2048, 4096], P('section', 'tok', 'head')
- select_weight_grad: float32 [2, 2048, 256], P('section', 'tok')
- step_weight_grad: float32 [2, 2048, 64], P('section', 'tok', 'head')
- conv_value_grad: float32 [2, 4, 64, 64], P('section', None, 'head', 'tok')
- conv_value_bias_grad: float32 [2, 64, 64], P('section', 'head', 'tok')
- conv_select_grad: float32 [2, 4, 256], P('section', None, 'tok')
- conv_select_bias_grad: float32 [2, 256], P('section', 'tok')
- step_bias_grad: float32 [2, 64], P('section', 'head')
- log_rate_grad: float32 [2, 64], P('section', 'head')
- skip_gain_grad: float32 [2, 64], P('section', 'head')
- gate_gain_grad: float32 [2, 64, 64], P('section', 'head', 'tok')
- output_weight_grad: float32 [2, 4096, 2048], P('section', 'head', 'tok')
Inputs may be any that keep to these rules, and one draw needn't show every extreme that they name: Each row lists the lengths of 4 sequences packed in order into the 1024 rows of a micro-batch and sums to 1024; one of them, at a place drawn anew, holds all but fewer than 256 rows, so it starts in the first 256 rows and ends in the last 256 rows; in one micro-batch all others have length 1.
All inputs are finite; a program needn't handle non-finite values.
Results may differ from a plain program's by a relative error of at most 0.012.
The roundings to bfloat16 on the way count: a program that leaves them out, or rounds other values in their place, can miss the bound.
Values sent between devices are 32-bit elements; how exact they have to be, the bound alone decides.
No kernel may reach another device: no remote copies, remote signals or barrier semaphores. Data moves between devices by JAX's collectives and lax.ppermute only.
A program may use at most 192 MiB of HBM per device.

v0:
```python
from functools import partial

import jax
import jax.numpy as jnp
from jax import lax
from jax.sharding import PartitionSpec as P

D = 2048
H = 64
P_SIZE = 64
NST = 128
K = 4
BLOCK = 256
MICRO = 2


EPSILON = 1e-05
PRECISE = lax.Precision.HIGHEST


def shifted(value, axis, steps):
    count = lax.axis_size(axis)
    leading, last = (max(0, -steps), min(count, count - steps))
    return lax.ppermute(value, axis, [(source, source + steps) for source in range(leading, last)])


def entering_2(value, axis, join, neutral, backward):
    count, mine = (lax.axis_size(axis), lax.axis_index(axis))
    pieces = jax.tree.map(lambda part: lax.all_gather(part, axis), value)
    if backward:
        pieces = jax.tree.map(lambda part: part[::-1], pieces)
        mine = count - 1 - mine
    subtotal = jax.tree.map(
        lambda part, zero: jnp.full_like(part, 0) + jnp.asarray(zero, part.dtype), value, neutral
    )

    def turn(position, subtotal):
        longer = join(subtotal, jax.tree.map(lambda part: part[position], pieces))
        return jax.tree.map(lambda new, old: jnp.where(position < mine, new, old), longer, subtotal)

    return lax.fori_loop(0, count - 1, turn, subtotal)


def seg_of(points, seq_ends):
    inside = jnp.sum((points[:, None] >= seq_ends[None, :]).astype(jnp.int32), axis=1)
    return jnp.where(points >= 0, inside, -1)


def chain_state(earlier, later_part):
    return (earlier[0] * later_part[0], later_part[0][:, None, None] * earlier[1] + later_part[1])


def ssd_blocks(x_act, b_act, c_act, step_size, log_decay, segment, seg_prev, start_state):
    block_count = x_act.shape[0] // BLOCK
    heads_here = log_decay.shape[1]
    block_items = (
        x_act.reshape(block_count, BLOCK, heads_here, P_SIZE),
        b_act.reshape(block_count, BLOCK, NST),
        c_act.reshape(block_count, BLOCK, NST),
        step_size.reshape(block_count, BLOCK, heads_here),
        log_decay.reshape(block_count, BLOCK, heads_here),
        segment.reshape(block_count, BLOCK),
        seg_prev.reshape(block_count, BLOCK)[:, 0],
    )

    def one_block(carried, items):
        x_rows, b_rows, c_rows, step_rows, decay_rows, seg_rows, seg_before = items
        cum_decay = jnp.cumsum(decay_rows, axis=0)
        row_ids = jnp.arange(BLOCK)
        mask_rows = (
            (seg_rows[:, None] == seg_rows[None, :]) & (row_ids[:, None] >= row_ids[None, :])
        ).astype(jnp.float32)
        cum_heads = cum_decay.T
        decay_matrix = (
            jnp.exp(
                jnp.where(mask_rows[None] > 0, cum_heads[:, :, None] - cum_heads[:, None, :], 0.0)
            )
            * mask_rows[None]
        )
        scores = jnp.dot(c_rows, b_rows.T, precision=PRECISE)
        mixing = decay_matrix * scores[None] * step_rows.T[:, None, :]
        block_out = jnp.einsum("hts,shp->thp", mixing, x_rows, precision=PRECISE)
        carry_in = (seg_rows == seg_before).astype(jnp.float32)
        decay_in = jnp.exp(cum_decay) * carry_in[:, None]
        block_out = (
            block_out
            + jnp.einsum("tn,hpn->thp", c_rows, carried, precision=PRECISE) * decay_in[:, :, None]
        )
        tail_mask = (seg_rows == seg_rows[-1]).astype(jnp.float32)
        end_weight = jnp.exp(cum_decay[-1][None, :] - cum_decay) * tail_mask[:, None] * step_rows
        fresh_state = carried * decay_in[-1][:, None, None] + jnp.einsum(
            "sh,sn,shp->hpn", end_weight, b_rows, x_rows, precision=PRECISE
        )
        return (fresh_state, block_out)

    last_state, outputs = lax.scan(one_block, start_state, block_items)
    return (outputs.reshape(x_act.shape[0], heads_here * P_SIZE), last_state)


def device_decay(log_decay, segment, seg_prev):
    carry_mask = (segment == seg_prev[0]).astype(jnp.float32)
    return jnp.exp(jnp.cumsum(log_decay, axis=0)) * carry_mask[:, None]


def entering_term(c_act, entering, dev_decay):
    row_count = c_act.shape[0]
    term_value = (
        jnp.einsum("tn,hpn->thp", c_act, entering, precision=PRECISE) * dev_decay[:, :, None]
    )
    return term_value.reshape(row_count, -1)


def ssd_device(segment, seg_prev, x_act, b_act, c_act, step_size, log_decay, entering):
    heads_here = log_decay.shape[1]
    y_local, s_local = ssd_blocks(
        x_act,
        b_act,
        c_act,
        step_size,
        log_decay,
        segment,
        seg_prev,
        jnp.zeros((heads_here, P_SIZE, NST), jnp.float32),
    )
    dev_decay = device_decay(log_decay, segment, seg_prev)
    return (
        y_local + entering_term(c_act, entering, dev_decay),
        dev_decay[-1][:, None, None] * entering + s_local,
    )


def context_of(lens_row, row_count):
    positions = lax.axis_index("tok") * row_count + jnp.arange(row_count, dtype=jnp.int32)
    seq_ends = jnp.cumsum(lens_row)
    segment = seg_of(positions, seq_ends)
    seg_prev = seg_of(positions - 1, seq_ends)
    tap_masks = jnp.stack(
        [
            (seg_of(positions - (K - 1 - tap_index), seq_ends) == segment).astype(jnp.float32)
            for tap_index in range(K)
        ]
    )
    return (segment, seg_prev, tap_masks)


def normalize(hidden_in, norm_gain):
    inv_rms = lax.rsqrt(jnp.mean(hidden_in * hidden_in, axis=-1, keepdims=True) + EPSILON)
    return (inv_rms, (hidden_in * inv_rms * norm_gain).astype(jnp.bfloat16))


def in_products(normed, weights):
    return tuple(
        (
            jnp.dot(normed, weights[weight_index], preferred_element_type=jnp.float32)
            for weight_index in (1, 2, 3, 4)
        )
    )


def conv_tables(weights):
    value_width = weights[6].size
    kernel = jnp.concatenate([weights[5].reshape(K, value_width), weights[7]], axis=1)
    kernel_bias = jnp.concatenate([weights[6].reshape(value_width), weights[8]])
    return (kernel, kernel_bias)


def conv_apply(extended, kernel, kernel_bias, tap_masks):
    row_count = tap_masks.shape[1]
    conv_total = jnp.broadcast_to(kernel_bias[None, :], (row_count, kernel_bias.shape[0]))
    for tap_index in range(K):
        conv_total = (
            conv_total
            + kernel[tap_index][None, :]
            * extended[tap_index : tap_index + row_count]
            * tap_masks[tap_index][:, None]
        )
    return conv_total


def activate(conv_total, step_pre, weights, value_width):
    activated = jax.nn.silu(conv_total)
    step_size = jax.nn.softplus(step_pre + weights[9])
    log_decay = -jnp.exp(weights[10]) * step_size
    return (
        activated[:, :value_width],
        activated[:, value_width : value_width + NST],
        activated[:, value_width + NST :],
        step_size,
        log_decay,
    )


def silu_slope(values):
    sigmoid_value = jax.nn.sigmoid(values)
    return sigmoid_value * (1.0 + values * (1.0 - sigmoid_value))


def skip_term(x_act, skip_gain):
    row_count = x_act.shape[0]
    return (
        x_act.reshape(row_count, skip_gain.shape[0], P_SIZE) * skip_gain[None, :, None]
    ).reshape(row_count, -1)


def contract_rows(left_side, right_side):
    return lax.dot_general(
        left_side, right_side, (((0,), (0,)), ((), ())), preferred_element_type=jnp.float32
    )


def contract_cols(left_side, right_side):
    return lax.dot_general(
        left_side, right_side, (((1,), (1,)), ((), ())), preferred_element_type=jnp.float32
    )


def forward_layer(hidden_in, context_info, weights):
    segment, seg_prev, tap_masks = context_info
    row_count = hidden_in.shape[0]
    inv_rms, normed = normalize(hidden_in, weights[0])
    projections = in_products(normed, weights)
    gate_pre, value_pre, select_pre, step_pre = projections
    value_width = value_pre.shape[1]
    conv_input = jnp.concatenate([value_pre, select_pre], axis=1)
    halo_rows = shifted(conv_input[row_count - (K - 1) :], "tok", 1)
    kernel, kernel_bias = conv_tables(weights)
    conv_total = conv_apply(
        jnp.concatenate([halo_rows, conv_input], axis=0), kernel, kernel_bias, tap_masks
    )
    x_act, b_act, c_act, step_size, log_decay = activate(conv_total, step_pre, weights, value_width)
    heads_here = log_decay.shape[1]
    y_local, s_local = ssd_blocks(
        x_act,
        b_act,
        c_act,
        step_size,
        log_decay,
        segment,
        seg_prev,
        jnp.zeros((heads_here, P_SIZE, NST), jnp.float32),
    )
    dev_decay = device_decay(log_decay, segment, seg_prev)
    carried_decay, entering = entering_2(
        (dev_decay[-1], s_local),
        "tok",
        chain_state,
        (jnp.ones((heads_here,), jnp.float32), jnp.zeros_like(s_local)),
        False,
    )
    scan_out = y_local + entering_term(c_act, entering, dev_decay) + skip_term(x_act, weights[11])
    gated_value = scan_out * jax.nn.silu(gate_pre)
    square_sum = lax.psum(jnp.sum(gated_value * gated_value, axis=-1), "head")
    inv_gate = lax.rsqrt(square_sum / (H * P_SIZE) + EPSILON)[:, None]
    scaled = (gated_value * inv_gate * weights[12].reshape(value_width)).astype(jnp.bfloat16)
    branch = lax.psum(jnp.dot(scaled, weights[13], preferred_element_type=jnp.float32), "head")
    return (hidden_in + branch, (halo_rows, entering, square_sum), projections)


def backward_layer(hidden_in, grad_out, context_info, weights, saved_items):
    segment, seg_prev, tap_masks = context_info
    halo_rows, entering, square_sum = saved_items
    row_count = hidden_in.shape[0]
    inv_rms, normed = normalize(hidden_in, weights[0])
    projections = in_products(normed, weights)
    gate_pre, value_pre, select_pre, step_pre = projections
    value_width = value_pre.shape[1]
    conv_input = jnp.concatenate([value_pre, select_pre], axis=1)
    kernel, kernel_bias = conv_tables(weights)
    extended = jnp.concatenate([halo_rows, conv_input], axis=0)
    conv_total = conv_apply(extended, kernel, kernel_bias, tap_masks)
    x_act, b_act, c_act, step_size, log_decay = activate(conv_total, step_pre, weights, value_width)
    heads_here = log_decay.shape[1]
    (core_out, leaving), pullback = jax.vjp(
        partial(ssd_device, segment, seg_prev), x_act, b_act, c_act, step_size, log_decay, entering
    )
    scan_out = core_out + skip_term(x_act, weights[11])
    gate_act = jax.nn.silu(gate_pre)
    gated_value = scan_out * gate_act
    inv_gate = lax.rsqrt(square_sum / (H * P_SIZE) + EPSILON)[:, None]
    gain_flat = weights[12].reshape(value_width)
    scaled = (gated_value * inv_gate * gain_flat).astype(jnp.bfloat16)
    grad_branch = grad_out.astype(jnp.bfloat16)
    output_grad = contract_rows(scaled, grad_branch)
    grad_scaled = contract_cols(grad_branch, weights[13])
    gate_gain_grad = jnp.sum(grad_scaled * gated_value * inv_gate, axis=0).reshape(
        weights[12].shape
    )
    weighted = grad_scaled * gain_flat
    inner_sum = lax.psum(jnp.sum(weighted * gated_value, axis=-1), "head")
    grad_gated = (
        inv_gate * weighted - gated_value * inv_gate**3 * (inner_sum / (H * P_SIZE))[:, None]
    )
    grad_scan = grad_gated * gate_act
    grad_gate_pre = (grad_gated * scan_out * silu_slope(gate_pre)).astype(jnp.bfloat16)
    skip_gain_grad = jnp.sum(
        grad_scan.reshape(row_count, heads_here, P_SIZE)
        * x_act.reshape(row_count, heads_here, P_SIZE),
        axis=(0, 2),
    )
    dev_decay = device_decay(log_decay, segment, seg_prev)
    entering_grad = jnp.einsum(
        "tn,thp,th->hpn",
        c_act,
        grad_scan.reshape(row_count, heads_here, P_SIZE),
        dev_decay,
        precision=PRECISE,
    )
    carried_decay, later_grad = entering_2(
        (dev_decay[-1], entering_grad),
        "tok",
        chain_state,
        (jnp.ones((heads_here,), jnp.float32), jnp.zeros_like(entering)),
        True,
    )
    pulled = pullback((grad_scan, later_grad))
    grad_x = pulled[0] + skip_term(grad_scan, weights[11])
    grad_b = pulled[1]
    grad_c = pulled[2]
    grad_step = pulled[3]
    grad_decay = pulled[4]
    select_grad = lax.psum(jnp.concatenate([grad_b, grad_c], axis=1), "head")
    log_rate_grad = jnp.sum(grad_decay * log_decay, axis=0)
    grad_step_pre = (grad_step - grad_decay * jnp.exp(weights[10])) * jax.nn.sigmoid(
        step_pre + weights[9]
    )
    step_bias_grad = jnp.sum(grad_step_pre, axis=0)
    grad_conv = jnp.concatenate([grad_x, select_grad], axis=1) * silu_slope(conv_total)
    bias_grad = jnp.sum(grad_conv, axis=0)
    kernel_grad = jnp.stack(
        [
            jnp.sum(
                grad_conv
                * extended[tap_index : tap_index + row_count]
                * tap_masks[tap_index][:, None],
                axis=0,
            )
            for tap_index in range(K)
        ]
    )
    grad_extended = jnp.zeros((row_count + K - 1, grad_conv.shape[1]), jnp.float32)
    for tap_index in range(K):
        grad_extended = grad_extended + jnp.pad(
            kernel[tap_index][None, :] * grad_conv * tap_masks[tap_index][:, None],
            ((tap_index, K - 1 - tap_index), (0, 0)),
        )
    sent_back = shifted(grad_extended[: K - 1], "tok", -1)
    grad_input = grad_extended[K - 1 :] + jnp.pad(sent_back, ((row_count - (K - 1), 0), (0, 0)))
    grad_value_pre = grad_input[:, :value_width].astype(jnp.bfloat16)
    grad_select_pre = grad_input[:, value_width:].astype(jnp.bfloat16)
    grad_step_low = grad_step_pre.astype(jnp.bfloat16)
    partial_normed = (
        contract_cols(grad_gate_pre, weights[1])
        + contract_cols(grad_value_pre, weights[2])
        + contract_cols(grad_step_low, weights[4])
    )
    grad_normed = lax.psum(partial_normed, "head") + contract_cols(grad_select_pre, weights[3])
    norm_gain_grad = jnp.sum(grad_normed * hidden_in * inv_rms, axis=0)
    weighted_in = grad_normed * weights[0]
    grad_hidden = (
        grad_out
        + inv_rms * weighted_in
        - hidden_in * inv_rms**3 * jnp.mean(weighted_in * hidden_in, axis=-1, keepdims=True)
    )
    gradients = (
        norm_gain_grad,
        contract_rows(normed, grad_gate_pre),
        contract_rows(normed, grad_value_pre),
        contract_rows(normed, grad_select_pre),
        contract_rows(normed, grad_step_low),
        kernel_grad[:, :value_width].reshape(weights[5].shape),
        bias_grad[:value_width].reshape(weights[6].shape),
        kernel_grad[:, value_width:],
        bias_grad[value_width:],
        step_bias_grad,
        log_rate_grad,
        skip_gain_grad,
        gate_gain_grad,
        output_grad,
    )
    return (grad_hidden, gradients)


def reduce_grads(gradients):
    spread = (
        lax.psum_scatter(gradients[0], "tok", scatter_dimension=0, tiled=True),
        lax.psum_scatter(gradients[1], "tok", scatter_dimension=0, tiled=True),
        lax.psum_scatter(gradients[2], "tok", scatter_dimension=0, tiled=True),
        lax.psum_scatter(gradients[3], "tok", scatter_dimension=0, tiled=True),
        lax.psum_scatter(gradients[4], "tok", scatter_dimension=0, tiled=True),
        lax.psum_scatter(gradients[5], "tok", scatter_dimension=2, tiled=True),
        lax.psum_scatter(gradients[6], "tok", scatter_dimension=1, tiled=True),
        lax.psum_scatter(gradients[7], "tok", scatter_dimension=1, tiled=True),
        lax.psum_scatter(gradients[8], "tok", scatter_dimension=0, tiled=True),
        lax.psum_scatter(gradients[12], "tok", scatter_dimension=1, tiled=True),
        lax.psum_scatter(gradients[13], "tok", scatter_dimension=1, tiled=True),
    )
    per_head = lax.psum((gradients[9], gradients[10], gradients[11]), "tok")
    spread = tuple(spread)
    return spread[:9] + tuple(per_head) + spread[9:]


def store_slot(buffer, micro_slot, fresh_value, is_valid):
    current = lax.dynamic_index_in_dim(buffer, micro_slot, 0, keepdims=False)
    return lax.dynamic_update_index_in_dim(
        buffer, jnp.where(is_valid, fresh_value, current), micro_slot, 0
    )


def fetch_slot(buffer, micro_slot):
    return lax.dynamic_index_in_dim(buffer, micro_slot, 0, keepdims=False)


def shards(
    block_input,
    out_grad,
    lengths,
    norm_gain,
    gate_weight,
    value_weight,
    select_weight,
    step_weight,
    conv_value,
    conv_value_bias,
    conv_select,
    conv_select_bias,
    step_bias,
    log_rate,
    skip_gain,
    gate_gain,
    output_weight,
):
    weights = tuple(
        (
            weight[0]
            for weight in (
                norm_gain,
                gate_weight,
                value_weight,
                select_weight,
                step_weight,
                conv_value,
                conv_value_bias,
                conv_select,
                conv_select_bias,
                step_bias,
                log_rate,
                skip_gain,
                gate_gain,
                output_weight,
            )
        )
    )
    section_index = lax.axis_index("section")
    row_count = block_input.shape[1]
    value_width = weights[1].shape[1]
    heads_here = weights[10].shape[0]
    channel_count = value_width + 2 * NST
    layer_store = jnp.zeros((MICRO, row_count, D), jnp.float32)
    input_store = jnp.zeros_like(layer_store)
    grad_store = jnp.zeros_like(layer_store)
    halo_store = jnp.zeros((MICRO, K - 1, channel_count), jnp.float32)
    state_store = jnp.zeros((MICRO, heads_here, P_SIZE, NST), jnp.float32)
    square_store = jnp.zeros((MICRO, row_count), jnp.float32)
    received = jnp.zeros((row_count, D), jnp.float32)
    for tick_index in range(MICRO + 1):
        micro_index = tick_index - section_index
        is_valid = (micro_index >= 0) & (micro_index < MICRO)
        micro_slot = jnp.clip(micro_index, 0, MICRO - 1)
        layer_in = jnp.where(
            section_index == 0, fetch_slot(block_input, micro_slot).astype(jnp.float32), received
        )
        context_info = context_of(fetch_slot(lengths, micro_slot), row_count)
        layer_result, saved_items, projections = forward_layer(layer_in, context_info, weights)
        layer_store = store_slot(layer_store, micro_slot, layer_result, is_valid)
        input_store = store_slot(input_store, micro_slot, layer_in, is_valid)
        halo_store = store_slot(halo_store, micro_slot, saved_items[0], is_valid)
        state_store = store_slot(state_store, micro_slot, saved_items[1], is_valid)
        square_store = store_slot(square_store, micro_slot, saved_items[2], is_valid)
        if tick_index < MICRO:
            received = shifted(layer_result, "section", 1)
    grad_received = jnp.zeros((row_count, D), jnp.float32)
    totals = None
    for tick_index in range(MICRO + 1):
        micro_index = tick_index - (1 - section_index)
        is_valid = (micro_index >= 0) & (micro_index < MICRO)
        micro_slot = jnp.clip(micro_index, 0, MICRO - 1)
        grad_in = jnp.where(
            section_index == 1, fetch_slot(out_grad, micro_slot).astype(jnp.float32), grad_received
        )
        context_info = context_of(fetch_slot(lengths, micro_slot), row_count)
        saved_items = (
            fetch_slot(halo_store, micro_slot),
            fetch_slot(state_store, micro_slot),
            fetch_slot(square_store, micro_slot),
        )
        grad_hidden, gradients = backward_layer(
            fetch_slot(input_store, micro_slot), grad_in, context_info, weights, saved_items
        )
        grad_store = store_slot(grad_store, micro_slot, grad_hidden, is_valid)
        gradients = tuple((jnp.where(is_valid, one_grad, 0.0) for one_grad in gradients))
        totals = gradients if totals is None else tuple(jax.tree.map(jnp.add, totals, gradients))
        if tick_index < MICRO:
            grad_received = shifted(grad_hidden, "section", -1)
    totals = reduce_grads(totals)
    return (layer_store[None], grad_store[None]) + tuple((one_grad[None] for one_grad in totals))


def solution(mesh):
    return jax.shard_map(
        shards,
        mesh=mesh,
        in_specs=(
            P(None, "tok", None),
            P(None, "tok", None),
            P(),
            P("section", None),
            P("section", None, "head"),
            P("section", None, "head"),
            P("section", None, None),
            P("section", None, "head"),
            P("section", None, "head", None),
            P("section", "head", None),
            P("section", None, None),
            P("section", None),
            P("section", "head"),
            P("section", "head"),
            P("section", "head"),
            P("section", "head", None),
            P("section", "head", None),
        ),
        out_specs=(
            P("section", None, "tok", None),
            P("section", None, "tok", None),
            P("section", "tok"),
            P("section", "tok", "head"),
            P("section", "tok", "head"),
            P("section", "tok", None),
            P("section", "tok", "head"),
            P("section", None, "head", "tok"),
            P("section", "head", "tok"),
            P("section", None, "tok"),
            P("section", "tok"),
            P("section", "head"),
            P("section", "head"),
            P("section", "head"),
            P("section", "head", "tok"),
            P("section", "head", "tok"),
        ),
        check_vma=False,
    )
```

profile of v0, /device:TPU:0, one launch (start us, length us, event | category | flops | bytes accessed | tf_op | source)
XLA Modules:
  0.0 2071.5 jit_solution(7745570040889561491)
XLA Ops:
  71.4 21.9 %all-gather.19.cloned.1.call-done = f32[64,64,128]{2,1,0:T(8,128)} async-done(((f32[16,64,128]{2,1,0:T(8,128)}), f32[64,64,128]{2,1,0:T(8,128)}) %all-gather.19.cloned.1.call-update) | async-done | bytes 2097168 | tf_op jit(solution)/shard_map/all_gather | solution.py:29
  124.1 66.8 %all-reduce.37.cloned.1.call-done = f32[256,2048]{1,0:T(8,128)} async-done(((f32[256,2048]{1,0:T(8,128)}), f32[256,2048]{1,0:T(8,128)}) %all-reduce.37.cloned.1.call-update) | async-done | bytes 2097168 | tf_op jit(solution)/shard_map/psum | solution.py:255
  233.6 11.1 all-gather.7
  255.3 18.1 all-gather.21.cloned.1.call-done
  293.1 9.9 psum.128
  323.7 51.4 %all-reduce.39.cloned.1.call-done = f32[256,2048]{1,0:T(8,128)} async-done(((f32[256,2048]{1,0:T(8,128)}), f32[256,2048]{1,0:T(8,128)}) %all-reduce.39.cloned.1.call-update) | async-done | bytes 2097168 | tf_op jit(solution)/shard_map/psum | solution.py:255
  470.1 18.6 all-gather.23.cloned.1.call-done
  509.9 10.9 psum.130
  596.9 12.3 all-gather.25.cloned.1.call-done
  684.0 36.8 %all-reduce.41.cloned.1.call-done = f32[256,256]{1,0:T(8,128)} async-done(((f32[256,256]{1,0:T(8,128)}), f32[256,256]{1,0:T(8,128)}) %all-reduce.41.cloned.1.call-update) | async-done | bytes 262160 | tf_op jit(solution)/shard_map/psum | solution.py:321
  743.6 59.7 %all-reduce.43.cloned.1.call-done = f32[256,2048]{1,0:T(8,128)} async-done(((f32[256,2048]{1,0:T(8,128)}), f32[256,2048]{1,0:T(8,128)}) %all-reduce.43.cloned.1.call-update) | async-done | bytes 2097168 | tf_op jit(solution)/shard_map/psum | solution.py:356
  884.4 11.4 all-gather.10
  917.5 12.0 all-gather.27.cloned.1.call-done
  1004.2 36.8 %all-reduce.45.cloned.1.call-done = f32[256,256]{1,0:T(8,128)} async-done(((f32[256,256]{1,0:T(8,128)}), f32[256,256]{1,0:T(8,128)}) %all-reduce.45.cloned.1.call-update) | async-done | bytes 262160 | tf_op jit(solution)/shard_map/psum | solution.py:321
  1063.4 60.4 %all-reduce.47.cloned.1.call-done = f32[256,2048]{1,0:T(8,128)} async-done(((f32[256,2048]{1,0:T(8,128)}), f32[256,2048]{1,0:T(8,128)}) %all-reduce.47.cloned.1.call-update) | async-done | bytes 2097168 | tf_op jit(solution)/shard_map/psum | solution.py:356
  1208.2 11.1 all-gather.11
  1322.9 36.7 %all-reduce.49.cloned.1.call-done = f32[256,256]{1,0:T(8,128)} async-done(((f32[256,256]{1,0:T(8,128)}), f32[256,256]{1,0:T(8,128)}) %all-reduce.49.cloned.1.call-update) | async-done | bytes 262160 | tf_op jit(solution)/shard_map/psum | solution.py:321
  1383.4 93.5 %all-reduce.51.cloned.1.call-done = (f32[256,2048]{1,0:T(8,128)}, f32[256,2048]{1,0:T(8,128)}) async-done(((f32[256,2048]{1,0:T(8,128)}, f32[256,2048]{1,0:T(8,128)}), (f32[256,2048]{1,0:T(8,128)}, f32[256,2048]{1,0:T(8,128)})) %all-reduce.51.cloned.1.call-update) | async-done | bytes 4194320 | tf_op jit(solution)/shard_map/psum | solution.py:255
  1537.9 18.7 reduce-scatter.28.cloned.1.call-done
  1558.1 16.5 all-reduce.27
  1586.2 35.5 %reduce-scatter.22.cloned.1.call-done = f32[512,256]{1,0:T(8,128)} async-done(((f32[2048,256]{1,0:T(8,128)}), f32[512,256]{1,0:T(8,128)}) %reduce-scatter.22.cloned.1.call-update) | async-done | bytes 524304 | tf_op jit(solution)/shard_map/reduce_scatter | solution.py:388
  1621.7 146.8 %reduce-scatter.26.cloned.1.call-done = f32[1024,512]{1,0:T(8,128)} async-done(((f32[1024,2048]{1,0:T(8,128)}), f32[1024,512]{1,0:T(8,128)}) %reduce-scatter.26.cloned.1.call-update) | async-done | bytes 2097168 | tf_op jit(solution)/shard_map/reduce_scatter | solution.py:395
  1768.5 148.2 %reduce-scatter.20.cloned.1.call-done = f32[512,1024]{1,0:T(8,128)} async-done(((f32[2048,1024]{1,0:T(8,128)}), f32[512,1024]{1,0:T(8,128)}) %reduce-scatter.20.cloned.1.call-update) | async-done | bytes 2097168 | tf_op jit(solution)/shard_map/reduce_scatter | solution.py:387
  1916.7 148.2 %reduce-scatter.18.cloned.1.call-done = f32[512,1024]{1,0:T(8,128)} async-done(((f32[2048,1024]{1,0:T(8,128)}), f32[512,1024]{1,0:T(8,128)}) %reduce-scatter.18.cloned.1.call-update) | async-done | bytes 2097168 | tf_op jit(solution)/shard_map/reduce_scatter | solution.py:386
  (1188 shorter events, 999.1 us)
Async XLA Ops:
  7.2 86.1 %all-gather.19.cloned.1.call-start = ((), (), s32[]{:S(2)}) async-start(), calls=%async_computation.21 | async-start | bytes 2621440 | tf_op jit(solution)/shard_map/all_gather | solution.py:29
  47.5 143.4 %all-reduce.37.cloned.1.call-start = ((), (), s32[]{:S(2)}) async-start(), calls=%async_computation.9 | async-start | bytes 4194304 | tf_op jit(solution)/shard_map/psum | solution.py:255
  124.1 149.3 %all-gather.21.cloned.1.call-start = ((), (), s32[]{:S(2)}) async-start(), calls=%async_computation.22 | async-start | bytes 2621440 | tf_op jit(solution)/shard_map/all_gather | solution.py:29
  227.1 148.0 %all-reduce.39.cloned.1.call-start = ((), (), s32[]{:S(2)}) async-start(), calls=%async_computation.10 | async-start | bytes 4194304 | tf_op jit(solution)/shard_map/psum | solution.py:255
  308.2 180.4 %all-gather.23.cloned.1.call-start = ((), (), s32[]{:S(2)}) async-start(), calls=%async_computation.23 | async-start | bytes 2621440 | tf_op jit(solution)/shard_map/all_gather | solution.py:29
  445.3 163.9 %all-gather.25.cloned.1.call-start = ((), (), s32[]{:S(2)}) async-start(), calls=%async_computation.24 | async-start | bytes 2621440 | tf_op jit(solution)/shard_map/all_gather | solution.py:29
  565.2 155.6 %all-reduce.41.cloned.1.call-start = ((), (), s32[]{:S(2)}) async-start(), calls=%async_computation.11 | async-start | bytes 524288 | tf_op jit(solution)/shard_map/psum | solution.py:321
  679.0 124.3 %all-reduce.43.cloned.1.call-start = ((), (), s32[]{:S(2)}) async-start(), calls=%async_computation.12 | async-start | bytes 4194304 | tf_op jit(solution)/shard_map/psum | solution.py:356
  733.9 195.7 %all-gather.27.cloned.1.call-start = ((), (), s32[]{:S(2)}) async-start(), calls=%async_computation.25 | async-start | bytes 2621440 | tf_op jit(solution)/shard_map/all_gather | solution.py:29
  819.7 36.1 %collective-permute-start.6 = (f32[256,2048]{1,0:T(8,128)}, f32[256,2048]{1,0:T(8,128)}, u32[]{:S(2)}, u32[]{:S(2)}) collective-permute-start(f32[256,2048]{1,0:T(8,128)} %get-tuple-element.1574), channel_id=1, source_target_pairs={{16,0},{17,1},{18,2},{19,3},{20,4},{21,5},{22,6},{23,7},{24,8},{25... | collective-permute-start | bytes 6291464 | tf_op jit(solution)/shard_map/ppermute | solution.py:24
  883.5 157.5 %all-reduce.45.cloned.1.call-start = ((), (), s32[]{:S(2)}) async-start(), calls=%async_computation.13 | async-start | bytes 524288 | tf_op jit(solution)/shard_map/psum | solution.py:321
  999.2 124.5 %all-reduce.47.cloned.1.call-start = ((), (), s32[]{:S(2)}) async-start(), calls=%async_computation.14 | async-start | bytes 4194304 | tf_op jit(solution)/shard_map/psum | solution.py:356
  1054.0 194.6 %all-gather.29.cloned.1.call-start = ((), (), s32[]{:S(2)}) async-start(), calls=%async_computation.26 | async-start | bytes 2621440 | tf_op jit(solution)/shard_map/all_gather | solution.py:29
  1202.6 157.0 %all-reduce.49.cloned.1.call-start = ((), (), s32[]{:S(2)}) async-start(), calls=%async_computation.15 | async-start | bytes 524288 | tf_op jit(solution)/shard_map/psum | solution.py:321
  1317.8 159.1 %all-reduce.51.cloned.1.call-start = ((), (), s32[]{:S(2)}) async-start(), calls=%async_computation.31 | async-start | bytes 8388608 | tf_op jit(solution)/shard_map/psum | solution.py:255
  1372.6 156.5 %reduce-scatter.34.cloned.1.call-start = ((), (), s32[]{:S(2)}) async-start(), calls=%async_computation.30 | async-start | bytes 40960
  1379.7 151.5 %reduce-scatter.30.cloned.1.call-start = ((), (), s32[]{:S(2)}) async-start(), calls=%async_computation.28 | async-start | bytes 40960
  1380.7 155.8 %reduce-scatter.32.cloned.1.call-start = ((), (), s32[]{:S(2)}) async-start(), calls=%async_computation.29 | async-start | bytes 163840
  1382.3 174.3 %reduce-scatter.28.cloned.1.call-start = ((), (), s32[]{:S(2)}) async-start(), calls=%async_computation.27 | async-start | bytes 40960
  1383.3 202.8 %reduce-scatter.24.cloned.1.call-start = ((), (), s32[]{:S(2)}) async-start(), calls=%async_computation.19 | async-start | bytes 163840 | tf_op jit(solution)/shard_map/reduce_scatter | solution.py:389
  1483.2 138.5 %reduce-scatter.22.cloned.1.call-start = ((), (), s32[]{:S(2)}) async-start(), calls=%async_computation.18 | async-start | bytes 2621440 | tf_op jit(solution)/shard_map/reduce_scatter | solution.py:388
  1487.1 281.3 %reduce-scatter.26.cloned.1.call-start = ((), (), s32[]{:S(2)}) async-start(), calls=%async_computation.20 | async-start | bytes 10485760 | tf_op jit(solution)/shard_map/reduce_scatter | solution.py:395
  1497.8 418.9 %reduce-scatter.20.cloned.1.call-start = ((), (), s32[]{:S(2)}) async-start(), calls=%async_computation.17 | async-start | bytes 10485760 | tf_op jit(solution)/shard_map/reduce_scatter | solution.py:387
  1507.2 557.7 %reduce-scatter.18.cloned.1.call-start = ((), (), s32[]{:S(2)}) async-start(), calls=%async_computation.16 | async-start | bytes 10485760 | tf_op jit(solution)/shard_map/reduce_scatter | solution.py:386
  (303 other events, 3145.0 us)
Sparse Core Ops, SparseCore 0:
  47.7 45.6 all-gather.18
  124.2 66.6 all-reduce.36
  227.2 46.1 all-gather.20
  308.3 66.7 all-reduce.38
  445.4 43.1 all-gather.22
  565.4 43.7 all-gather.24
  679.1 41.6 all-reduce.40
  734.0 69.3 all-reduce.42
  883.6 45.9 all-gather.26
  999.3 41.6 all-reduce.44
  1054.1 69.5 all-reduce.46
  1202.7 45.9 all-gather.28
  1317.9 41.6 all-reduce.48
  1372.7 104.0 all-reduce.50
  1478.9 18.9 reduce-scatter.33
  1500.1 17.0 reduce-scatter.29
  1519.3 17.2 reduce-scatter.31
  1539.3 17.2 reduce-scatter.27
  1559.4 17.2 reduce-scatter.23
  1579.6 42.0 reduce-scatter.21
  1624.6 143.8 reduce-scatter.25
  1771.4 145.1 reduce-scatter.19
  1919.6 145.1 reduce-scatter.17
where the time goes:
time: 2080 us; the launch traced here: 2070 us
  waiting for transfers between devices  1050 us (50%)
  matrix products  346 us (17%)
  other arithmetic  268 us (13%)
  local copies, waits for them, and re-layouts  223 us (11%)
  blocking collectives  136 us (7%)
  starting transfers between devices  27.3 us (1%)
  between operations  26.6 us (1%)
    psum x3, waiting for transfers between devices, forward_layer(): lax.psum(jnp.dot(scaled, weights[13], preferred_element_type=jnp.float32)...  212 us
    reduce_scatter x1, waiting for transfers between devices, reduce_grads(): lax.psum_scatter(gradients[1], 'tok', scatter_dimension=0, tiled=True)  148 us
    reduce_scatter x1, waiting for transfers between devices, reduce_grads(): lax.psum_scatter(gradients[2], 'tok', scatter_dimension=0, tiled=True)  148 us
    reduce_scatter x1, waiting for transfers between devices, reduce_grads(): lax.psum_scatter(gradients[13], 'tok', scatter_dimension=1, tiled=True)  147 us
    psum x2, waiting for transfers between devices, backward_layer(): lax.psum(partial_normed, 'head')  120 us
    psum x3, waiting for transfers between devices, backward_layer(): select_grad = lax.psum(jnp.concatenate([grad_b, grad_c], axis=1), 'head')  110 us
    all_gather x6, waiting for transfers between devices, entering_2(): pieces = jax.tree.map(lambda part: lax.all_gather(part, axis), value)  90.6 us
    dot_general x12, matrix products, one_block(): block_out = jnp.einsum('hts,shp->thp', mixing, x_rows, precision=PRECISE)  79.6 us
  transfers between devices with their start and end apart: 33, of which 23 were waited for; matrix products, arithmetic and copies ran while one was open for 16% of the time, Pallas kernels for 0%

commit v1 on v0

v1 whole, which is shorter than its diff:
```python
from functools import partial
from types import SimpleNamespace

import jax
import jax.numpy as jnp
from jax import lax
from jax.experimental import pallas as pl
from jax.experimental.pallas import tpu as pltpu
from jax.sharding import PartitionSpec as P

D = 2048
H = 64
P_SIZE = 64
NST = 128
K = 4
EPSILON = 1e-05
SECTION, TOK, HEAD = AXES = ("section", "tok", "head")
F32 = jnp.float32
BF16 = jnp.bfloat16
EXACT = lax.Precision.HIGHEST
VMEM_BYTES = 58 * 1024 * 1024
PAD = 128

DT, CUM, SIG, LOG, ENDW, DECIN, BASE = (0, 16, 32, 48, 64, 80, 96)


def send(value, section, move):
    tok_count, head_count = (lax.axis_size(TOK), lax.axis_size(HEAD))

    def flat(tok, head):
        return (section * tok_count + tok) * head_count + head

    pairs = []
    for tok in range(tok_count):
        for head in range(head_count):
            target = move(tok, head)
            if 0 <= target[0] < tok_count:
                pairs.append((flat(tok, head), flat(*target)))
    return lax.ppermute(value, AXES, pairs)


def to_head(value, section, step):
    return send(value, section, lambda tok, head: (tok, head ^ step))


def to_tok(value, section, step):
    return send(value, section, lambda tok, head: (tok + step, head))


def nn(left, right, precision=None):
    return lax.dot_general(
        left, right, (((1,), (0,)), ((), ())), precision=precision, preferred_element_type=F32
    )


def nt(left, right, precision=None):
    return lax.dot_general(
        left, right, (((1,), (1,)), ((), ())), precision=precision, preferred_element_type=F32
    )


def tn(left, right):
    return lax.dot_general(left, right, (((0,), (0,)), ((), ())), preferred_element_type=F32)


def split(values):
    high = values.astype(BF16)
    return (high, (values - high.astype(F32)).astype(BF16))


def fine(product, left, right):
    return product(left[0], right[0]) + (product(left[0], right[1]) + product(left[1], right[0]))


def act_of(values):
    return values * sigmoid(values)


def sigmoid(values):
    return 1.0 / (1.0 + jnp.exp(-values))


def seg_at(points, ends, micro):
    inside = (points >= ends[micro, 0]).astype(jnp.int32)
    for which in range(1, 4):
        inside = inside + (points >= ends[micro, which]).astype(jnp.int32)
    return jnp.where(points >= 0, inside, -1)


def call(body, grid, scalars, ins, in_specs, outs, out_specs, scratch=(), flops=0, name=None):
    flag = len(scalars) - 1

    def guarded(*refs):
        @pl.when(refs[flag][4] == 1)
        def _():
            body(*refs)

    moved = sum(a.size * a.dtype.itemsize for a in ins)
    moved += sum(o.size * o.dtype.itemsize for o in outs)
    return pl.pallas_call(
        guarded,
        grid_spec=pltpu.PrefetchScalarGridSpec(
            num_scalar_prefetch=len(scalars),
            grid=grid,
            in_specs=in_specs,
            out_specs=out_specs,
            scratch_shapes=list(scratch),
        ),
        out_shape=outs,
        compiler_params=pltpu.CompilerParams(vmem_limit_bytes=VMEM_BYTES),
        cost_estimate=pl.CostEstimate(flops=flops, bytes_accessed=moved, transcendentals=0),
        name=name,
    )(*scalars, *ins)


def rows(count, width):
    return pl.BlockSpec((count, width), lambda m, *_: (m, 0))


def whole(shape):
    return pl.BlockSpec(shape, lambda m, *_: (0,) * len(shape))


def struct(shape, dtype=F32):
    return jax.ShapeDtypeStruct(shape, dtype)


def pair_of(table, base, pair, lane):
    first = table[:, base + 2 * pair : base + 2 * pair + 1]
    second = table[:, base + 2 * pair + 1 : base + 2 * pair + 2]
    return jnp.where(lane < P_SIZE, first, second)


def head_sums(values, pair, head_count):
    owner = lax.broadcasted_iota(jnp.int32, (head_count, 2 * P_SIZE), 0)
    lane = lax.broadcasted_iota(jnp.int32, (head_count, 2 * P_SIZE), 1)
    chosen = (owner == 2 * pair + (lane >= P_SIZE).astype(jnp.int32)).astype(BF16)
    high = values.astype(BF16)
    low = (values - high.astype(F32)).astype(BF16)
    return nt(chosen, high) + nt(chosen, low)


def in_body(idx, *refs, part_count, micro_count, row_count):
    parts, refs = (refs[:part_count], refs[part_count:])
    gain, w_value, w_select, w_step, normed, value, select, step = refs
    chunk = row_count // 4
    step_id = pl.program_id(0)

    @pl.when(step_id == 0)
    def _():
        for micro in range(micro_count):
            for piece in range(4):
                if part_count == 1:
                    place = micro * row_count + piece * chunk
                    values = parts[0][place : place + chunk, :].astype(F32)
                else:
                    place = pl.multiple_of(micro * row_count + (idx[1] ^ piece) * chunk, chunk)
                    values = parts[piece][micro * chunk : (micro + 1) * chunk, :]
                inv = lax.rsqrt(jnp.mean(values * values, axis=-1, keepdims=True) + EPSILON)
                normed[pl.ds(place, chunk), :] = (values * inv * gain[...]).astype(BF16)
        select[...] = nn(normed[...], w_select[...])
        step[...] = nn(normed[...], w_step[...])

    value[...] = nn(normed[...], w_value[...])


def in_project(idx, parts, weights, micro_count, row_count):
    total = micro_count * row_count
    width = weights.value.shape[1]
    heads = weights.step.shape[1]
    tile = width // 4
    outs = [
        struct((total, D), BF16),
        struct((total, width)),
        struct((total, 2 * NST)),
        struct((total, heads)),
    ]
    cols = pl.BlockSpec((total, tile), lambda j, *_: (0, j))
    wcols = pl.BlockSpec((D, tile), lambda j, *_: (0, j))
    return call(
        partial(in_body, part_count=len(parts), micro_count=micro_count, row_count=row_count),
        (4,),
        (idx,),
        [*parts, weights.gain, weights.value, weights.select, weights.step],
        [whole(part.shape) for part in parts]
        + [whole((1, D)), wcols, whole((D, 2 * NST)), whole((D, heads))],
        outs,
        [whole((total, D)), cols, whole((total, 2 * NST)), whole((total, heads))],
        flops=2 * total * D * (width + 2 * NST),
    )


def gate_body(idx, normed, w_gate, gate):
    gate[...] = nn(normed[...], w_gate[...])


def gate_project(idx, normed, w_gate):
    total, width = (normed.shape[0], w_gate.shape[1])
    tile = width // 4
    return call(
        gate_body,
        (4,),
        (idx,),
        [normed, w_gate],
        [whole((total, D)), pl.BlockSpec((D, tile), lambda j, *_: (0, j))],
        [struct((total, width))],
        [pl.BlockSpec((total, tile), lambda j, *_: (0, j))],
        flops=2 * total * D * width,
    )[0]


def conv_body(
    ends, idx, value, select, step, halo, taps, head_rows,
    conv, table, table_t, state, extended, weighted, weighted_low,
):
    micro = pl.program_id(0)
    row_count, width = value.shape
    heads = step.shape[1]
    base = idx[0]
    at = base + lax.broadcasted_iota(jnp.int32, (row_count, 1), 0)
    seg = seg_at(at, ends, micro)
    seg_before = seg_at(base - 1 + jnp.zeros((1, 1), jnp.int32), ends, micro)
    seg_last = seg_at(base + row_count - 1 + jnp.zeros((1, 1), jnp.int32), ends, micro)
    carry = (seg == seg_before).astype(F32)
    tail = (seg == seg_last).astype(F32)

    pre = step[...] + head_rows[0:1, 0:heads]
    step_size = jnp.maximum(pre, 0.0) + jnp.log1p(jnp.exp(-jnp.abs(pre)))
    log_decay = -jnp.exp(head_rows[1:2, 0:heads]) * step_size
    row_id = lax.broadcasted_iota(jnp.int32, (row_count, row_count), 0)
    col_id = lax.broadcasted_iota(jnp.int32, (row_count, row_count), 1)
    cum = nn((row_id >= col_id).astype(F32), log_decay, EXACT)
    end_base = jnp.exp(cum[row_count - 1 : row_count, :] - cum) * tail
    decay_in = jnp.exp(cum) * carry
    table[...] = jnp.zeros_like(table)
    for place, part in (
        (DT, step_size),
        (CUM, cum),
        (SIG, sigmoid(pre)),
        (LOG, log_decay),
        (ENDW, end_base * step_size),
        (DECIN, decay_in),
        (BASE, end_base),
    ):
        table[:, place : place + heads] = part
    table_t[...] = table[...].T

    extended[0:8, :] = halo[...]
    extended[8:, 0:width] = value[...]
    extended[8:, width:] = select[...]
    masks = [(seg_at(at - (K - 1 - tap), ends, micro) == seg).astype(F32) for tap in range(K - 1)]
    lane = lax.broadcasted_iota(jnp.int32, (row_count, 128), 1)
    columns = width + 2 * NST
    for left in range(0, columns, 128):
        span = slice(left, left + 128)
        total = taps[4:5, span] + taps[3:4, span] * extended[8 : 8 + row_count, span]
        for tap in range(K - 1):
            total = total + taps[tap : tap + 1, span] * (
                extended[5 + tap : 5 + tap + row_count, span] * masks[tap]
            )
        conv[:, span] = total
        if left < width:
            weighted[:, span], weighted_low[:, span] = split(
                act_of(total) * pair_of(table[...], ENDW, left // 128, lane)
            )
    b_act = split(act_of(conv[:, width : width + NST]))
    state[...] = fine(tn, (weighted[...], weighted_low[...]), b_act)


def conv_state(ends, idx, value, select, step, halo, params, micro_count, row_count):
    width = value.shape[1]
    heads = step.shape[1]
    total = micro_count * row_count
    return call(
        conv_body,
        (micro_count,),
        (ends, idx),
        [value, select, step, halo, params.taps, params.head_rows],
        [
            rows(row_count, width),
            rows(row_count, 2 * NST),
            rows(row_count, heads),
            rows(8, width + 2 * NST),
            whole((8, width + 2 * NST)),
            whole((8, 128)),
        ],
        [
            struct((total, width + 2 * NST)),
            struct((total, 128)),
            struct((micro_count * 128, row_count)),
            struct((micro_count * width, NST)),
        ],
        [
            rows(row_count, width + 2 * NST),
            rows(row_count, 128),
            rows(128, row_count),
            rows(width, NST),
        ],
        [
            pltpu.VMEM((row_count + 8, width + 2 * NST), F32),
            pltpu.VMEM((row_count, width), BF16),
            pltpu.VMEM((row_count, width), BF16),
        ],
        flops=40 * total * width,
    )


def mask_bias(ends, idx, micro, row_count):
    base = idx[0]
    seg_col = seg_at(base + lax.broadcasted_iota(jnp.int32, (row_count, 1), 0), ends, micro)
    seg_row = seg_at(base + lax.broadcasted_iota(jnp.int32, (1, row_count), 1), ends, micro)
    row_id = lax.broadcasted_iota(jnp.int32, (row_count, row_count), 0)
    col_id = lax.broadcasted_iota(jnp.int32, (row_count, row_count), 1)
    return jnp.where((seg_col == seg_row) & (row_id >= col_id), 0.0, -1e30)


def sides(values, lane):
    return (
        split(jnp.where(lane < P_SIZE, values, 0.0)),
        split(jnp.where(lane < P_SIZE, 0.0, values)),
    )


def scan_body(ends, idx, conv, table, table_t, skip, out, scores, bias):
    micro = pl.program_id(0)
    row_count = conv.shape[0]
    width = conv.shape[1] - 2 * NST
    half = row_count // 2
    b_act = split(act_of(conv[:, width : width + NST]))
    c_act = split(act_of(conv[:, width + NST :]))
    scores[...] = fine(nt, c_act, b_act)
    bias[...] = mask_bias(ends, idx, micro, row_count)
    lane = lax.broadcasted_iota(jnp.int32, (row_count, 128), 1)
    for pair in range(width // 128):
        span = slice(128 * pair, 128 * pair + 128)
        x_act = act_of(conv[:, span])
        halves = sides(x_act * pair_of(table[...], DT, pair, lane), lane)
        direct = skip[:, span] * x_act
        for top, bottom in ((0, half), (half, row_count)):
            result = direct[top:bottom, :]
            for side in range(2):
                head = 2 * pair + side
                cum_col = table[top:bottom, CUM + head : CUM + head + 1]
                cum_row = table_t[CUM + head : CUM + head + 1, 0:bottom]
                decay = jnp.exp(cum_col - cum_row + bias[top:bottom, 0:bottom])
                mixing = split(decay * scores[top:bottom, 0:bottom])
                result = result + fine(nn, mixing, [part[0:bottom, :] for part in halves[side]])
            out[top:bottom, span] = result


def scan_local(ends, idx, conv, table, table_t, params, micro_count, row_count):
    width = conv.shape[1] - 2 * NST
    return call(
        scan_body,
        (micro_count,),
        (ends, idx),
        [conv, table, table_t, params.skip],
        [rows(row_count, width + 2 * NST), rows(row_count, 128), rows(128, row_count), whole((1, width))],
        [struct((micro_count * row_count, width))],
        [rows(row_count, width)],
        [pltpu.VMEM((row_count, row_count), F32), pltpu.VMEM((row_count, row_count), F32)],
        flops=30 * micro_count * row_count * row_count * (width // P_SIZE),
    )[0]


def mix_body(idx, local, select, table, entering, gate, scan, gated, sums):
    row_count, width = local.shape
    c_act = split(act_of(select[:, NST:]))
    lane = lax.broadcasted_iota(jnp.int32, (row_count, 128), 1)
    squares = jnp.zeros((row_count, 128), F32)
    for pair in range(width // 128):
        span = slice(128 * pair, 128 * pair + 128)
        carried = fine(nt, c_act, split(entering[span, :]))
        value = local[:, span] + carried * pair_of(table[...], DECIN, pair, lane)
        scan[:, span] = value
        result = value * act_of(gate[:, span])
        gated[:, span] = result
        squares = squares + result * result
    sums[...] = nt(jnp.ones((8, 128), F32), squares, EXACT)


def gate_mix(idx, local, conv, table, entering, gate, micro_count, row_count):
    width = local.shape[1]
    total = micro_count * row_count
    select_block = pl.BlockSpec((row_count, 2 * NST), lambda m, *_: (m, width // (2 * NST)))
    return call(
        mix_body,
        (micro_count,),
        (idx,),
        [local, conv, table, entering, gate],
        [
            rows(row_count, width),
            select_block,
            rows(row_count, 128),
            rows(width, NST),
            rows(row_count, width),
        ],
        [struct((total, width)), struct((total, width)), struct((micro_count * 8, row_count))],
        [rows(row_count, width), rows(row_count, width), rows(8, row_count)],
        flops=6 * total * width * NST,
    )


def out_body(idx, gated, s0, s1, s2, s3, gain, w_out, scaled, inverse, *refs):
    chunks, (low, product) = (refs[:4], refs[4:])
    row_count, width = gated.shape
    chunk = row_count // 4
    squares = (s0[...] + s1[...]) + (s2[...] + s3[...])
    inverse[...] = jnp.broadcast_to(
        lax.rsqrt(squares / (H * P_SIZE) + EPSILON).T[:, 0:1], (row_count, 128)
    )
    inv = inverse[:, 0:1]
    for left in range(0, width, 128):
        span = slice(left, left + 128)
        rounded = (gated[:, span] * inv * gain[:, span]).astype(BF16)
        low[:, span] = rounded
        scaled[:, span] = rounded.astype(F32)
    for left in range(0, D, 512):
        product[:, left : left + 512] = nn(low[...], w_out[:, left : left + 512])
    for piece in range(4):
        place = pl.multiple_of((idx[1] ^ piece) * chunk, chunk)
        chunks[piece][...] = product[pl.ds(place, chunk), :]


def out_project(idx, gated, sums, weights, micro_count, row_count):
    width = gated.shape[1]
    total = micro_count * row_count
    chunk = row_count // 4
    return call(
        out_body,
        (micro_count,),
        (idx,),
        [gated, *sums, weights.gate_gain, weights.out],
        [rows(row_count, width)] + [rows(8, row_count)] * 4 + [whole((1, width)), whole((width, D))],
        [struct((total, width)), struct((total, 128))] + [struct((micro_count * chunk, D))] * 4,
        [rows(row_count, width), rows(row_count, 128)] + [rows(chunk, D)] * 4,
        [pltpu.VMEM((row_count, width), BF16), pltpu.VMEM((row_count, D), F32)],
        flops=2 * total * width * D,
    )


def gated_body(idx, *refs, from_parts):
    if from_parts:
        parts, refs = (refs[:4], refs[4:])
    else:
        grad, parts, refs = (refs[0], refs[1:5], refs[5:])
    gate, scan, inverse, select, table, gain, w_out = refs[:7]
    low_grad, grad_gate, grad_scan, state, gain_grad = refs[7:12]
    refs = refs[12:]
    if from_parts:
        full, refs = (refs[0], refs[1:])
    norms, carried, carried_low = refs
    row_count, width = gate.shape
    chunk = row_count // 4
    for piece in range(4):
        place = pl.ds(pl.multiple_of((idx[1] ^ piece) * chunk, chunk), chunk)
        if from_parts:
            values = parts[piece][:, 0:D]
            full[place, :] = values
            low_grad[place, :] = values.astype(BF16)
            norms[place, :] = parts[piece][:, D:]
        else:
            norms[place, :] = parts[piece][...]
    if not from_parts:
        low_grad[...] = grad[...]
    inv = inverse[:, 0:1]
    inner = norms[:, 0:1]
    c_act = split(act_of(select[:, NST:]))
    lane = lax.broadcasted_iota(jnp.int32, (row_count, 128), 1)
    gain_grad[...] = jnp.zeros_like(gain_grad)
    for pair in range(width // 128):
        span = slice(128 * pair, 128 * pair + 128)
        grad_scaled = nt(low_grad[...], w_out[span, :])
        gate_pre = gate[:, span]
        sig = sigmoid(gate_pre)
        act = gate_pre * sig
        out = scan[:, span]
        normal = out * act * inv
        gain_grad[0:1, span] = jnp.sum(grad_scaled * normal, axis=0, keepdims=True)
        grad_gated = inv * (grad_scaled * gain[:, span]) - normal * (inv * inner)
        grad_out = grad_gated * act
        grad_scan[:, span] = grad_out
        grad_gate[:, span] = (
            (grad_gated * out * (sig * (1.0 + gate_pre * (1.0 - sig)))).astype(BF16).astype(F32)
        )
        carried[:, span], carried_low[:, span] = split(
            grad_out * pair_of(table[...], DECIN, pair, lane)
        )
    state[...] = fine(tn, (carried[...], carried_low[...]), c_act)


def gated_back(idx, grad, parts, gate, scan, inverse, conv, table, weights, micro_count, row_count):
    width = gate.shape[1]
    total = micro_count * row_count
    chunk = row_count // 4
    from_parts = grad is None
    select_block = pl.BlockSpec((row_count, 2 * NST), lambda m, *_: (m, width // (2 * NST)))
    ins = ([] if from_parts else [grad]) + [
        *parts, gate, scan, inverse, conv, table, weights.gate_gain, weights.out
    ]
    in_specs = (
        ([] if from_parts else [rows(row_count, D)])
        + [rows(chunk, part.shape[1]) for part in parts]
        + [
            rows(row_count, width),
            rows(row_count, width),
            rows(row_count, 128),
            select_block,
            rows(row_count, 128),
            whole((1, width)),
            whole((width, D)),
        ]
    )
    outs = [
        struct((total, D), BF16),
        struct((total, width)),
        struct((total, width)),
        struct((micro_count * width, NST)),
        struct((micro_count * 8, width)),
    ]
    out_specs = [
        rows(row_count, D),
        rows(row_count, width),
        rows(row_count, width),
        rows(width, NST),
        rows(8, width),
    ]
    if from_parts:
        outs.append(struct((total, D)))
        out_specs.append(rows(row_count, D))
    return call(
        partial(gated_body, from_parts=from_parts),
        (micro_count,),
        (idx,),
        ins,
        in_specs,
        outs,
        out_specs,
        [
            pltpu.VMEM((row_count, PAD), F32),
            pltpu.VMEM((row_count, width), BF16),
            pltpu.VMEM((row_count, width), BF16),
        ],
        flops=2 * total * width * D,
    )


def scan_back_body(
    ends, idx, conv, table, table_t, grad, entering, skip,
    grad_x, grad_bc, grad_rows, skip_grad,
    scores, bias, grad_scores, row_sums, col_sums,
):
    micro = pl.program_id(0)
    row_count, width = grad.shape
    heads = width // P_SIZE
    half = row_count // 2
    b_act = split(act_of(conv[:, width : width + NST]))
    c_act = split(act_of(conv[:, width + NST :]))
    scores[...] = fine(nt, c_act, b_act)
    bias[...] = mask_bias(ends, idx, micro, row_count)
    grad_scores[...] = jnp.zeros_like(grad_scores)
    row_sums[...] = jnp.zeros_like(row_sums)
    lane = lax.broadcasted_iota(jnp.int32, (row_count, 128), 1)
    grad_c = jnp.zeros((row_count, NST), F32)
    cum_grad = jnp.zeros((heads, row_count), F32)
    step_grad = jnp.zeros((heads, row_count), F32)
    direct_sum = jnp.zeros((heads, row_count), F32)
    for pair in range(width // 128):
        span = slice(128 * pair, 128 * pair + 128)
        pre = conv[:, span]
        x_act = pre * sigmoid(pre)
        step_pair = pair_of(table[...], DT, pair, lane)
        x_step = split(x_act * step_pair)
        grad_out = grad[:, span]
        halves = sides(grad_out, lane)
        pulled = []
        for top, bottom in ((0, half), (half, row_count)):
            pulled_here = jnp.zeros((bottom, 128), F32)
            for side in range(2):
                head = 2 * pair + side
                cum_col = table[top:bottom, CUM + head : CUM + head + 1]
                cum_row = table_t[CUM + head : CUM + head + 1, 0:bottom]
                decay = jnp.exp(cum_col - cum_row + bias[top:bottom, 0:bottom])
                mixing = decay * scores[top:bottom, 0:bottom]
                grad_mix = fine(
                    nt, [part[top:bottom, :] for part in halves[side]], [part[0:bottom, :] for part in x_step]
                )
                grad_scores[top:bottom, 0:bottom] += grad_mix * decay
                turn = grad_mix * mixing
                row_sums[top:bottom, head : head + 1] = jnp.sum(turn, axis=1, keepdims=True)
                col_part = jnp.sum(turn, axis=0, keepdims=True)
                if top == 0:
                    col_sums[head : head + 1, 0:bottom] = col_part
                else:
                    col_sums[head : head + 1, 0:top] += col_part[:, 0:top]
                    col_sums[head : head + 1, top:bottom] = col_part[:, top:bottom]
                pulled_here = pulled_here + tn(mixing.astype(BF16), halves[side][0][top:bottom, :])
            pulled.append(pulled_here)
        grad_step_x = jnp.concatenate([pulled[0] + pulled[1][0:half, :], pulled[1][half:, :]], axis=0)
        grad_x[:, span] = grad_step_x * step_pair + grad_out * skip[:, span]
        step_grad = step_grad + head_sums(grad_step_x * x_act, pair, heads)
        direct_sum = direct_sum + head_sums(grad_out * x_act, pair, heads)
        decayed = grad_out * pair_of(table[...], DECIN, pair, lane)
        state = split(entering[span, :])
        cum_grad = cum_grad + head_sums(decayed * fine(nt, c_act, state), pair, heads)
        grad_c = grad_c + fine(nn, split(decayed), state)
    low_scores = split(grad_scores[...])
    grad_bc[:, 0:NST] = fine(tn, low_scores, c_act)
    grad_bc[:, NST:] = grad_c + fine(nn, low_scores, b_act)
    grad_rows[0:heads, :] = cum_grad + row_sums[...].T[0:heads, :] - col_sums[...]
    grad_rows[heads:, :] = step_grad
    skip_grad[...] = jnp.broadcast_to(jnp.sum(direct_sum, axis=1, keepdims=True), (heads, 128))


def scan_back(ends, idx, conv, table, table_t, grad, entering, params, micro_count, row_count):
    width = grad.shape[1]
    heads = width // P_SIZE
    total = micro_count * row_count
    square = pltpu.VMEM((row_count, row_count), F32)
    return call(
        scan_back_body,
        (micro_count,),
        (ends, idx),
        [conv, table, table_t, grad, entering, params.skip],
        [
            rows(row_count, width + 2 * NST),
            rows(row_count, 128),
            rows(128, row_count),
            rows(row_count, width),
            rows(width, NST),
            whole((1, width)),
        ],
        [
            struct((total, width)),
            struct((total, 2 * NST)),
            struct((micro_count * 2 * heads, row_count)),
            struct((micro_count * heads, 128)),
        ],
        [
            rows(row_count, width),
            rows(row_count, 2 * NST),
            rows(2 * heads, row_count),
            rows(heads, 128),
        ],
        [square, square, square, pltpu.VMEM((row_count, 128), F32), pltpu.VMEM((heads, row_count), F32)],
        flops=100 * total * row_count * heads,
    )


def finish_body(
    idx, conv, table, table_t, grad_x, grad_bc, grad_rows, later, entering, head_cols,
    grad_value, grad_select, grad_step, small, weighted, weighted_low,
):
    row_count, width = grad_x.shape
    heads = width // P_SIZE
    b_pre = conv[:, width : width + NST]
    b_sig = sigmoid(b_pre)
    b_act = split(b_pre * b_sig)
    lane = lax.broadcasted_iota(jnp.int32, (row_count, 128), 1)
    end_grad = jnp.zeros((heads, row_count), F32)
    for pair in range(width // 128):
        span = slice(128 * pair, 128 * pair + 128)
        pre = conv[:, span]
        sig = sigmoid(pre)
        x_act = pre * sig
        end_pair = pair_of(table[...], ENDW, pair, lane)
        reached = fine(nt, b_act, split(later[span, :]))
        end_grad = end_grad + head_sums(x_act * reached, pair, heads)
        weighted[:, span], weighted_low[:, span] = split(x_act * end_pair)
        grad_value[:, span] = (grad_x[:, span] + end_pair * reached) * (
            sig * (1.0 + pre * (1.0 - sig))
        )
    grad_b = grad_bc[:, 0:NST] + fine(nn, (weighted[...], weighted_low[...]), split(later[...]))
    grad_select[:, 0:NST] = grad_b * (b_sig * (1.0 + b_pre * (1.0 - b_sig)))
    c_pre = conv[:, width + NST :]
    c_sig = sigmoid(c_pre)
    grad_select[:, NST:] = grad_bc[:, NST:] * (c_sig * (1.0 + c_pre * (1.0 - c_sig)))

    crossing = (later[...] * entering[...]).reshape(heads, P_SIZE, NST)
    crossing = jnp.sum(jnp.sum(crossing, axis=1), axis=1, keepdims=True)
    end_weighted = end_grad * table_t[ENDW : ENDW + heads, :]
    last = jnp.sum(end_weighted, axis=1, keepdims=True) + crossing * table_t[
        DECIN : DECIN + heads, row_count - 1 : row_count
    ]
    place = lax.broadcasted_iota(jnp.int32, (heads, row_count), 1)
    cum_grad = grad_rows[0:heads, :] - end_weighted + jnp.where(place == row_count - 1, last, 0.0)
    row_id = lax.broadcasted_iota(jnp.int32, (row_count, row_count), 0)
    col_id = lax.broadcasted_iota(jnp.int32, (row_count, row_count), 1)
    grad_decay = nn(cum_grad, (row_id >= col_id).astype(F32), EXACT)
    step_grad = grad_rows[heads:, :] + end_grad * table_t[BASE : BASE + heads, :]
    grad_pre = (step_grad - grad_decay * jnp.exp(head_cols[:, 0:1])) * table_t[SIG : SIG + heads, :]
    small[...] = jnp.zeros_like(small)
    small[:, 0:1] = jnp.sum(grad_pre, axis=1, keepdims=True)
    small[:, 1:2] = jnp.sum(grad_decay * table_t[LOG : LOG + heads, :], axis=1, keepdims=True)
    padded = jnp.concatenate([grad_pre, jnp.zeros((128 - heads, row_count), F32)], axis=0)
    grad_step[...] = padded.T.astype(BF16).astype(F32)


def scan_finish(
    idx, conv, table, table_t, grad_x, grad_bc, grad_rows, later, entering, params, micro_count, row_count
):
    width = grad_x.shape[1]
    heads = width // P_SIZE
    total = micro_count * row_count
    return call(
        finish_body,
        (micro_count,),
        (idx,),
        [conv, table, table_t, grad_x, grad_bc, grad_rows, later, entering, params.head_cols],
        [
            rows(row_count, width + 2 * NST),
            rows(row_count, 128),
            rows(128, row_count),
            rows(row_count, width),
            rows(row_count, 2 * NST),
            rows(2 * heads, row_count),
            rows(width, NST),
            rows(width, NST),
            whole((heads, 128)),
        ],
        [
            struct((total, width)),
            struct((total, 2 * NST)),
            struct((total, 128)),
            struct((micro_count * heads, 128)),
        ],
        [rows(row_count, width), rows(row_count, 2 * NST), rows(row_count, 128), rows(heads, 128)],
        [pltpu.VMEM((row_count, width), BF16), pltpu.VMEM((row_count, width), BF16)],
        flops=60 * total * width,
    )


def taps_back(taps, own_grads, inputs, row_count, span, before, after, tap_grads):
    own = own_grads[0:row_count, span]
    tap_grads[4:5, span] = jnp.sum(own, axis=0, keepdims=True)
    tap_grads[3:4, span] = jnp.sum(own * inputs[8:, span], axis=0, keepdims=True)
    total = own * taps[3:4, span]
    for step in range(1, K):
        tap = K - 1 - step
        tap_grads[tap : tap + 1, span] = jnp.sum(
            own * (inputs[8 - step : 8 - step + row_count, span] * before[step - 1]),
            axis=0,
            keepdims=True,
        )
        total = total + taps[tap : tap + 1, span] * (
            own_grads[step : step + row_count, span] * after[step - 1]
        )
    return total.astype(BF16)


def near_masks(ends, idx, row_count):
    micro = pl.program_id(0)
    at = idx[0] + lax.broadcasted_iota(jnp.int32, (row_count, 1), 0)
    seg = seg_at(at, ends, micro)
    before = [(seg_at(at - step, ends, micro) == seg).astype(F32) for step in range(1, K)]
    after = [(seg_at(at + step, ends, micro) == seg).astype(F32) for step in range(1, K)]
    return (before, after)


def conv_back_body(
    ends, idx, grad_value, halo_value, value, halo_in, taps, gate_part, grad_step, w_value, w_step,
    low_value, tap_grads, c0, c1, c2, c3,
    grads, extended, low, product,
):
    row_count, width = grad_value.shape
    chunk = row_count // 4
    before, after = near_masks(ends, idx, row_count)
    grads[0:row_count, :] = grad_value[...]
    grads[row_count:, :] = halo_value[...]
    extended[0:8, :] = halo_in[...]
    extended[8:, :] = value[...]
    tap_grads[...] = jnp.zeros_like(tap_grads)
    for left in range(0, width, 128):
        span = slice(left, left + 128)
        rounded = taps_back(taps, grads, extended, row_count, span, before, after, tap_grads)
        low[:, span] = rounded
        low_value[:, span] = rounded.astype(F32)
    low_step = grad_step[:, 0 : w_step.shape[1]].astype(BF16)
    for left in range(0, D, 512):
        span = slice(left, left + 512)
        product[:, span] = (
            gate_part[:, span] + nt(low[...], w_value[span, :]) + nt(low_step, w_step[span, :])
        )
    for piece, target in enumerate((c0, c1, c2, c3)):
        place = pl.multiple_of((idx[1] ^ piece) * chunk, chunk)
        target[...] = product[pl.ds(place, chunk), :]


def conv_back(
    ends, idx, grad_value, halo_value, value, halo_in, gate_part, grad_step, params, weights, micro_count, row_count
):
    width = grad_value.shape[1]
    heads = weights.step.shape[1]
    total = micro_count * row_count
    chunk = row_count // 4
    return call(
        conv_back_body,
        (micro_count,),
        (ends, idx),
        [
            grad_value, halo_value, value, halo_in, params.taps, gate_part, grad_step, weights.value,
            weights.step,
        ],
        [
            rows(row_count, width),
            rows(8, width),
            rows(row_count, width),
            rows(8, width),
            whole((8, width)),
            rows(row_count, D),
            rows(row_count, 128),
            whole((D, width)),
            whole((D, heads)),
        ],
        [struct((total, width + 128)), struct((micro_count * 8, width))] + [struct((micro_count * chunk, D))] * 4,
        [rows(row_count, width), rows(8, width)] + [rows(chunk, D)] * 4,
        [
            pltpu.VMEM((row_count + 8, width), F32),
            pltpu.VMEM((row_count + 8, width), F32),
            pltpu.VMEM((row_count, width), BF16),
            pltpu.VMEM((row_count, D), F32),
        ],
        flops=2 * total * width * D,
    )


def select_back_body(
    ends, idx, s0, s1, s2, s3, halo, select, halo_in, taps, grad_step, kept,
    low_select, tap_grads, rest, grads, extended,
):
    del kept
    row_count, columns = select.shape
    before, after = near_masks(ends, idx, row_count)
    grads[0:row_count, :] = (s0[...] + s1[...]) + (s2[...] + s3[...])
    grads[row_count:, :] = halo[...]
    extended[0:8, :] = halo_in[...]
    extended[8:, :] = select[...]
    tap_grads[...] = jnp.zeros_like(tap_grads)
    for left in range(0, columns, 128):
        span = slice(left, left + 128)
        rounded = taps_back(taps, grads, extended, row_count, span, before, after, tap_grads)
        low_select[:, span] = rounded.astype(F32)
    part = columns // 4
    rest[:, part:] = grad_step[:, 0 : 128 - part]
    for head in range(4):

        @pl.when(idx[1] == head)
        def _():
            rest[:, 0:part] = low_select[:, head * part : (head + 1) * part]


def select_back(ends, idx, selects, halo, select, halo_in, grad_step, kept, params, micro_count, row_count):
    total, columns = select.shape
    width = kept.shape[1] - 128
    right = width // columns
    ins = [*selects, halo, select, halo_in, params.taps, grad_step, kept]
    outs = [
        struct((total, columns)),
        struct((micro_count * 8, columns)),
        struct((total, width + 128)),
    ]

    def guarded(*refs):
        @pl.when(refs[1][4] == 1)
        def _():
            select_back_body(*refs)

    return pl.pallas_call(
        guarded,
        grid_spec=pltpu.PrefetchScalarGridSpec(
            num_scalar_prefetch=2,
            grid=(micro_count,),
            in_specs=[rows(row_count, columns)] * 4
            + [
                rows(8, columns),
                rows(row_count, columns),
                pl.BlockSpec((8, columns), lambda m, *_: (m, right)),
                pl.BlockSpec((8, columns), lambda m, *_: (0, right)),
                rows(row_count, 128),
                pl.BlockSpec(memory_space=pl.ANY),
            ],
            out_specs=[
                rows(row_count, columns),
                rows(8, columns),
                pl.BlockSpec((row_count, 128), lambda m, *_: (m, width // 128)),
            ],
            scratch_shapes=[
                pltpu.VMEM((row_count + 8, columns), F32),
                pltpu.VMEM((row_count + 8, columns), F32),
            ],
        ),
        out_shape=outs,
        input_output_aliases={11: 2},
        compiler_params=pltpu.CompilerParams(vmem_limit_bytes=VMEM_BYTES),
        cost_estimate=pl.CostEstimate(flops=30 * total * columns, bytes_accessed=9 * total * columns * 4, transcendentals=0),
    )(ends, idx, *ins)


def weight_body(idx, split, split_other, kept, kept_other, far, own, *, flip):
    def product(a, b):
        return tn(b, a) if flip else tn(a, b)

    low = kept[...].astype(BF16)
    low_other = kept_other[...].astype(BF16)
    result = product(split[...], low) + product(split_other[...].astype(BF16), low_other)

    @pl.when(pl.program_id(0) == 0)
    def _():
        far[...] = result

    @pl.when(pl.program_id(0) == 1)
    def _():
        own[...] = result


def weight_grad(idx, split, split_other, kept, kept_other, flip):
    total, width = kept.shape
    block = split.shape[1] // 4
    shape = (width, block) if flip else (block, width)
    return call(
        partial(weight_body, flip=flip),
        (2,),
        (idx,),
        [split, split_other, kept, kept_other],
        [
            pl.BlockSpec((total, block), lambda b, idx: (0, idx[2] ^ (2 - 2 * b))),
            pl.BlockSpec((total, block), lambda b, idx: (0, b)),
            whole((total, width)),
            whole((total, width)),
        ],
        [struct(shape), struct(shape)],
        [whole(shape), whole(shape)],
        flops=8 * total * block * width,
    )


def join_body(idx, p0, p1, p2, p3, *refs):
    out = refs[-1]
    chunk = p0.shape[0]
    use_other = idx[3] == 1 if len(refs) > 1 else False

    def from_parts():
        for piece, part in enumerate((p0, p1, p2, p3)):
            out[pl.ds(pl.multiple_of((idx[1] ^ piece) * chunk, chunk), chunk), :] = part[...]

    if len(refs) == 1:
        from_parts()
    else:

        @pl.when(use_other)
        def _():
            out[...] = refs[0][...]

        pl.when(jnp.logical_not(use_other))(from_parts)


def join(idx, parts, other, micro_count, row_count):
    chunk = row_count // 4
    others = [] if other is None else [other]
    return call(
        join_body,
        (micro_count,),
        (idx,),
        [*parts, *others],
        [rows(chunk, D)] * 4 + [rows(row_count, D)] * len(others),
        [struct((micro_count * row_count, D))],
        [rows(row_count, D)],
    )[0]


def after(value, *others):
    return lax.optimization_barrier((value, *others))[0]


def shards(
    block_input,
    out_grad,
    lengths,
    norm_gain,
    gate_weight,
    value_weight,
    select_weight,
    step_weight,
    conv_value,
    conv_value_bias,
    conv_select,
    conv_select_bias,
    step_bias,
    log_rate,
    skip_gain,
    gate_gain,
    output_weight,
):
    micros, row_count, _ = block_input.shape
    total = micros * row_count
    width = gate_weight.shape[2]
    heads = width // P_SIZE
    chunk = row_count // 4
    tok_count = lax.axis_size(TOK)
    section, tok, head = (lax.axis_index(axis) for axis in AXES)
    ends = jnp.cumsum(lengths, axis=1).astype(jnp.int32)

    def scalars(flag, active):
        values = [tok * row_count, head, tok, flag, active]
        return jnp.stack([jnp.asarray(value, jnp.int32) for value in values])

    weights = SimpleNamespace(
        gain=norm_gain,
        gate=gate_weight[0],
        value=value_weight[0],
        select=select_weight[0],
        step=step_weight[0],
        out=output_weight[0],
        gate_gain=gate_gain[0].reshape(1, width),
    )
    taps = jnp.concatenate(
        [
            jnp.concatenate([conv_value[0].reshape(K, width), conv_select[0]], axis=1),
            jnp.concatenate([conv_value_bias[0].reshape(1, width), conv_select_bias], axis=1),
            jnp.zeros((3, width + 2 * NST), F32),
        ],
        axis=0,
    )
    params = SimpleNamespace(
        taps=taps,
        head_rows=jnp.pad(jnp.concatenate([step_bias, log_rate], axis=0), ((0, 6), (0, 128 - heads))),
        head_cols=jnp.pad(log_rate[0][:, None], ((0, 0), (0, 127))),
        skip=jnp.repeat(skip_gain[0], P_SIZE)[None, :],
    )

    def chunk_of(values):
        parts = values.reshape(micros, 4, chunk, values.shape[-1])
        mine = lax.dynamic_index_in_dim(parts, head, 1, keepdims=False)
        return mine.reshape(micros * chunk, values.shape[-1])

    def gather(values, layer):
        return [values] + [to_head(values, layer, step) for step in (1, 2, 3)]

    def reduce_chunks(parts, layer):
        moved = [to_head(parts[step], layer, step) for step in (1, 2, 3)]
        return (parts[0] + moved[0]) + (moved[1] + moved[2])

    def wave(layer, local, table, backward, ahead):
        decay = table.reshape(micros, row_count, 128)[:, row_count - 1, DECIN : DECIN + heads]
        shape = (micros, heads, P_SIZE, NST)
        entering = None
        for hop in range(tok_count - 1):
            leaving = local
            if entering is not None:
                leaving = (
                    local.reshape(shape) + decay[:, :, None, None] * entering.reshape(shape)
                ).reshape(local.shape)
            source = tok_count - 1 - hop if backward else hop
            target = source - 1 if backward else source + 1

            def move(t, h, source=source, target=target):
                return (target if t == source else -1, h)

            if hop in ahead:
                leaving = after(leaving, *ahead[hop])
            received = send(leaving, layer, move)
            entering = received if entering is None else entering + received
        return entering

    def forward(layer, parts, chunk_in):
        idx = scalars(0, section == layer)
        normed, value, select, step = in_project(idx, parts, weights, micros, row_count)
        edge = jnp.concatenate(
            [
                value.reshape(micros, row_count, width)[:, row_count - 8 :],
                select.reshape(micros, row_count, 2 * NST)[:, row_count - 8 :],
            ],
            axis=-1,
        ).reshape(micros * 8, width + 2 * NST)
        halo = to_tok(edge, layer, 1)
        conv, table, table_t, state = conv_state(
            ends, idx, value, select, step, halo, params, micros, row_count
        )
        gate = gate_project(idx, after(normed, state), weights.gate)
        local = scan_local(ends, idx, conv, table, table_t, params, micros, row_count)
        entering = wave(layer, state, table, False, {1: (gate, local)})
        scan, gated, sums = gate_mix(idx, local, conv, table, entering, gate, micros, row_count)
        scaled, inverse, *pieces = out_project(
            idx, gated, gather(sums, layer), weights, micros, row_count
        )
        branch = reduce_chunks(pieces, layer)
        saved = SimpleNamespace(
            normed=normed, gate=gate, value=value, select=select, halo=halo, conv=conv,
            table=table, table_t=table_t, entering=entering, scan=scan, inverse=inverse,
            scaled=scaled, branch=branch, chunk_in=chunk_in,
        )
        return (chunk_in + branch, saved)

    def norm_lanes(grad_chunk, branch):
        low = lax.reduce_precision(grad_chunk, 8, 7)
        inner = jnp.sum(low * branch, axis=-1, keepdims=True) / (H * P_SIZE)
        return jnp.broadcast_to(inner, (micros * chunk, PAD))

    def exchange(layer, values):
        return send(values, layer, lambda t, h: (t ^ 1, h))

    def split_blocks(values):
        block = values.shape[1] // 4
        return jnp.concatenate(
            [
                lax.dynamic_slice_in_dim(values, (tok ^ 3) * block, block, 1),
                lax.dynamic_slice_in_dim(values, (tok ^ 1) * block, block, 1),
            ],
            axis=1,
        ).astype(F32)

    def backward(layer, saved, grad, norm_parts, grad_chunk, pairs, shown, ahead, waits):
        idx = scalars(0, section == layer)
        low_grad, grad_gate, grad_scan, state, gain_grad, *full = gated_back(
            idx, grad, norm_parts, saved.gate, saved.scan, saved.inverse, saved.conv, saved.table,
            weights, micros, row_count,
        )
        grad_x, grad_bc, grad_rows, skip_grad = scan_back(
            ends, idx, saved.conv, saved.table, saved.table_t, grad_scan, saved.entering, params,
            micros, row_count,
        )
        gate_part = lax.dot_general(
            after(grad_gate, grad_bc).astype(BF16),
            weights.gate,
            (((1,), (1,)), ((), ())),
            preferred_element_type=F32,
        )
        pieces = shown(state)
        later = wave(
            layer,
            state,
            saved.table,
            True,
            {1: (grad_bc, *ahead[0], *pieces[1:2]), 2: (gate_part, *ahead[1], *pieces[2:3])},
        )
        later = after(later, *pieces[3:], *waits[0])
        grad_value, grad_select, grad_step, small = scan_finish(
            idx, saved.conv, saved.table, saved.table_t, grad_x, grad_bc, grad_rows, later,
            saved.entering, params, micros, row_count,
        )
        first_value = grad_value.reshape(micros, row_count, width)[:, :8].reshape(micros * 8, width)
        halo_value = to_tok(first_value, layer, -1)
        selects = gather(grad_select, layer)
        low_value, value_taps, *pieces = conv_back(
            ends, idx, grad_value, halo_value, saved.value, saved.halo, gate_part, grad_step, params,
            weights, micros, row_count,
        )
        kept = SimpleNamespace(scaled=saved.scaled, gate=grad_gate, low_grad=low_grad)
        products, first_needed = pairs(kept, halo_value)
        grad_normed = after(reduce_chunks(pieces, layer), *first_needed, *waits[1])
        first_select = sum(
            part.reshape(micros, row_count, 2 * NST)[:, :8].reshape(micros * 8, 2 * NST) for part in selects
        )
        halo_select = to_tok(first_select, layer, -1)
        low_select, select_taps, low_rest = select_back(
            ends, idx, selects, halo_select, saved.select, saved.halo, grad_step, low_value, params,
            micros, row_count,
        )
        grad_normed = grad_normed + lax.dot_general(
            chunk_of(low_select).astype(BF16),
            weights.select,
            (((1,), (1,)), ((), ())),
            preferred_element_type=F32,
        )
        hidden = saved.chunk_in
        inv = lax.rsqrt(jnp.mean(hidden * hidden, axis=-1, keepdims=True) + EPSILON)
        norm_grad = jnp.sum(grad_normed * hidden * inv, axis=0)
        weighted = grad_normed * weights.gain
        grad_hidden = (
            grad_chunk
            + inv * weighted
            - hidden * (inv * inv * inv) * jnp.mean(weighted * hidden, axis=-1, keepdims=True)
        )
        kept.value = low_rest
        sums = (
            norm_grad,
            jnp.concatenate(
                [
                    value_taps.reshape(micros, 8, -1)[:, : K + 1].sum(0).reshape(-1),
                    select_taps.reshape(micros, 8, -1)[:, : K + 1].sum(0).reshape(-1),
                    gain_grad.reshape(micros, 8, -1)[:, 0].sum(0),
                    small.reshape(micros, heads, 128).sum(0)[:, :2].T.reshape(-1),
                    skip_grad.reshape(micros, heads, 128).sum(0)[:, 0],
                ]
            ),
        )
        return (grad_hidden, kept, sums, full, products)

    def pair_product(layer, split, split_other, kept, flip, other):
        idx = scalars(0, section == layer)
        far, own = weight_grad(idx, split, split_other, kept, other, flip)
        return (own, send(far, layer, lambda t, h: (t ^ 2, h)))

    first = section == 0
    pairwise = tok_count == 4
    grad_rows_1 = out_grad.reshape(total, D)

    input_rows = block_input.reshape(total, D)
    chunk_0 = chunk_of(input_rows).astype(F32)
    out_0, saved_0 = forward(0, [input_rows], chunk_0)
    moved = out_0
    if pairwise:
        grad_other_1 = exchange(1, split_blocks(grad_rows_1))
        moved = after(out_0, grad_other_1)

    chunk_1 = lax.ppermute(moved, SECTION, [(0, 1)])
    parts_1 = gather(chunk_1, 1)
    if pairwise:
        other_0 = exchange(0, after(split_blocks(saved_0.normed), out_0))
        scaled_0 = exchange(0, after(saved_0.scaled, out_0))
        parts_1[0] = after(parts_1[0], other_0)
    out_1, saved_1 = forward(1, parts_1, chunk_1)

    grad_chunk_1 = chunk_of(grad_rows_1).astype(F32)
    lanes_1 = norm_lanes(grad_chunk_1, saved_1.branch)
    all_lanes_1 = gather(lanes_1, 1)
    if pairwise:
        other_1 = exchange(1, after(split_blocks(saved_1.normed), saved_1.entering))
        scaled_1 = exchange(1, saved_1.scaled)
        all_lanes_1[0] = after(all_lanes_1[0], other_1, scaled_0)

    def pairs_1(kept, done):
        if not pairwise:
            return ([], ())
        products = [
            pair_product(1, kept.low_grad, grad_other_1, kept.scaled, True, scaled_1),
            pair_product(1, saved_1.normed, other_1, kept.gate, False, exchange(1, after(kept.gate, done))),
        ]
        return (products, (products[0][0],))

    shown_1 = []

    def show_1(state):
        shown_1.extend(gather(after(out_1, state), 1))
        return shown_1

    grad_mid, kept_1, sums_1, _, big_1 = backward(
        1, saved_1, grad_rows_1, all_lanes_1, grad_chunk_1, pairs_1, show_1, ((scaled_1,) if pairwise else (), ()), ((), ())
    )
    full_1 = join(scalars(0, section == 1), parts_1, None, micros, row_count)
    layer_out = join(
        scalars(first, 1), shown_1, lax.ppermute(full_1, SECTION, [(1, 0)]), micros, row_count
    )
    if pairwise:
        big_1.append(
            pair_product(1, saved_1.normed, other_1, kept_1.value, False, exchange(1, kept_1.value))
        )

    grad_chunk_0 = lax.ppermute(grad_mid, SECTION, [(1, 0)])
    lanes_0 = norm_lanes(grad_chunk_0, saved_0.branch)
    payload = jnp.concatenate([grad_chunk_0, lanes_0], axis=1)

    def pairs_0(kept, done):
        if not pairwise:
            return ([], ())
        grad_other_0 = exchange(0, after(split_blocks(kept.low_grad), done))
        products = [
            pair_product(0, saved_0.normed, other_0, kept.gate, False, exchange(0, after(kept.gate, done))),
            pair_product(0, kept.low_grad, grad_other_0, kept.scaled, True, scaled_0),
        ]
        return (products, (products[0][0],))

    parts_0 = gather(payload, 0)
    ahead, waits = (((), ()), ((), ()))
    if pairwise:
        (_, scaled_far), (gate_own, gate_far), (value_own, value_far) = big_1
        parts_0[0] = after(parts_0[0], gate_own, scaled_far)
        ahead = ((value_own, gate_far), ())
        waits = ((), (value_far,))
    grad_in, kept_0, sums_0, (full_0,), big_0 = backward(
        0, saved_0, None, parts_0, grad_chunk_0, pairs_0, lambda state: [], ahead, waits
    )
    input_grad = join(
        scalars(section == 1, 1),
        gather(grad_in, 0),
        lax.ppermute(full_0, SECTION, [(0, 1)]),
        micros,
        row_count,
    )

    def chosen(left, right):
        return jnp.where(first, left, right)

    if pairwise:
        last = after(saved_0.normed, big_0[0][1])
        big_0.append(pair_product(0, last, other_0, kept_0.value, False, exchange(0, kept_0.value)))
        big_0[0], big_0[1] = (big_0[1], big_0[0])
        scaled_sum, gate_sum, value_sum = (
            chosen(own_0 + far_0, own_1 + far_1)
            for (own_0, far_0), (own_1, far_1) in zip(big_0, big_1, strict=True)
        )
    else:
        normed = chosen(saved_0.normed, saved_1.normed)

        def scattered(left, right, axis):
            return lax.psum_scatter(
                tn(left.astype(BF16), right.astype(BF16)), TOK, scatter_dimension=axis, tiled=True
            )

        scaled_sum = scattered(
            chosen(kept_0.scaled, kept_1.scaled), chosen(kept_0.low_grad, kept_1.low_grad), 1
        )
        gate_sum = scattered(normed, chosen(kept_0.gate, kept_1.gate), 0)
        value_sum = scattered(normed, chosen(kept_0.value, kept_1.value), 0)
    quarter = 2 * NST // 4
    select_sum = lax.all_gather(value_sum[:, width : width + quarter], HEAD, axis=1, tiled=True)

    def sum_over(values, axis):
        count = lax.axis_size(axis)
        if count != 4:
            return lax.psum(values, axis)
        moved = [
            lax.ppermute(values, axis, [(source, source ^ step) for source in range(count)])
            for step in (1, 2, 3)
        ]
        return (values + moved[0]) + (moved[1] + moved[2])

    norm_sum, head_sum = (chosen(left, right) for left, right in zip(sums_0, sums_1, strict=True))
    packed = sum_over(jnp.concatenate([norm_sum, head_sum]), TOK)
    norm_sum = sum_over(lax.dynamic_slice_in_dim(packed[:D], tok * (D // tok_count), D // tok_count, 0), HEAD)
    head_sum = packed[D:]
    pieces, place = ([], 0)
    for shape in ((K + 1, width), (K + 1, 2 * NST), (heads, P_SIZE), (heads,), (heads,), (heads,)):
        size = 1
        for extent in shape:
            size *= extent
        pieces.append(head_sum[place : place + size].reshape(shape))
        place += size
    value_taps, select_taps, gain_sum, bias_sum, rate_sum, skip_sum = pieces

    def mine(values, axis):
        size = values.shape[axis] // tok_count
        return lax.dynamic_slice_in_dim(values, tok * size, size, axis)

    outs = (
        layer_out.reshape(micros, row_count, D),
        input_grad.reshape(micros, row_count, D),
        norm_sum,
        gate_sum,
        value_sum[:, :width],
        select_sum,
        value_sum[:, width + quarter : width + quarter + heads],
        mine(value_taps[:K].reshape(K, heads, P_SIZE), 2),
        mine(value_taps[K].reshape(heads, P_SIZE), 1),
        mine(select_taps[:K], 1),
        mine(select_taps[K], 0),
        bias_sum,
        rate_sum,
        skip_sum,
        mine(gain_sum, 1),
        scaled_sum,
    )
    return tuple(value[None] for value in outs)


def solution(mesh):
    return jax.shard_map(
        shards,
        mesh=mesh,
        in_specs=(
            P(None, TOK, None),
            P(None, TOK, None),
            P(),
            P(SECTION, None),
            P(SECTION, None, HEAD),
            P(SECTION, None, HEAD),
            P(SECTION, None, None),
            P(SECTION, None, HEAD),
            P(SECTION, None, HEAD, None),
            P(SECTION, HEAD, None),
            P(SECTION, None, None),
            P(SECTION, None),
            P(SECTION, HEAD),
            P(SECTION, HEAD),
            P(SECTION, HEAD),
            P(SECTION, HEAD, None),
            P(SECTION, HEAD, None),
        ),
        out_specs=(
            P(SECTION, None, TOK, None),
            P(SECTION, None, TOK, None),
            P(SECTION, TOK),
            P(SECTION, TOK, HEAD),
            P(SECTION, TOK, HEAD),
            P(SECTION, TOK, None),
            P(SECTION, TOK, HEAD),
            P(SECTION, None, HEAD, TOK),
            P(SECTION, HEAD, TOK),
            P(SECTION, None, TOK),
            P(SECTION, TOK),
            P(SECTION, HEAD),
            P(SECTION, HEAD),
            P(SECTION, HEAD),
            P(SECTION, HEAD, TOK),
            P(SECTION, HEAD, TOK),
        ),
        check_vma=False,
    )
```

time: 2080 us -> 953 us (0.46)
  waiting for transfers between devices: 1050 us -> 391 us
  matrix products: 346 us -> 14 us
  Pallas kernels: 0 us -> 231 us
  other arithmetic: 268 us -> 58.5 us
  local copies, waits for them, and re-layouts: 223 us -> 33.4 us
  starting transfers between devices: 27.3 us -> 200 us
  blocking collectives: 136 us -> 10.4 us
  between operations: 26.6 us -> 2.83 us
    reduce_scatter x5 -> x0, waiting for transfers between devices: 479 us -> none  [the longest x1 148 us: reduce_grads(): lax.psum_scatter(gradients[1], 'tok', scatter_dimension=0, tiled=True)]
    psum x8 -> x0, waiting for transfers between devices: 442 us -> none  [the longest x3 212 us: forward_layer(): lax.psum(jnp.dot(scaled, weights[13], preferred_element_type=jnp.float32)...]
    ppermute x10 -> x83, waiting for transfers between devices: 10.9 us -> 391 us  [the longest x73 185 us: send(): return lax.ppermute(value, AXES, pairs)]
    dot_general x111 -> x4, matrix products: 346 us -> 14 us  [the longest x2 11.6 us: backward(): lax.dot_general(after(grad_gate, grad_bc).astype(BF16), weights.gate, (((...]
    pallas_call x0 -> x31, Pallas kernels: none -> 231 us  [the longest x29 222 us: call(): pl.pallas_call(guarded, grid_spec=pltpu.PrefetchScalarGridSpec(num_scalar...]
    ppermute x10 -> x83, starting transfers between devices: 25.8 us -> 200 us  [the longest x73 171 us: send(): return lax.ppermute(value, AXES, pairs)]
    all_gather x6 -> x0, waiting for transfers between devices: 90.6 us -> none  [entering_2(): pieces = jax.tree.map(lambda part: lax.all_gather(part, axis), value)]
    psum x6 -> x0, blocking collectives: 58.3 us -> none  [the longest x3 30.5 us: forward_layer(): square_sum = lax.psum(jnp.sum(gated_value * gated_value, axis=-1), 'head')]
  transfers between devices with their start and end apart: 33 -> 83, of which waited for: 23 -> 20; matrix products, arithmetic and copies ran while one was open for 16% -> 9% of each run, Pallas kernels for 0% -> 21%
where the time goes in v1:
time: 953 us; the launch traced here: 941 us
  waiting for transfers between devices  391 us (41%)
  Pallas kernels  231 us (24%)
  starting transfers between devices  200 us (21%)
  other arithmetic  58.5 us (6%)
  local copies, waits for them, and re-layouts  33.4 us (4%)
  matrix products  14 us (1%)
  blocking collectives  10.4 us (1%)
    pallas_call x29, Pallas kernels, call(): pl.pallas_call(guarded, grid_spec=pltpu.PrefetchScalarGridSpec(num_scalar...  222 us
    ppermute x73, waiting for transfers between devices, send(): return lax.ppermute(value, AXES, pairs)  185 us
    ppermute x1, waiting for transfers between devices, shards(): grad_chunk_0 = lax.ppermute(grad_mid, SECTION, [(1, 0)])  173 us
    ppermute x73, starting transfers between devices, send(): return lax.ppermute(value, AXES, pairs)  171 us
    ppermute x6, waiting for transfers between devices, sum_over(): lax.ppermute(values, axis, [(source, source ^ step) for source in range(c...  31 us
    ppermute x6, starting transfers between devices, sum_over(): lax.ppermute(values, axis, [(source, source ^ step) for source in range(c...  22.2 us
  transfers between devices with their start and end apart: 83, of which 20 were waited for; matrix products, arithmetic and copies ran while one was open for 9% of the time, Pallas kernels for 21%

profile of v1, /device:TPU:0, one launch (start us, length us, event | category | flops | bytes accessed | tf_op | source)
XLA Modules:
  0.0 941.2 jit_solution(16747774814772100125)
XLA Ops:
  3.2 10.3 %shard_map.288 = (bf16[512,2048]{1,0:T(8,128)(2,1)}, f32[512,1024]{1,0:T(8,128)}, f32[512,256]{1,0:T(8,128)}, f32[512,16]{1,0:T(8,128)}) custom-call(s32[5]{0:T(128)} %stack.30.refs_0_.refs_1_, bf16[512,2048]{1,0:T(8,128)(2,1)} %bitcast.171, f32[1,2048]{1,0:T(1,128)} %refs_5_.1, bf16[2048,1024]{1,0:T(8,128)(2,1)} %bitcast.141, bf16[2048,256]{1,0:T(8,128)(2,1)} %bitcast.151, ...), custom_call_target="tpu_custom_call" | custom-call | flops 2684354560 | bytes 12165120 | tf_op jit(solution)/shard_map/pallas_call | solution.py:100
  22.9 9.5 %shard_map.289 = (f32[512,1280]{1,0:T(8,128)}, f32[512,128]{1,0:T(8,128)}, f32[256,256]{1,0:T(8,128)}, f32[2048,128]{1,0:T(8,128)}) custom-call(s32[2,4]{1,0:T(2,128)} %reduce_window_sum.11.refs_0_, s32[5]{0:T(128)} %stack.30.refs_0_.refs_1_, f32[512,1024]{1,0:T(8,128)} %get-tuple-element.132.refs_2_.refs_4_, f32[512,256]{1,0:T(8,128)} %get-tuple-element.133.refs_3_.refs_7_, ...), custom_call_target="tpu_custom_call" | custom-call | flops 20971520 | bytes 6975488 | tf_op jit(solution)/shard_map/pallas_call | solution.py:100
  39.1 8.2 shard_map.290.refs_1_
  86.8 8.7 shard_map.293
  112.5 13.8 %collective-permute-done.8 = f32[128,2048]{1,0:T(8,128)} collective-permute-done((f32[128,2048]{1,0:T(8,128)}, f32[128,2048]{1,0:T(8,128)}, u32[]{:S(2)}, u32[]{:S(2)}) %collective-permute-start.8) | collective-permute-done | bytes 1048608 | tf_op jit(solution)/shard_map/ppermute | solution.py:39
  129.5 15.7 %collective-permute-start.12 = (f32[512,1024]{1,0:T(8,128)}, f32[512,1024]{1,0:T(8,128)}, u32[]{:S(2)}, u32[]{:S(2)}) collective-permute-start(f32[512,1024]{1,0:T(8,128)} %maximum_convert_fusion.1), channel_id=1, source_target_pairs={{0,4},{1,5},{2,6},{3,7},{4,0},{5,1},{6,2},{7,3},{8,12},{9,13},{10,... | collective-permute-start | bytes 6291464 | tf_op jit(solution)/shard_map/ppermute | solution.py:39
  152.4 17.0 %collective-permute-done.12.refs_2_ = f32[512,1024]{1,0:T(8,128)} collective-permute-done((f32[512,1024]{1,0:T(8,128)}, f32[512,1024]{1,0:T(8,128)}, u32[]{:S(2)}, u32[]{:S(2)}) %collective-permute-start.12) | collective-permute-done | bytes 2097184 | tf_op jit(solution)/shard_map/ppermute | solution.py:39
  310.9 172.5 %collective-permute-done.47 = f32[128,2048]{1,0:T(8,128)S(1)} collective-permute-done((f32[128,2048]{1,0:T(8,128)S(1)}, f32[128,2048]{1,0:T(8,128)S(1)}, u32[]{:S(2)}, u32[]{:S(2)}) %collective-permute-start.47) | collective-permute-done | bytes 1048608 | tf_op jit(solution)/shard_map/ppermute | solution.py:1249
  503.0 11.8 %collective-permute-done.51.refs_3_ = f32[128,2176]{1,0:T(8,128)} collective-permute-done((f32[128,2176]{1,0:T(8,128)S(1)}, f32[128,2176]{1,0:T(8,128)}, u32[]{:S(2)}, u32[]{:S(2)}) %collective-permute-start.51) | collective-permute-done | bytes 1114144 | tf_op jit(solution)/shard_map/ppermute | solution.py:39
  514.9 14.6 %shard_map.309 = (bf16[512,2048]{1,0:T(8,128)(2,1)}, f32[512,1024]{1,0:T(8,128)}, f32[512,1024]{1,0:T(8,128)}, f32[2048,128]{1,0:T(8,128)}, f32[16,1024]{1,0:T(8,128)}, /*index=5*/f32[512,2048]{1,0:T(8,128)}) custom-call(s32[5]{0:T(128)} %stack.30.refs_0_.refs_1_, f32[128,2176]{1,0:T(8,128)} %copy-done.9, f32[128,2176]{1,0:T(8,128)} %collective-permute-done.50.refs_2_, ...), custom_call_target="tpu_custom_call" | custom-call | flops 2147483648 | bytes 27594752 | tf_op jit(solution)/shard_map/pallas_call | solution.py:100
  542.9 17.9 %shard_map.310 = (f32[512,1024]{1,0:T(8,128)}, f32[512,256]{1,0:T(8,128)}, f32[64,256]{1,0:T(8,128)}, f32[32,128]{1,0:T(8,128)}) custom-call(s32[2,4]{1,0:T(2,128)} %reduce_window_sum.11.refs_0_, s32[5]{0:T(128)} %stack.30.refs_0_.refs_1_, f32[512,1280]{1,0:T(8,128)} %get-tuple-element.135.refs_2_.refs_8_.refs_1_, ...), custom_call_target="tpu_custom_call" | custom-call | flops 209715200 | bytes 8998912 | tf_op jit(solution)/shard_map/pallas_call | solution.py:100
  575.6 36.0 %collective-permute-done.57 = f32[2048,128]{1,0:T(8,128)} collective-permute-done((f32[2048,128]{1,0:T(8,128)}, f32[2048,128]{1,0:T(8,128)}, u32[]{:S(2)}, u32[]{:S(2)}) %collective-permute-start.57) | collective-permute-done | bytes 1048608 | tf_op jit(solution)/shard_map/ppermute | solution.py:39
  613.8 9.1 shard_map.312
  640.2 20.9 %collective-permute-start.62 = (f32[512,1024]{1,0:T(8,128)}, f32[512,1024]{1,0:T(8,128)}, u32[]{:S(2)}, u32[]{:S(2)}) collective-permute-start(f32[512,1024]{1,0:T(8,128)} %get-tuple-element.221.refs_3_), channel_id=1, source_target_pairs={{0,4},{1,5},{2,6},{3,7},{4,0},{5,1},{6,2},{7,3},{8,12},{9,13},{10,... | collective-permute-start | bytes 6291464 | tf_op jit(solution)/shard_map/ppermute | solution.py:39
  661.2 13.2 %shard_map.313 = (f32[512,1152]{1,0:T(8,128)}, f32[16,1024]{1,0:T(8,128)}, f32[128,2048]{1,0:T(8,128)}, f32[128,2048]{1,0:T(8,128)}, f32[128,2048]{1,0:T(8,128)}, /*index=5*/f32[128,2048]{1,0:T(8,128)}) custom-call(s32[2,4]{1,0:T(2,128)} %reduce_window_sum.11.refs_0_, s32[5]{0:T(128)} %stack.30.refs_0_.refs_1_, f32[512,1024]{1,0:T(8,128)} %get-tuple-element.215.refs_2_, ...), custom_call_target="tpu_custom_call" | custom-call | flops 2147483648 | bytes 19718144 | tf_op jit(solution)/shard_map/pallas_call | solution.py:100
  684.5 21.4 %collective-permute-done.67.refs_6_ = f32[16,256]{1,0:T(8,128)S(1)} collective-permute-done((f32[16,256]{1,0:T(8,128)S(1)}, f32[16,256]{1,0:T(8,128)S(1)}, u32[]{:S(2)}, u32[]{:S(2)}) %collective-permute-start.67) | collective-permute-done | bytes 16416 | tf_op jit(solution)/shard_map/ppermute | solution.py:39
  722.5 11.7 %collective-permute-done.60 = f32[128,2048]{1,0:T(8,128)} collective-permute-done((f32[128,2048]{1,0:T(8,128)}, f32[128,2048]{1,0:T(8,128)}, u32[]{:S(2)}, u32[]{:S(2)}) %collective-permute-start.60) | collective-permute-done | bytes 1048608 | tf_op jit(solution)/shard_map/ppermute | solution.py:39
  741.3 8.3 shard_map.314
  759.2 16.1 %collective-permute-done.81.refs_2_ = f32[512,1024]{1,0:T(8,128)} collective-permute-done((f32[512,1024]{1,0:T(8,128)}, f32[512,1024]{1,0:T(8,128)}, u32[]{:S(2)}, u32[]{:S(2)}) %collective-permute-start.81) | collective-permute-done | bytes 2097184 | tf_op jit(solution)/shard_map/ppermute | solution.py:39
  777.9 31.0 %collective-permute-done.73 = f32[9520]{0:T(1024)S(1)} collective-permute-done((f32[9520]{0:T(1024)S(1)}, f32[9520]{0:T(1024)S(1)}, u32[]{:S(2)}, u32[]{:S(2)}) %collective-permute-start.73) | collective-permute-done | bytes 38112 | tf_op jit(solution)/shard_map/ppermute | solution.py:1313
  837.5 9.2 shard_map.317
  870.1 11.2 %collective-permute-done.69.refs_3_ = f32[128,2048]{1,0:T(8,128)} collective-permute-done((f32[128,2048]{1,0:T(8,128)S(1)}, f32[128,2048]{1,0:T(8,128)}, u32[]{:S(2)}, u32[]{:S(2)}) %collective-permute-start.69) | collective-permute-done | bytes 1048608 | tf_op jit(solution)/shard_map/ppermute | solution.py:39
  902.6 21.1 %collective-permute-done.80 = f32[512,1152]{1,0:T(8,128)} collective-permute-done((f32[512,1152]{1,0:T(8,128)}, f32[512,1152]{1,0:T(8,128)}, u32[]{:S(2)}, u32[]{:S(2)}) %collective-permute-start.80) | collective-permute-done | bytes 2359328 | tf_op jit(solution)/shard_map/ppermute | solution.py:39
  929.3 10.4 %all_gather.3 = f32[512,256]{0,1:T(8,128)S(1)} all-gather(f32[512,64]{0,1:T(8,128)S(1)} %copy.61), channel_id=1, replica_groups=mesh['section'=2,'tok'=4,'head'=4] {'head'}, dimensions={1}, use_global_device_ids=true | all-gather | bytes 655360 | tf_op jit(solution)/shard_map/all_gather | solution.py:1306
  (448 shorter events, 418.6 us)
Async XLA Ops:
  63.0 66.5 %collective-permute-start.10 = (f32[512,1024]{1,0:T(8,128)}, f32[512,1024]{1,0:T(8,128)}, u32[]{:S(2)}, u32[]{:S(2)}) collective-permute-start(f32[512,1024]{1,0:T(8,128)} %maximum_convert_fusion), channel_id=1, source_target_pairs={{16,20},{17,21},{18,22},{19,23},{20,16},{21,17},{22,18},{23,19},{2... | collective-permute-start | bytes 6291464 | tf_op jit(solution)/shard_map/ppermute | solution.py:39
  129.5 40.0 %collective-permute-start.12 = (f32[512,1024]{1,0:T(8,128)}, f32[512,1024]{1,0:T(8,128)}, u32[]{:S(2)}, u32[]{:S(2)}) collective-permute-start(f32[512,1024]{1,0:T(8,128)} %maximum_convert_fusion.1), channel_id=1, source_target_pairs={{0,4},{1,5},{2,6},{3,7},{4,0},{5,1},{6,2},{7,3},{8,12},{9,13},{10,... | collective-permute-start | bytes 6291464 | tf_op jit(solution)/shard_map/ppermute | solution.py:39
  295.8 195.6 %collective-permute-start.48 = (f32[512,1024]{1,0:T(8,128)}, f32[512,1024]{1,0:T(8,128)}, u32[]{:S(2)}, u32[]{:S(2)}) collective-permute-start(f32[512,1024]{1,0:T(8,128)} %get-tuple-element.197.refs_3_), channel_id=1, source_target_pairs={{16,20},{17,21},{18,22},{19,23},{20,16},{21,17},{22,18},{23,19},{2... | collective-permute-start | bytes 6291464 | tf_op jit(solution)/shard_map/ppermute | solution.py:39
  306.7 176.7 %collective-permute-start.47 = (f32[128,2048]{1,0:T(8,128)S(1)}, f32[128,2048]{1,0:T(8,128)S(1)}, u32[]{:S(2)}, u32[]{:S(2)}) collective-permute-start(f32[128,2048]{1,0:T(8,128)S(1)} %fusion.2), channel_id=1, source_target_pairs={{16,0},{17,1},{18,2},{19,3},{20,4},{21,5},{22,6},{23,7},{24,8},{25... | collective-permute-start | bytes 3145736 | tf_op jit(solution)/shard_map/ppermute | solution.py:1249
  308.0 191.5 %collective-permute-start.49 = (f32[1024,512]{1,0:T(8,128)}, f32[1024,512]{1,0:T(8,128)S(1)}, u32[]{:S(2)}, u32[]{:S(2)}) collective-permute-start(f32[1024,512]{1,0:T(8,128)} %get-tuple-element.199), channel_id=1, source_target_pairs={{16,24},{17,25},{18,26},{19,27},{20,28},{21,29},{22,30},{23,31},{2... | collective-permute-start | bytes 6291464 | tf_op jit(solution)/shard_map/ppermute | solution.py:39
  308.8 227.9 %collective-permute-start.54 = (f32[512,1152]{1,0:T(8,128)}, f32[512,1152]{1,0:T(8,128)}, u32[]{:S(2)}, u32[]{:S(2)}) collective-permute-start(f32[512,1152]{1,0:T(8,128)} %get-tuple-element.208.refs_3_), channel_id=1, source_target_pairs={{16,20},{17,21},{18,22},{19,23},{20,16},{21,17},{22,18},{23,19},{2... | collective-permute-start | bytes 7077896 | tf_op jit(solution)/shard_map/ppermute | solution.py:39
  499.5 63.4 %collective-permute-start.55 = (f32[512,1024]{1,0:T(8,128)}, f32[512,1024]{1,0:T(8,128)}, u32[]{:S(2)}, u32[]{:S(2)}) collective-permute-start(f32[512,1024]{1,0:T(8,128)} %get-tuple-element.210), channel_id=1, source_target_pairs={{16,24},{17,25},{18,26},{19,27},{20,28},{21,29},{22,30},{23,31},{2... | collective-permute-start | bytes 6291464 | tf_op jit(solution)/shard_map/ppermute | solution.py:39
  535.4 98.9 %collective-permute-start.34 = (f32[512,2048]{1,0:T(8,128)}, f32[512,2048]{1,0:T(8,128)}, u32[]{:S(2)}, u32[]{:S(2)}) collective-permute-start(f32[512,2048]{1,0:T(8,128)} %shard_map.301), channel_id=1, source_target_pairs={{16,0},{17,1},{18,2},{19,3},{20,4},{21,5},{22,6},{23,7},{24,8},{25... | collective-permute-start | bytes 12582920 | tf_op jit(solution)/shard_map/ppermute | solution.py:1242
  570.9 40.7 %collective-permute-start.57 = (f32[2048,128]{1,0:T(8,128)}, f32[2048,128]{1,0:T(8,128)}, u32[]{:S(2)}, u32[]{:S(2)}) collective-permute-start(f32[2048,128]{1,0:T(8,128)} %get-tuple-element.214), channel_id=1, source_target_pairs={{4,0},{5,1},{6,2},{7,3}} | collective-permute-start | bytes 3145736 | tf_op jit(solution)/shard_map/ppermute | solution.py:39
  622.9 54.2 %collective-permute-start.66 = (f32[512,256]{1,0:T(8,128)}, f32[512,256]{1,0:T(8,128)S(1)}, u32[]{:S(2)}, u32[]{:S(2)}) collective-permute-start(f32[512,256]{1,0:T(8,128)} %get-tuple-element.225.refs_2_), channel_id=1, source_target_pairs={{0,3},{1,2},{2,1},{3,0},{4,7},{5,6},{6,5},{7,4},{8,11},{9,10},{10,... | collective-permute-start | bytes 1572872 | tf_op jit(solution)/shard_map/ppermute | solution.py:39
  627.4 51.7 %collective-permute-start.65 = (f32[512,256]{1,0:T(8,128)}, f32[512,256]{1,0:T(8,128)}, u32[]{:S(2)}, u32[]{:S(2)}) collective-permute-start(f32[512,256]{1,0:T(8,128)} %get-tuple-element.225.refs_2_), channel_id=1, source_target_pairs={{0,2},{1,3},{2,0},{3,1},{4,6},{5,7},{6,4},{7,5},{8,10},{9,11},{10,... | collective-permute-start | bytes 1572872 | tf_op jit(solution)/shard_map/ppermute | solution.py:39
  629.8 52.6 %collective-permute-start.64 = (f32[512,256]{1,0:T(8,128)}, f32[512,256]{1,0:T(8,128)}, u32[]{:S(2)}, u32[]{:S(2)}) collective-permute-start(f32[512,256]{1,0:T(8,128)} %get-tuple-element.225.refs_2_), channel_id=1, source_target_pairs={{0,1},{1,0},{2,3},{3,2},{4,5},{5,4},{6,7},{7,6},{8,9},{9,8},{10,11... | collective-permute-start | bytes 1572872 | tf_op jit(solution)/shard_map/ppermute | solution.py:39
  640.2 96.8 %collective-permute-start.62 = (f32[512,1024]{1,0:T(8,128)}, f32[512,1024]{1,0:T(8,128)}, u32[]{:S(2)}, u32[]{:S(2)}) collective-permute-start(f32[512,1024]{1,0:T(8,128)} %get-tuple-element.221.refs_3_), channel_id=1, source_target_pairs={{0,4},{1,5},{2,6},{3,7},{4,0},{5,1},{6,2},{7,3},{8,12},{9,13},{10,... | collective-permute-start | bytes 6291464 | tf_op jit(solution)/shard_map/ppermute | solution.py:39
  674.4 38.8 %collective-permute-start.59 = (f32[128,2048]{1,0:T(8,128)}, f32[128,2048]{1,0:T(8,128)S(1)}, u32[]{:S(2)}, u32[]{:S(2)}) collective-permute-start(f32[128,2048]{1,0:T(8,128)} %get-tuple-element.218), channel_id=1, source_target_pairs={{0,1},{1,0},{2,3},{3,2},{4,5},{5,4},{6,7},{7,6},{8,9},{9,8},{10,11... | collective-permute-start | bytes 3145736 | tf_op jit(solution)/shard_map/ppermute | solution.py:39
  677.0 76.3 %collective-permute-start.63 = (f32[512,1152]{1,0:T(8,128)}, f32[512,1152]{1,0:T(8,128)}, u32[]{:S(2)}, u32[]{:S(2)}) collective-permute-start(f32[512,1152]{1,0:T(8,128)} %get-tuple-element.223), channel_id=1, source_target_pairs={{16,24},{17,25},{18,26},{19,27},{20,28},{21,29},{22,30},{23,31},{2... | collective-permute-start | bytes 7077896 | tf_op jit(solution)/shard_map/ppermute | solution.py:39
  679.1 167.6 %collective-permute-start.71 = (f32[512,2048]{1,0:T(8,128)}, f32[512,2048]{1,0:T(8,128)}, u32[]{:S(2)}, u32[]{:S(2)}) collective-permute-start(f32[512,2048]{1,0:T(8,128)} %get-tuple-element.228), channel_id=1, source_target_pairs={{0,16},{1,17},{2,18},{3,19},{4,20},{5,21},{6,22},{7,23},{8,24},{9,... | collective-permute-start | bytes 12582920 | tf_op jit(solution)/shard_map/ppermute | solution.py:1276
  713.2 36.4 %collective-permute-start.61 = (f32[128,2048]{1,0:T(8,128)}, f32[128,2048]{1,0:T(8,128)}, u32[]{:S(2)}, u32[]{:S(2)}) collective-permute-start(f32[128,2048]{1,0:T(8,128)} %get-tuple-element.220), channel_id=1, source_target_pairs={{0,3},{1,2},{2,1},{3,0},{4,7},{5,6},{6,5},{7,4},{8,11},{9,10},{10,... | collective-permute-start | bytes 3145736 | tf_op jit(solution)/shard_map/ppermute | solution.py:39
  734.1 41.2 %collective-permute-start.81 = (f32[512,1024]{1,0:T(8,128)}, f32[512,1024]{1,0:T(8,128)}, u32[]{:S(2)}, u32[]{:S(2)}) collective-permute-start(f32[512,1024]{1,0:T(8,128)} %maximum_convert_fusion.3), channel_id=1, source_target_pairs={{0,4},{1,5},{2,6},{3,7},{4,0},{5,1},{6,2},{7,3},{8,12},{9,13},{10,... | collective-permute-start | bytes 6291464 | tf_op jit(solution)/shard_map/ppermute | solution.py:39
  737.0 98.6 %collective-permute-start.79 = (f32[512,1152]{1,0:T(8,128)}, f32[512,1152]{1,0:T(8,128)}, u32[]{:S(2)}, u32[]{:S(2)}) collective-permute-start(f32[512,1152]{1,0:T(8,128)} %get-tuple-element.241.refs_3_), channel_id=1, source_target_pairs={{0,4},{1,5},{2,6},{3,7},{4,0},{5,1},{6,2},{7,3},{8,12},{9,13},{10,... | collective-permute-start | bytes 7077896 | tf_op jit(solution)/shard_map/ppermute | solution.py:39
  749.6 80.3 %collective-permute-start.78 = (f32[512,1024]{1,0:T(8,128)}, f32[512,1024]{1,0:T(8,128)}, u32[]{:S(2)}, u32[]{:S(2)}) collective-permute-start(f32[512,1024]{1,0:T(8,128)} %get-tuple-element.239), channel_id=1, source_target_pairs={{0,8},{1,9},{2,10},{3,11},{4,12},{5,13},{6,14},{7,15},{8,0},{9,1},... | collective-permute-start | bytes 6291464 | tf_op jit(solution)/shard_map/ppermute | solution.py:39
  755.1 53.8 %collective-permute-start.73 = (f32[9520]{0:T(1024)S(1)}, f32[9520]{0:T(1024)S(1)}, u32[]{:S(2)}, u32[]{:S(2)}) collective-permute-start(f32[9520]{0:T(1024)S(1)} %pad_maximum_fusion.1), channel_id=1, source_target_pairs={{0,8},{4,12},{8,0},{12,4},{1,9},{5,13},{9,1},{13,5},{2,10},{6,14},... | collective-permute-start | bytes 114248 | tf_op jit(solution)/shard_map/ppermute | solution.py:1313
  775.3 46.3 %collective-permute-start.74 = (f32[9520]{0:T(1024)S(1)}, f32[9520]{0:T(1024)S(1)}, u32[]{:S(2)}, u32[]{:S(2)}) collective-permute-start(f32[9520]{0:T(1024)S(1)} %pad_maximum_fusion.1), channel_id=1, source_target_pairs={{0,12},{4,8},{8,4},{12,0},{1,13},{5,9},{9,5},{13,1},{2,14},{6,10},... | collective-permute-start | bytes 114248 | tf_op jit(solution)/shard_map/ppermute | solution.py:1313
  821.6 76.9 %collective-permute-start.82 = (f32[1024,512]{1,0:T(8,128)}, f32[1024,512]{1,0:T(8,128)}, u32[]{:S(2)}, u32[]{:S(2)}) collective-permute-start(f32[1024,512]{1,0:T(8,128)} %get-tuple-element.247), channel_id=1, source_target_pairs={{0,8},{1,9},{2,10},{3,11},{4,12},{5,13},{6,14},{7,15},{8,0},{9,1},... | collective-permute-start | bytes 6291464 | tf_op jit(solution)/shard_map/ppermute | solution.py:39
  846.7 77.0 %collective-permute-start.80 = (f32[512,1152]{1,0:T(8,128)}, f32[512,1152]{1,0:T(8,128)}, u32[]{:S(2)}, u32[]{:S(2)}) collective-permute-start(f32[512,1152]{1,0:T(8,128)} %get-tuple-element.243), channel_id=1, source_target_pairs={{0,8},{1,9},{2,10},{3,11},{4,12},{5,13},{6,14},{7,15},{8,0},{9,1},... | collective-permute-start | bytes 7077896 | tf_op jit(solution)/shard_map/ppermute | solution.py:39
  (130 other events, 1776.8 us)

commit v2 on v1

--- a/solution.py
+++ b/solution.py
@@ -87,13 +87,14 @@
     return jnp.where(points >= 0, inside, -1)
 
 
-def call(body, grid, scalars, ins, in_specs, outs, out_specs, scratch=(), flops=0, name=None):
+def call(body, grid, scalars, ins, in_specs, outs, out_specs, scratch=(), flops=0, marks=()):
     flag = len(scalars) - 1
+    read = len(scalars) + len(ins)
 
     def guarded(*refs):
         @pl.when(refs[flag][4] == 1)
         def _():
-            body(*refs)
+            body(*refs[:read], *refs[read + len(marks) :])
 
     moved = sum(a.size * a.dtype.itemsize for a in ins)
     moved += sum(o.size * o.dtype.itemsize for o in outs)
@@ -102,15 +103,14 @@
         grid_spec=pltpu.PrefetchScalarGridSpec(
             num_scalar_prefetch=len(scalars),
             grid=grid,
-            in_specs=in_specs,
+            in_specs=in_specs + [whole(mark.shape) for mark in marks],
             out_specs=out_specs,
             scratch_shapes=list(scratch),
         ),
         out_shape=outs,
         compiler_params=pltpu.CompilerParams(vmem_limit_bytes=VMEM_BYTES),
         cost_estimate=pl.CostEstimate(flops=flops, bytes_accessed=moved, transcendentals=0),
-        name=name,
-    )(*scalars, *ins)
+    )(*scalars, *ins, *marks)
 
 
 def rows(count, width):
@@ -363,11 +363,13 @@
     )[0]
 
 
-def mix_body(idx, local, select, table, entering, gate, scan, gated, sums):
+def mix_body(idx, local, select, table, entering, gate, *refs):
+    grads, (scan, gated, sums) = (refs[:-3], refs[-3:])
     row_count, width = local.shape
     c_act = split(act_of(select[:, NST:]))
     lane = lax.broadcasted_iota(jnp.int32, (row_count, 128), 1)
     squares = jnp.zeros((row_count, 128), F32)
+    inner = jnp.zeros((row_count, 128), F32)
     for pair in range(width // 128):
         span = slice(128 * pair, 128 * pair + 128)
         carried = fine(nt, c_act, split(entering[span, :]))
@@ -376,10 +378,14 @@
         result = value * act_of(gate[:, span])
         gated[:, span] = result
         squares = squares + result * result
-    sums[...] = nt(jnp.ones((8, 128), F32), squares, EXACT)
-
-
-def gate_mix(idx, local, conv, table, entering, gate, micro_count, row_count):
+        if grads:
+            inner = inner + result * (grads[0][:, span] * grads[1][:, span])
+    ones = jnp.ones((4, 128), F32)
+    sums[0:4, :] = nt(ones, squares, EXACT)
+    sums[4:8, :] = nt(ones, inner, EXACT)
+
+
+def gate_mix(idx, local, conv, table, entering, gate, grads, micro_count, row_count):
     width = local.shape[1]
     total = micro_count * row_count
     select_block = pl.BlockSpec((row_count, 2 * NST), lambda m, *_: (m, width // (2 * NST)))
@@ -387,29 +393,52 @@
         mix_body,
         (micro_count,),
         (idx,),
-        [local, conv, table, entering, gate],
+        [local, conv, table, entering, gate, *grads],
         [
             rows(row_count, width),
             select_block,
             rows(row_count, 128),
             rows(width, NST),
             rows(row_count, width),
-        ],
+        ]
+        + ([rows(row_count, width), whole((1, width))] if grads else []),
         [struct((total, width)), struct((total, width)), struct((micro_count * 8, row_count))],
         [rows(row_count, width), rows(row_count, width), rows(8, row_count)],
         flops=6 * total * width * NST,
     )
 
 
-def out_body(idx, gated, s0, s1, s2, s3, gain, w_out, scaled, inverse, *refs):
+def back_body(idx, grad, w_out, out):
+    out[...] = nt(grad[...], w_out[...])
+
+
+def back_project(idx, grad, w_out, micro_count, row_count):
+    total, width = (grad.shape[0], w_out.shape[0])
+    tile = width // 4
+    return call(
+        back_body,
+        (4,),
+        (idx,),
+        [grad, w_out],
+        [whole((total, D)), pl.BlockSpec((tile, D), lambda j, *_: (j, 0))],
+        [struct((total, width))],
+        [pl.BlockSpec((total, tile), lambda j, *_: (0, j))],
+        flops=2 * total * width * D,
+    )[0]
+
+
+def norms_of(sums):
+    total = ((sums[0][...] + sums[1][...]) + (sums[2][...] + sums[3][...])) / (H * P_SIZE)
+    total = total.T
+    inv = lax.rsqrt(total[:, 0:1] + EPSILON)
+    return (inv, total[:, 4:5] * inv)
+
+
+def out_body(idx, gated, s0, s1, s2, s3, gain, w_out, scaled, *refs):
     chunks, (low, product) = (refs[:4], refs[4:])
     row_count, width = gated.shape
     chunk = row_count // 4
-    squares = (s0[...] + s1[...]) + (s2[...] + s3[...])
-    inverse[...] = jnp.broadcast_to(
-        lax.rsqrt(squares / (H * P_SIZE) + EPSILON).T[:, 0:1], (row_count, 128)
-    )
-    inv = inverse[:, 0:1]
+    inv, _ = norms_of((s0, s1, s2, s3))
     for left in range(0, width, 128):
         span = slice(left, left + 128)
         rounded = (gated[:, span] * inv * gain[:, span]).astype(BF16)
@@ -422,7 +451,7 @@
         chunks[piece][...] = product[pl.ds(place, chunk), :]
 
 
-def out_project(idx, gated, sums, weights, micro_count, row_count):
+def out_project(idx, gated, sums, weights, micro_count, row_count, marks=()):
     width = gated.shape[1]
     total = micro_count * row_count
     chunk = row_count // 4
@@ -432,51 +461,51 @@
         (idx,),
         [gated, *sums, weights.gate_gain, weights.out],
         [rows(row_count, width)] + [rows(8, row_count)] * 4 + [whole((1, width)), whole((width, D))],
-        [struct((total, width)), struct((total, 128))] + [struct((micro_count * chunk, D))] * 4,
-        [rows(row_count, width), rows(row_count, 128)] + [rows(chunk, D)] * 4,
+        [struct((total, width))] + [struct((micro_count * chunk, D))] * 4,
+        [rows(row_count, width)] + [rows(chunk, D)] * 4,
         [pltpu.VMEM((row_count, width), BF16), pltpu.VMEM((row_count, D), F32)],
         flops=2 * total * width * D,
+        marks=marks,
     )
 
 
 def gated_body(idx, *refs, from_parts):
+    sums, (gate, scan, select, table, gain), refs = (refs[:4], refs[4:9], refs[9:])
     if from_parts:
-        parts, refs = (refs[:4], refs[4:])
+        parts, w_out, refs = (refs[:4], refs[4], refs[5:])
     else:
-        grad, parts, refs = (refs[0], refs[1:5], refs[5:])
-    gate, scan, inverse, select, table, gain, w_out = refs[:7]
-    low_grad, grad_gate, grad_scan, state, gain_grad = refs[7:12]
-    refs = refs[12:]
+        grads, refs = (refs[0], refs[1:])
+    grad_gate, grad_scan, state, gain_grad = refs[:4]
     if from_parts:
-        full, refs = (refs[0], refs[1:])
-    norms, carried, carried_low = refs
+        low_grad, full, norms = refs[4:7]
+    else:
+        scaled = refs[4]
+    carried, carried_low = refs[-2:]
     row_count, width = gate.shape
     chunk = row_count // 4
-    for piece in range(4):
-        place = pl.ds(pl.multiple_of((idx[1] ^ piece) * chunk, chunk), chunk)
-        if from_parts:
+    inv, inner = norms_of(sums)
+    if from_parts:
+        for piece in range(4):
+            place = pl.ds(pl.multiple_of((idx[1] ^ piece) * chunk, chunk), chunk)
             values = parts[piece][:, 0:D]
             full[place, :] = values
             low_grad[place, :] = values.astype(BF16)
             norms[place, :] = parts[piece][:, D:]
-        else:
-            norms[place, :] = parts[piece][...]
-    if not from_parts:
-        low_grad[...] = grad[...]
-    inv = inverse[:, 0:1]
-    inner = norms[:, 0:1]
+        inner = norms[:, 0:1]
     c_act = split(act_of(select[:, NST:]))
     lane = lax.broadcasted_iota(jnp.int32, (row_count, 128), 1)
     gain_grad[...] = jnp.zeros_like(gain_grad)
     for pair in range(width // 128):
         span = slice(128 * pair, 128 * pair + 128)
-        grad_scaled = nt(low_grad[...], w_out[span, :])
+        grad_scaled = nt(low_grad[...], w_out[span, :]) if from_parts else grads[:, span]
         gate_pre = gate[:, span]
         sig = sigmoid(gate_pre)
         act = gate_pre * sig
         out = scan[:, span]
         normal = out * act * inv
         gain_grad[0:1, span] = jnp.sum(grad_scaled * normal, axis=0, keepdims=True)
+        if not from_parts:
+            scaled[:, span] = (normal * gain[:, span]).astype(BF16).astype(F32)
         grad_gated = inv * (grad_scaled * gain[:, span]) - normal * (inv * inner)
         grad_out = grad_gated * act
         grad_scan[:, span] = grad_out
@@ -489,45 +518,39 @@
     state[...] = fine(tn, (carried[...], carried_low[...]), c_act)
 
 
-def gated_back(idx, grad, parts, gate, scan, inverse, conv, table, weights, micro_count, row_count):
+def gated_back(idx, grads, parts, sums, gate, scan, conv, table, weights, micro_count, row_count):
     width = gate.shape[1]
     total = micro_count * row_count
     chunk = row_count // 4
-    from_parts = grad is None
+    from_parts = grads is None
     select_block = pl.BlockSpec((row_count, 2 * NST), lambda m, *_: (m, width // (2 * NST)))
-    ins = ([] if from_parts else [grad]) + [
-        *parts, gate, scan, inverse, conv, table, weights.gate_gain, weights.out
+    ins = [*sums, gate, scan, conv, table, weights.gate_gain]
+    in_specs = [rows(8, row_count)] * 4 + [
+        rows(row_count, width),
+        rows(row_count, width),
+        select_block,
+        rows(row_count, 128),
+        whole((1, width)),
     ]
-    in_specs = (
-        ([] if from_parts else [rows(row_count, D)])
-        + [rows(chunk, part.shape[1]) for part in parts]
-        + [
-            rows(row_count, width),
-            rows(row_count, width),
-            rows(row_count, 128),
-            select_block,
-            rows(row_count, 128),
-            whole((1, width)),
-            whole((width, D)),
-        ]
-    )
     outs = [
-        struct((total, D), BF16),
         struct((total, width)),
         struct((total, width)),
         struct((micro_count * width, NST)),
         struct((micro_count * 8, width)),
     ]
-    out_specs = [
-        rows(row_count, D),
-        rows(row_count, width),
-        rows(row_count, width),
-        rows(width, NST),
-        rows(8, width),
-    ]
+    out_specs = [rows(row_count, width), rows(row_count, width), rows(width, NST), rows(8, width)]
+    scratch = [pltpu.VMEM((row_count, width), BF16), pltpu.VMEM((row_count, width), BF16)]
     if from_parts:
-        outs.append(struct((total, D)))
-        out_specs.append(rows(row_count, D))
+        ins += [*parts, weights.out]
+        in_specs += [rows(chunk, D + PAD)] * 4 + [whole((width, D))]
+        outs += [struct((total, D), BF16), struct((total, D))]
+        out_specs += [rows(row_count, D), rows(row_count, D)]
+        scratch = [pltpu.VMEM((row_count, PAD), F32)] + scratch
+    else:
+        ins.append(grads)
+        in_specs.append(rows(row_count, width))
+        outs.append(struct((total, width)))
+        out_specs.append(rows(row_count, width))
     return call(
         partial(gated_body, from_parts=from_parts),
         (micro_count,),
@@ -536,12 +559,8 @@
         in_specs,
         outs,
         out_specs,
-        [
-            pltpu.VMEM((row_count, PAD), F32),
-            pltpu.VMEM((row_count, width), BF16),
-            pltpu.VMEM((row_count, width), BF16),
-        ],
-        flops=2 * total * width * D,
+        scratch,
+        flops=2 * total * width * (D if from_parts else NST),
     )
 
 
@@ -812,7 +831,7 @@
             whole((D, width)),
             whole((D, heads)),
         ],
-        [struct((total, width + 128)), struct((micro_count * 8, width))] + [struct((micro_count * chunk, D))] * 4,
+        [struct((total, width)), struct((micro_count * 8, width))] + [struct((micro_count * chunk, D))] * 4,
         [rows(row_count, width), rows(8, width)] + [rows(chunk, D)] * 4,
         [
             pltpu.VMEM((row_count + 8, width), F32),
@@ -825,10 +844,9 @@
 
 
 def select_back_body(
-    ends, idx, s0, s1, s2, s3, halo, select, halo_in, taps, grad_step, kept,
+    ends, idx, s0, s1, s2, s3, halo, select, halo_in, taps, grad_step,
     low_select, tap_grads, rest, grads, extended,
 ):
-    del kept
     row_count, columns = select.shape
     before, after = near_masks(ends, idx, row_count)
     grads[0:row_count, :] = (s0[...] + s1[...]) + (s2[...] + s3[...])
@@ -849,51 +867,27 @@
             rest[:, 0:part] = low_select[:, head * part : (head + 1) * part]
 
 
-def select_back(ends, idx, selects, halo, select, halo_in, grad_step, kept, params, micro_count, row_count):
+def select_back(ends, idx, selects, halo, select, halo_in, grad_step, params, micro_count, row_count):
     total, columns = select.shape
-    width = kept.shape[1] - 128
-    right = width // columns
-    ins = [*selects, halo, select, halo_in, params.taps, grad_step, kept]
-    outs = [
-        struct((total, columns)),
-        struct((micro_count * 8, columns)),
-        struct((total, width + 128)),
-    ]
-
-    def guarded(*refs):
-        @pl.when(refs[1][4] == 1)
-        def _():
-            select_back_body(*refs)
-
-    return pl.pallas_call(
-        guarded,
-        grid_spec=pltpu.PrefetchScalarGridSpec(
-            num_scalar_prefetch=2,
-            grid=(micro_count,),
-            in_specs=[rows(row_count, columns)] * 4
-            + [
-                rows(8, columns),
-                rows(row_count, columns),
-                pl.BlockSpec((8, columns), lambda m, *_: (m, right)),
-                pl.BlockSpec((8, columns), lambda m, *_: (0, right)),
-                rows(row_count, 128),
-                pl.BlockSpec(memory_space=pl.ANY),
-            ],
-            out_specs=[
-                rows(row_count, columns),
-                rows(8, columns),
-                pl.BlockSpec((row_count, 128), lambda m, *_: (m, width // 128)),
-            ],
-            scratch_shapes=[
-                pltpu.VMEM((row_count + 8, columns), F32),
-                pltpu.VMEM((row_count + 8, columns), F32),
-            ],
-        ),
-        out_shape=outs,
-        input_output_aliases={11: 2},
-        compiler_params=pltpu.CompilerParams(vmem_limit_bytes=VMEM_BYTES),
-        cost_estimate=pl.CostEstimate(flops=30 * total * columns, bytes_accessed=9 * total * columns * 4, transcendentals=0),
-    )(ends, idx, *ins)
+    right = halo_in.shape[1] // columns - 1
+    return call(
+        select_back_body,
+        (micro_count,),
+        (ends, idx),
+        [*selects, halo, select, halo_in, params.taps, grad_step],
+        [rows(row_count, columns)] * 4
+        + [
+            rows(8, columns),
+            rows(row_count, columns),
+            pl.BlockSpec((8, columns), lambda m, *_: (m, right)),
+            pl.BlockSpec((8, columns), lambda m, *_: (0, right)),
+            rows(row_count, 128),
+        ],
+        [struct((total, columns)), struct((micro_count * 8, columns)), struct((total, 128))],
+        [rows(row_count, columns), rows(8, columns), rows(row_count, 128)],
+        [pltpu.VMEM((row_count + 8, columns), F32), pltpu.VMEM((row_count + 8, columns), F32)],
+        flops=30 * total * columns,
+    )
 
 
 def weight_body(idx, split, split_other, kept, kept_other, far, own, *, flip):
@@ -913,7 +907,7 @@
         own[...] = result
 
 
-def weight_grad(idx, split, split_other, kept, kept_other, flip):
+def weight_grad(idx, split, split_other, kept, kept_other, flip, marks=()):
     total, width = kept.shape
     block = split.shape[1] // 4
     shape = (width, block) if flip else (block, width)
@@ -931,6 +925,7 @@
         [struct(shape), struct(shape)],
         [whole(shape), whole(shape)],
         flops=8 * total * block * width,
+        marks=marks,
     )
 
 
@@ -1043,7 +1038,7 @@
     def wave(layer, local, table, backward, ahead):
         decay = table.reshape(micros, row_count, 128)[:, row_count - 1, DECIN : DECIN + heads]
         shape = (micros, heads, P_SIZE, NST)
-        entering = None
+        entering, hops = (None, [])
         for hop in range(tok_count - 1):
             leaving = local
             if entering is not None:
@@ -1058,11 +1053,11 @@
 
             if hop in ahead:
                 leaving = after(leaving, *ahead[hop])
-            received = send(leaving, layer, move)
-            entering = received if entering is None else entering + received
-        return entering
-
-    def forward(layer, parts, chunk_in):
+            hops.append(send(leaving, layer, move))
+            entering = hops[-1] if entering is None else entering + hops[-1]
+        return (entering, hops)
+
+    def scan_forward(layer, parts, grads):
         idx = scalars(0, section == layer)
         normed, value, select, step = in_project(idx, parts, weights, micros, row_count)
         edge = jnp.concatenate(
@@ -1078,23 +1073,19 @@
         )
         gate = gate_project(idx, after(normed, state), weights.gate)
         local = scan_local(ends, idx, conv, table, table_t, params, micros, row_count)
-        entering = wave(layer, state, table, False, {1: (gate, local)})
-        scan, gated, sums = gate_mix(idx, local, conv, table, entering, gate, micros, row_count)
-        scaled, inverse, *pieces = out_project(
-            idx, gated, gather(sums, layer), weights, micros, row_count
-        )
-        branch = reduce_chunks(pieces, layer)
-        saved = SimpleNamespace(
-            normed=normed, gate=gate, value=value, select=select, halo=halo, conv=conv,
-            table=table, table_t=table_t, entering=entering, scan=scan, inverse=inverse,
-            scaled=scaled, branch=branch, chunk_in=chunk_in,
-        )
-        return (chunk_in + branch, saved)
-
-    def norm_lanes(grad_chunk, branch):
-        low = lax.reduce_precision(grad_chunk, 8, 7)
-        inner = jnp.sum(low * branch, axis=-1, keepdims=True) / (H * P_SIZE)
-        return jnp.broadcast_to(inner, (micros * chunk, PAD))
+        entering, _ = wave(layer, state, table, False, {1: (gate, local)})
+        scan, gated, sums = gate_mix(
+            idx, local, conv, table, entering, gate, grads, micros, row_count
+        )
+        return SimpleNamespace(
+            normed=normed, gate=gate, value=value, select=select, halo=halo, conv=conv, table=table,
+            table_t=table_t, entering=entering, scan=scan, gated=gated, sums=gather(sums, layer),
+        )
+
+    def project_out(layer, saved, marks=()):
+        idx = scalars(0, section == layer)
+        scaled, *pieces = out_project(idx, saved.gated, saved.sums, weights, micros, row_count, marks)
+        return (scaled, reduce_chunks(pieces, layer))
 
     def exchange(layer, values):
         return send(values, layer, lambda t, h: (t ^ 1, h))
@@ -1109,12 +1100,18 @@
             axis=1,
         ).astype(F32)
 
-    def backward(layer, saved, grad, norm_parts, grad_chunk, pairs, shown, ahead, waits):
+    def pair_product(layer, split, split_other, kept, other, flip=False, hold=(), marks=()):
         idx = scalars(0, section == layer)
-        low_grad, grad_gate, grad_scan, state, gain_grad, *full = gated_back(
-            idx, grad, norm_parts, saved.gate, saved.scan, saved.inverse, saved.conv, saved.table,
-            weights, micros, row_count,
-        )
+        far, own = weight_grad(idx, split, split_other, kept, other, flip, marks)
+        return (own, send(after(far, *hold), layer, lambda t, h: (t ^ 2, h)))
+
+    def backward(layer, saved, grads, parts, plan):
+        idx = scalars(0, section == layer)
+        grad_gate, grad_scan, state, gain_grad, *given = gated_back(
+            idx, grads, parts, saved.sums, saved.gate, saved.scan, saved.conv, saved.table, weights,
+            micros, row_count,
+        )
+        state = after(state, *plan.before_wave)
         grad_x, grad_bc, grad_rows, skip_grad = scan_back(
             ends, idx, saved.conv, saved.table, saved.table_t, grad_scan, saved.entering, params,
             micros, row_count,
@@ -1125,15 +1122,11 @@
             (((1,), (1,)), ((), ())),
             preferred_element_type=F32,
         )
-        pieces = shown(state)
-        later = wave(
-            layer,
-            state,
-            saved.table,
-            True,
-            {1: (grad_bc, *ahead[0], *pieces[1:2]), 2: (gate_part, *ahead[1], *pieces[2:3])},
-        )
-        later = after(later, *pieces[3:], *waits[0])
+        one, two = plan.in_wave(grad_gate, gate_part, given)
+        later, hops = wave(
+            layer, state, saved.table, True, {1: (grad_bc, *one), 2: (gate_part, *two)}
+        )
+        later = after(later, *plan.after_wave(grad_gate, hops))
         grad_value, grad_select, grad_step, small = scan_finish(
             idx, saved.conv, saved.table, saved.table_t, grad_x, grad_bc, grad_rows, later,
             saved.entering, params, micros, row_count,
@@ -1141,20 +1134,21 @@
         first_value = grad_value.reshape(micros, row_count, width)[:, :8].reshape(micros * 8, width)
         halo_value = to_tok(first_value, layer, -1)
         selects = gather(grad_select, layer)
+        first_select = grad_select.reshape(micros, row_count, 2 * NST)[:, :8].reshape(micros * 8, 2 * NST)
+        halos = [
+            send(first_select, layer, lambda t, h, step=step: (t - 1, h ^ step)) for step in range(4)
+        ]
+        waits = (*halos, *plan.before_conv(grad_step, (halo_value, *halos)))
         low_value, value_taps, *pieces = conv_back(
-            ends, idx, grad_value, halo_value, saved.value, saved.halo, gate_part, grad_step, params,
-            weights, micros, row_count,
-        )
-        kept = SimpleNamespace(scaled=saved.scaled, gate=grad_gate, low_grad=low_grad)
-        products, first_needed = pairs(kept, halo_value)
-        grad_normed = after(reduce_chunks(pieces, layer), *first_needed, *waits[1])
-        first_select = sum(
-            part.reshape(micros, row_count, 2 * NST)[:, :8].reshape(micros * 8, 2 * NST) for part in selects
-        )
-        halo_select = to_tok(first_select, layer, -1)
-        low_select, select_taps, low_rest = select_back(
-            ends, idx, selects, halo_select, saved.select, saved.halo, grad_step, low_value, params,
-            micros, row_count,
+            ends, idx, after(grad_value, *waits), halo_value, saved.value, saved.halo, gate_part, grad_step,
+            params, weights, micros, row_count,
+        )
+        grad_sum = reduce_chunks(pieces, layer)
+        selects = [selects[0]] + [after(part, grad_sum) for part in selects[1:]]
+        halo_select = sum(halos)
+        grad_normed = after(grad_sum, *plan.beside_sum(pieces[0], low_value))
+        low_select, select_taps, rest = select_back(
+            ends, idx, selects, halo_select, saved.select, saved.halo, grad_step, params, micros, row_count
         )
         grad_normed = grad_normed + lax.dot_general(
             chunk_of(low_select).astype(BF16),
@@ -1167,11 +1161,10 @@
         norm_grad = jnp.sum(grad_normed * hidden * inv, axis=0)
         weighted = grad_normed * weights.gain
         grad_hidden = (
-            grad_chunk
+            saved.grad_chunk
             + inv * weighted
             - hidden * (inv * inv * inv) * jnp.mean(weighted * hidden, axis=-1, keepdims=True)
         )
-        kept.value = low_rest
         sums = (
             norm_grad,
             jnp.concatenate(
@@ -1184,110 +1177,199 @@
                 ]
             ),
         )
-        return (grad_hidden, kept, sums, full, products)
-
-    def pair_product(layer, split, split_other, kept, flip, other):
-        idx = scalars(0, section == layer)
-        far, own = weight_grad(idx, split, split_other, kept, other, flip)
-        return (own, send(far, layer, lambda t, h: (t ^ 2, h)))
+        return (grad_hidden, SimpleNamespace(gate=grad_gate, value=low_value, rest=rest), sums)
 
     first = section == 0
     pairwise = tok_count == 4
     grad_rows_1 = out_grad.reshape(total, D)
+    scaled_grads_1 = back_project(scalars(0, section == 1), grad_rows_1, weights.out, micros, row_count)
 
     input_rows = block_input.reshape(total, D)
-    chunk_0 = chunk_of(input_rows).astype(F32)
-    out_0, saved_0 = forward(0, [input_rows], chunk_0)
-    moved = out_0
+    saved_0 = scan_forward(0, [input_rows], [])
+    saved_0.chunk_in = chunk_of(input_rows).astype(F32)
+    saved_0.scaled, saved_0.branch = project_out(0, saved_0)
+    out_0 = moved = saved_0.chunk_in + saved_0.branch
     if pairwise:
         grad_other_1 = exchange(1, split_blocks(grad_rows_1))
-        moved = after(out_0, grad_other_1)
+        moved = after(out_0, grad_other_1, scaled_grads_1)
 
     chunk_1 = lax.ppermute(moved, SECTION, [(0, 1)])
     parts_1 = gather(chunk_1, 1)
     if pairwise:
         other_0 = exchange(0, after(split_blocks(saved_0.normed), out_0))
         scaled_0 = exchange(0, after(saved_0.scaled, out_0))
-        parts_1[0] = after(parts_1[0], other_0)
-    out_1, saved_1 = forward(1, parts_1, chunk_1)
-
-    grad_chunk_1 = chunk_of(grad_rows_1).astype(F32)
-    lanes_1 = norm_lanes(grad_chunk_1, saved_1.branch)
-    all_lanes_1 = gather(lanes_1, 1)
+        parts_1[0] = after(parts_1[0], other_0, scaled_0)
+    saved_1 = scan_forward(1, parts_1, [scaled_grads_1, weights.gate_gain])
+    saved_1.chunk_in = chunk_1
+    saved_1.grad_chunk = chunk_of(grad_rows_1).astype(F32)
+
+    work = SimpleNamespace()
+    before_wave_1 = ()
     if pairwise:
         other_1 = exchange(1, after(split_blocks(saved_1.normed), saved_1.entering))
-        scaled_1 = exchange(1, saved_1.scaled)
-        all_lanes_1[0] = after(all_lanes_1[0], other_1, scaled_0)
-
-    def pairs_1(kept, done):
+        before_wave_1 = (other_1,)
+
+    def in_wave_1(grad_gate, gate_part, given):
+        saved_1.scaled = given[0]
+        work.kept_gate = grad_gate
+        return ((), ())
+
+    def after_wave_1(grad_gate, hops):
+        if pairwise:
+            work.gate_other = exchange(1, after(grad_gate, hops[0]))
+        return ()
+
+    def before_conv_1(done, halo):
         if not pairwise:
-            return ([], ())
-        products = [
-            pair_product(1, kept.low_grad, grad_other_1, kept.scaled, True, scaled_1),
-            pair_product(1, saved_1.normed, other_1, kept.gate, False, exchange(1, after(kept.gate, done))),
-        ]
-        return (products, (products[0][0],))
-
-    shown_1 = []
-
-    def show_1(state):
-        shown_1.extend(gather(after(out_1, state), 1))
-        return shown_1
-
-    grad_mid, kept_1, sums_1, _, big_1 = backward(
-        1, saved_1, grad_rows_1, all_lanes_1, grad_chunk_1, pairs_1, show_1, ((scaled_1,) if pairwise else (), ()), ((), ())
-    )
+            return ()
+        work.gate_1 = pair_product(
+            1, saved_1.normed, other_1, after(work.kept_gate, done), work.gate_other, hold=halo
+        )
+        return (work.gate_1[0],)
+
+    def beside_sum_1(piece, low_value):
+        if pairwise:
+            work.value_other = exchange(1, low_value)
+            return (work.gate_1[1], work.value_other)
+        return ()
+
+    grad_mid, kept_1, sums_1 = backward(
+        1, saved_1, scaled_grads_1, None,
+        SimpleNamespace(
+            before_wave=before_wave_1, in_wave=in_wave_1, after_wave=after_wave_1, before_conv=before_conv_1,
+            beside_sum=beside_sum_1,
+        ),
+    )
+
+    saved_0.grad_chunk = lax.ppermute(grad_mid, SECTION, [(1, 0)])
+    low_chunk = lax.reduce_precision(saved_0.grad_chunk, 8, 7)
+    inner = jnp.sum(low_chunk * saved_0.branch, axis=-1, keepdims=True) / (H * P_SIZE)
+    payload = jnp.concatenate(
+        [saved_0.grad_chunk, jnp.broadcast_to(inner, (micros * chunk, PAD))], axis=1
+    )
+    parts_0 = gather(payload, 0)
+    before_wave_0 = ()
+    if pairwise:
+        work.value_1 = pair_product(
+            1, saved_1.normed, other_1, kept_1.value, after(work.value_other, grad_mid)
+        )
+        parts_0[0] = after(parts_0[0], work.value_1[0])
+
+    def tell(values):
+        return lax.ppermute(values[:8, :128], SECTION, [(0, 1)])
+
+    def in_wave_0(grad_gate, gate_part, given):
+        work.low_grad_0, work.full_0 = given
+        work.kept_gate_0 = grad_gate
+        marks = (work.value_1[1][:8, :128],) if pairwise else ()
+        _, branch = project_out(1, saved_1, marks)
+        work.out_1 = chunk_1 + branch
+        work.shown_1 = gather(work.out_1, 1)
+        return ((), ())
+
+    def after_wave_0(grad_gate, hops):
+        if not pairwise:
+            return (work.out_1,)
+        work.gate_other_0 = exchange(0, after(grad_gate, hops[0]))
+        work.grad_other_0 = exchange(0, after(split_blocks(work.low_grad_0), hops[-1]))
+        return (work.out_1,)
+
+    def before_conv_0(done, halo):
+        if not pairwise:
+            return ()
+        work.gate_0 = pair_product(
+            0, saved_0.normed, other_0, after(work.kept_gate_0, done), work.gate_other_0, hold=halo
+        )
+        return (work.gate_0[0], *work.shown_1)
+
+    def beside_sum_0(piece, low_value):
+        if not pairwise:
+            return ()
+        work.value_other_0 = exchange(0, low_value)
+        work.scaled_0 = pair_product(
+            0, work.low_grad_0, work.grad_other_0, after(saved_0.scaled, piece), scaled_0, True
+        )
+        mark = tell(piece)
+        scaled_other = exchange(1, after(saved_1.scaled, mark))
+        work.scaled_1 = pair_product(
+            1, grad_rows_1, grad_other_1, saved_1.scaled, scaled_other, True, marks=(mark,)
+        )
+        return (work.scaled_0[0],)
+
+    grad_in, kept_0, sums_0 = backward(
+        0, saved_0, None, parts_0,
+        SimpleNamespace(
+            before_wave=before_wave_0, in_wave=in_wave_0, after_wave=after_wave_0, before_conv=before_conv_0,
+            beside_sum=beside_sum_0,
+        ),
+    )
+    shown_0 = gather(grad_in, 0)
+
+    def chosen(left, right):
+        return jnp.where(first, left, right)
+
+    rest_sum = chosen(
+        tn(saved_0.normed, kept_0.rest.astype(BF16)), tn(saved_1.normed, kept_1.rest.astype(BF16))
+    )
+    norm_sum, head_sum = (chosen(left, right) for left, right in zip(sums_0, sums_1, strict=True))
+    packed = jnp.concatenate([norm_sum, head_sum])
+    size = -(-packed.size // 1024) * 1024
+    packed = jnp.pad(packed, (0, size - packed.size)).reshape(-1, 128)
+    block = D // tok_count
+
+    def block_of(which):
+        return lax.dynamic_slice_in_dim(rest_sum, which * block, block, 0)
+
+    if pairwise:
+        total_sum = jnp.concatenate([block_of(tok), packed], axis=0)
+        for step in (1, 2, 3):
+            total_sum = total_sum + lax.ppermute(
+                jnp.concatenate([block_of(tok ^ step), packed], axis=0),
+                TOK,
+                [(source, source ^ step) for source in range(4)],
+            )
+        rest_sum, packed = (total_sum[:block], total_sum[block:])
+    else:
+        rest_sum = lax.psum_scatter(rest_sum, TOK, scatter_dimension=0, tiled=True)
+        packed = lax.psum(packed, TOK)
+    quarter = 2 * NST // 4
+    packed = packed.reshape(-1)
+    norm_sum, head_sum = (lax.dynamic_slice_in_dim(packed[:D], tok * block, block, 0), packed[D:])
+    lanes = jnp.concatenate(
+        [rest_sum[:, :quarter], jnp.broadcast_to(norm_sum[:, None], (block, 128 - quarter))], axis=1
+    )
+    norm_sum = norm_sum[:, None]
+    select_sum = jnp.zeros((block, 2 * NST), F32)
+    for step in range(4):
+        moved = lanes
+        if step > 0:
+            moved = lax.ppermute(lanes, HEAD, [(source, source ^ step) for source in range(4)])
+            norm_sum = norm_sum + moved[:, quarter : quarter + 1]
+        select_sum = lax.dynamic_update_slice_in_dim(
+            select_sum, moved[:, :quarter], (head ^ step) * quarter, 1
+        )
+    norm_sum = norm_sum[:, 0]
+
+    if pairwise:
+        work.value_0 = pair_product(
+            0, saved_0.normed, other_0, after(kept_0.value, grad_in, work.scaled_0[1]), work.value_other_0
+        )
+        parts_1[0] = after(parts_1[0], work.value_0[0])
+        work.full_0 = after(work.full_0, work.value_0[0])
     full_1 = join(scalars(0, section == 1), parts_1, None, micros, row_count)
     layer_out = join(
-        scalars(first, 1), shown_1, lax.ppermute(full_1, SECTION, [(1, 0)]), micros, row_count
-    )
+        scalars(first, 1), work.shown_1, lax.ppermute(full_1, SECTION, [(1, 0)]), micros, row_count
+    )
+    full_0 = lax.ppermute(work.full_0, SECTION, [(0, 1)])
+    input_grad = join(scalars(section == 1, 1), shown_0, full_0, micros, row_count)
     if pairwise:
-        big_1.append(
-            pair_product(1, saved_1.normed, other_1, kept_1.value, False, exchange(1, kept_1.value))
-        )
-
-    grad_chunk_0 = lax.ppermute(grad_mid, SECTION, [(1, 0)])
-    lanes_0 = norm_lanes(grad_chunk_0, saved_0.branch)
-    payload = jnp.concatenate([grad_chunk_0, lanes_0], axis=1)
-
-    def pairs_0(kept, done):
-        if not pairwise:
-            return ([], ())
-        grad_other_0 = exchange(0, after(split_blocks(kept.low_grad), done))
-        products = [
-            pair_product(0, saved_0.normed, other_0, kept.gate, False, exchange(0, after(kept.gate, done))),
-            pair_product(0, kept.low_grad, grad_other_0, kept.scaled, True, scaled_0),
-        ]
-        return (products, (products[0][0],))
-
-    parts_0 = gather(payload, 0)
-    ahead, waits = (((), ()), ((), ()))
-    if pairwise:
-        (_, scaled_far), (gate_own, gate_far), (value_own, value_far) = big_1
-        parts_0[0] = after(parts_0[0], gate_own, scaled_far)
-        ahead = ((value_own, gate_far), ())
-        waits = ((), (value_far,))
-    grad_in, kept_0, sums_0, (full_0,), big_0 = backward(
-        0, saved_0, None, parts_0, grad_chunk_0, pairs_0, lambda state: [], ahead, waits
-    )
-    input_grad = join(
-        scalars(section == 1, 1),
-        gather(grad_in, 0),
-        lax.ppermute(full_0, SECTION, [(0, 1)]),
-        micros,
-        row_count,
-    )
-
-    def chosen(left, right):
-        return jnp.where(first, left, right)
-
-    if pairwise:
-        last = after(saved_0.normed, big_0[0][1])
-        big_0.append(pair_product(0, last, other_0, kept_0.value, False, exchange(0, kept_0.value)))
-        big_0[0], big_0[1] = (big_0[1], big_0[0])
         scaled_sum, gate_sum, value_sum = (
-            chosen(own_0 + far_0, own_1 + far_1)
-            for (own_0, far_0), (own_1, far_1) in zip(big_0, big_1, strict=True)
+            chosen(left[0] + after(left[1], *waits), right[0] + right[1])
+            for left, right, waits in (
+                (work.scaled_0, work.scaled_1, ()),
+                (work.gate_0, work.gate_1, ()),
+                (work.value_0, work.value_1, (select_sum, layer_out, input_grad)),
+            )
         )
     else:
         normed = chosen(saved_0.normed, saved_1.normed)
@@ -1298,27 +1380,12 @@
             )
 
         scaled_sum = scattered(
-            chosen(kept_0.scaled, kept_1.scaled), chosen(kept_0.low_grad, kept_1.low_grad), 1
-        )
-        gate_sum = scattered(normed, chosen(kept_0.gate, kept_1.gate), 0)
-        value_sum = scattered(normed, chosen(kept_0.value, kept_1.value), 0)
-    quarter = 2 * NST // 4
-    select_sum = lax.all_gather(value_sum[:, width : width + quarter], HEAD, axis=1, tiled=True)
-
-    def sum_over(values, axis):
-        count = lax.axis_size(axis)
-        if count != 4:
-            return lax.psum(values, axis)
-        moved = [
-            lax.ppermute(values, axis, [(source, source ^ step) for source in range(count)])
-            for step in (1, 2, 3)
-        ]
-        return (values + moved[0]) + (moved[1] + moved[2])
-
-    norm_sum, head_sum = (chosen(left, right) for left, right in zip(sums_0, sums_1, strict=True))
-    packed = sum_over(jnp.concatenate([norm_sum, head_sum]), TOK)
-    norm_sum = sum_over(lax.dynamic_slice_in_dim(packed[:D], tok * (D // tok_count), D // tok_count, 0), HEAD)
-    head_sum = packed[D:]
+            chosen(saved_0.scaled, saved_1.scaled), chosen(work.low_grad_0, grad_rows_1), 1
+        )
+        gate_sum, value_sum = (
+            scattered(normed, chosen(left, right), 0)
+            for left, right in ((kept_0.gate, kept_1.gate), (kept_0.value, kept_1.value))
+        )
     pieces, place = ([], 0)
     for shape in ((K + 1, width), (K + 1, 2 * NST), (heads, P_SIZE), (heads,), (heads,), (heads,)):
         size = 1
@@ -1337,9 +1404,9 @@
         input_grad.reshape(micros, row_count, D),
         norm_sum,
         gate_sum,
-        value_sum[:, :width],
+        value_sum,
         select_sum,
-        value_sum[:, width + quarter : width + quarter + heads],
+        rest_sum[:, quarter : quarter + heads],
         mine(value_taps[:K].reshape(K, heads, P_SIZE), 2),
         mine(value_taps[K].reshape(heads, P_SIZE), 1),
         mine(select_taps[:K], 1),

time: 953 us -> 928 us (0.974)
  the two profiles are of different devices: /device:TPU:0 before, /device:TPU:29 now
where the time goes in v2:
time: 928 us; the launch traced here: 916 us
  waiting for transfers between devices  293 us (32%)
  starting transfers between devices  268 us (29%)
  Pallas kernels  235 us (25%)
  other arithmetic  56.7 us (6%)
  local copies, waits for them, and re-layouts  45.1 us (5%)
  matrix products  15.9 us (2%)
    pallas_call x32, Pallas kernels, call(): pl.pallas_call(guarded, grid_spec=pltpu.PrefetchScalarGridSpec(num_scalar...  235 us
    ppermute x76, starting transfers between devices, send(): return lax.ppermute(value, AXES, pairs)  183 us
    ppermute x76, waiting for transfers between devices, send(): return lax.ppermute(value, AXES, pairs)  172 us
    ppermute x1, waiting for transfers between devices, shards(): chunk_1 = lax.ppermute(moved, SECTION, [(0, 1)])  84.4 us
    ppermute x3, starting transfers between devices, shards(): lax.ppermute(jnp.concatenate([block_of(tok ^ step), packed], axis=0), TOK...  37.9 us
    ppermute x1, starting transfers between devices, shards(): lax.ppermute(full_1, SECTION, [(1, 0)])  24.4 us
    ppermute x1, waiting for transfers between devices, tell(): return lax.ppermute(values[:8, :128], SECTION, [(0, 1)])  19.6 us
  transfers between devices with their start and end apart: 87, of which 19 were waited for; matrix products, arithmetic and copies ran while one was open for 10% of the time, Pallas kernels for 21%

profile of v2, /device:TPU:29, one launch (start us, length us, event | category | flops | bytes accessed | tf_op | source)
XLA Modules:
  0.0 915.9 jit_solution(4834013894028796676)
XLA Ops:
  77.1 84.4 %collective-permute-done.11.refs_1_ = f32[128,2048]{1,0:T(8,128)S(1)} collective-permute-done((f32[128,2048]{1,0:T(8,128)S(1)}, f32[128,2048]{1,0:T(8,128)S(1)}, u32[]{:S(2)}, u32[]{:S(2)}) %collective-permute-start.11) | collective-permute-done | bytes 1048608 | tf_op jit(solution)/shard_map/ppermute | solution.py:1196
  177.3 13.4 %collective-permute-done.15.refs_3_ = f32[128,2048]{1,0:T(8,128)S(1)} collective-permute-done((f32[128,2048]{1,0:T(8,128)S(1)}, f32[128,2048]{1,0:T(8,128)S(1)}, u32[]{:S(2)}, u32[]{:S(2)}) %collective-permute-start.15) | collective-permute-done | bytes 1048608 | tf_op jit(solution)/shard_map/ppermute | solution.py:39
  192.7 11.1 %shard_map.295 = (bf16[512,2048]{1,0:T(8,128)(2,1)}, f32[512,1024]{1,0:T(8,128)}, f32[512,256]{1,0:T(8,128)}, f32[512,16]{1,0:T(8,128)}) custom-call(s32[5]{0:T(128)} %stack.33.refs_0_.refs_1_, f32[128,2048]{1,0:T(8,128)} %copy-done.4, f32[128,2048]{1,0:T(8,128)} %copy-done.17, f32[128,2048]{1,0:T(8,128)} %copy-done.18, f32[128,2048]{1,0:T(8,128)} %copy-done.19, ...), custom_call_target="tpu_custom_call" | custom-call | flops 2684354560 | bytes 14262272 | tf_op jit(solution)/shard_map/pallas_call | solution.py:101
  211.2 9.5 %shard_map.296 = (f32[512,1280]{1,0:T(8,128)}, f32[512,128]{1,0:T(8,128)}, f32[256,256]{1,0:T(8,128)}, f32[2048,128]{1,0:T(8,128)}) custom-call(s32[2,4]{1,0:T(2,128)} %reduce_window_sum.11.refs_0_, s32[5]{0:T(128)} %stack.33.refs_0_.refs_1_, f32[512,1024]{1,0:T(8,128)} %get-tuple-element.167.refs_2_.refs_4_, f32[512,256]{1,0:T(8,128)} %get-tuple-element.168.refs_3_.refs_7_, ...), custom_call_target="tpu_custom_call" | custom-call | flops 20971520 | bytes 6975488 | tf_op jit(solution)/shard_map/pallas_call | solution.py:101
  222.8 8.3 shard_map.297.refs_1_
  241.6 26.3 %collective-permute-done.20 = f32[2048,128]{1,0:T(8,128)S(1)} collective-permute-done((f32[2048,128]{1,0:T(8,128)S(1)}, f32[2048,128]{1,0:T(8,128)S(1)}, u32[]{:S(2)}, u32[]{:S(2)}) %collective-permute-start.20) | collective-permute-done | bytes 1048608 | tf_op jit(solution)/shard_map/ppermute | solution.py:39
  290.4 8.8 shard_map.300
  303.7 18.0 %shard_map.301 = (f32[512,1024]{1,0:T(8,128)}, f32[512,256]{1,0:T(8,128)}, f32[64,256]{1,0:T(8,128)}, f32[32,128]{1,0:T(8,128)}) custom-call(s32[2,4]{1,0:T(2,128)} %reduce_window_sum.11.refs_0_, s32[5]{0:T(128)} %stack.33.refs_0_.refs_1_, f32[512,1280]{1,0:T(8,128)} %get-tuple-element.170.refs_2_.refs_7_.refs_1_, ...), custom_call_target="tpu_custom_call" | custom-call | flops 209715200 | bytes 8998912 | tf_op jit(solution)/shard_map/pallas_call | solution.py:101
  336.1 9.1 shard_map.302
  350.5 15.4 %collective-permute-start.29 = (f32[16,256]{1,0:T(8,128)S(1)}, f32[16,256]{1,0:T(8,128)S(1)}, u32[]{:S(2)}, u32[]{:S(2)}) collective-permute-start(f32[16,256]{1,0:T(8,128)S(1)} %slice_bitcast_fusion.5), channel_id=1, source_target_pairs={{20,17},{21,16},{22,19},{23,18},{24,21},{25,20},{26,23},{27,22},{2... | collective-permute-start | bytes 49160 | tf_op jit(solution)/shard_map/ppermute | solution.py:39
  384.2 13.1 %shard_map.304 = (f32[512,1024]{1,0:T(8,128)}, f32[16,1024]{1,0:T(8,128)}, f32[128,2048]{1,0:T(8,128)}, f32[128,2048]{1,0:T(8,128)}, f32[128,2048]{1,0:T(8,128)}, /*index=5*/f32[128,2048]{1,0:T(8,128)}) custom-call(s32[2,4]{1,0:T(2,128)} %reduce_window_sum.11.refs_0_, s32[5]{0:T(128)} %stack.33.refs_0_.refs_1_, f32[512,1024]{1,0:T(8,128)} %get-tuple-element.197.refs_2_, ...), custom_call_target="tpu_custom_call" | custom-call | flops 2147483648 | bytes 19456000 | tf_op jit(solution)/shard_map/pallas_call | solution.py:101
  411.6 16.7 %collective-permute-done.36 = f32[128,2048]{1,0:T(8,128)S(1)} collective-permute-done((f32[128,2048]{1,0:T(8,128)}, f32[128,2048]{1,0:T(8,128)S(1)}, u32[]{:S(2)}, u32[]{:S(2)}) %collective-permute-start.36) | collective-permute-done | bytes 1048608 | tf_op jit(solution)/shard_map/ppermute | solution.py:39
  468.8 8.3 shard_map.306
  480.6 9.2 %shard_map.308 = (f32[512,1024]{1,0:T(8,128)}, f32[512,1024]{1,0:T(8,128)}, f32[2048,128]{1,0:T(8,128)}, f32[16,1024]{1,0:T(8,128)}, bf16[512,2048]{1,0:T(8,128)(2,1)}, /*index=5*/f32[512,2048]{1,0:T(8,128)}) custom-call(s32[5]{0:T(128)} %stack.30.refs_0_.refs_1_, f32[16,256]{1,0:T(8,128)} %get-tuple-element.157.refs_2_.refs_1_, f32[16,256]{1,0:T(8,128)} %copy-done.74, ...), custom_call_target="tpu_custom_call" | custom-call | flops 2147483648 | bytes 27398144 | tf_op jit(solution)/shard_map/pallas_call | solution.py:101
  498.5 28.9 %collective-permute-done.42 = f32[512,1024]{1,0:T(8,128)S(1)} collective-permute-done((f32[512,1024]{1,0:T(8,128)}, f32[512,1024]{1,0:T(8,128)S(1)}, u32[]{:S(2)}, u32[]{:S(2)}) %collective-permute-start.42) | collective-permute-done | bytes 2097184 | tf_op jit(solution)/shard_map/ppermute | solution.py:39
  528.8 8.9 shard_map.307
  590.1 11.2 %collective-permute-done.47.refs_3_ = f32[128,2048]{1,0:T(8,128)} collective-permute-done((f32[128,2048]{1,0:T(8,128)S(1)}, f32[128,2048]{1,0:T(8,128)}, u32[]{:S(2)}, u32[]{:S(2)}) %collective-permute-start.47) | collective-permute-done | bytes 1048608 | tf_op jit(solution)/shard_map/ppermute | solution.py:39
  633.6 19.6 %collective-permute-done.84.refs_5_ = f32[8,128]{1,0:T(8,128)S(1)} collective-permute-done((f32[8,128]{1,0:T(8,128)S(1)}, f32[8,128]{1,0:T(8,128)S(1)}, u32[]{:S(2)}, u32[]{:S(2)}) %collective-permute-start.84) | collective-permute-done | bytes 4128 | tf_op jit(solution)/shard_map/ppermute | solution.py:1259
  655.9 15.4 %collective-permute-start.66 = (f32[512,256]{1,0:T(8,128)}, f32[512,256]{1,0:T(8,128)S(1)}, u32[]{:S(2)}, u32[]{:S(2)}) collective-permute-start(f32[512,256]{1,0:T(8,128)} %get-tuple-element.230.refs_2_), channel_id=1, source_target_pairs={{0,1},{1,0},{2,3},{3,2},{4,5},{5,4},{6,7},{7,6},{8,9},{9,8},{10,11... | collective-permute-start | bytes 1572872 | tf_op jit(solution)/shard_map/ppermute | solution.py:39
  676.4 11.4 %collective-permute-start.82 = (f32[512,1024]{1,0:T(8,128)}, f32[512,1024]{1,0:T(8,128)}, u32[]{:S(2)}, u32[]{:S(2)}) collective-permute-start(f32[512,1024]{1,0:T(8,128)} %get-tuple-element.269), channel_id=1, source_target_pairs={{0,8},{1,9},{2,10},{3,11},{4,12},{5,13},{6,14},{7,15},{8,0},{9,1},... | collective-permute-start | bytes 6291464 | tf_op jit(solution)/shard_map/ppermute | solution.py:39
  709.2 24.4 %collective-permute-start.71 = (f32[512,2048]{1,0:T(8,128)}, f32[512,2048]{1,0:T(8,128)}, u32[]{:S(2)}, u32[]{:S(2)}) collective-permute-start(f32[512,2048]{1,0:T(8,128)} %shard_map.316), channel_id=1, source_target_pairs={{16,0},{17,1},{18,2},{19,3},{20,4},{21,5},{22,6},{23,7},{24,8},{25... | collective-permute-start | bytes 12582920 | tf_op jit(solution)/shard_map/ppermute | solution.py:1361
  738.5 13.5 %collective-permute-start.78 = (f32[592,128]{1,0:T(8,128)}, f32[592,128]{1,0:T(8,128)}, u32[]{:S(2)}, u32[]{:S(2)}) collective-permute-start(f32[592,128]{1,0:T(8,128)} %get-tuple-element.371), channel_id=1, source_target_pairs={{0,12},{4,8},{8,4},{12,0},{1,13},{5,9},{9,5},{13,1},{2,14},{6,10},... | collective-permute-start | bytes 909320 | tf_op jit(solution)/shard_map/ppermute | solution.py:1326
  753.3 18.6 %collective-permute-start.77 = (f32[592,128]{1,0:T(8,128)}, f32[592,128]{1,0:T(8,128)S(1)}, u32[]{:S(2)}, u32[]{:S(2)}) collective-permute-start(f32[592,128]{1,0:T(8,128)} %get-tuple-element.370), channel_id=1, source_target_pairs={{0,8},{4,12},{8,0},{12,4},{1,9},{5,13},{9,1},{13,5},{2,10},{6,14},... | collective-permute-start | bytes 909320 | tf_op jit(solution)/shard_map/ppermute | solution.py:1326
  836.2 45.2 %collective-permute-done.86 = f32[1024,512]{1,0:T(8,128)} collective-permute-done((f32[1024,512]{1,0:T(8,128)}, f32[1024,512]{1,0:T(8,128)}, u32[]{:S(2)}, u32[]{:S(2)}) %collective-permute-start.86) | collective-permute-done | bytes 2097184 | tf_op jit(solution)/shard_map/ppermute | solution.py:39
  (498 shorter events, 464.3 us)
Async XLA Ops:
  74.2 95.7 %collective-permute-start.12 = (f32[512,1024]{1,0:T(8,128)}, f32[512,1024]{1,0:T(8,128)S(1)}, u32[]{:S(2)}, u32[]{:S(2)}) collective-permute-start(f32[512,1024]{1,0:T(8,128)} %maximum_convert_fusion.1), channel_id=1, source_target_pairs={{0,4},{1,5},{2,6},{3,7},{4,0},{5,1},{6,2},{7,3},{8,12},{9,13},{10,... | collective-permute-start | bytes 6291464 | tf_op jit(solution)/shard_map/ppermute | solution.py:39
  75.0 94.9 %collective-permute-start.13 = (f32[512,1024]{1,0:T(8,128)S(1)}, f32[512,1024]{1,0:T(8,128)S(1)}, u32[]{:S(2)}, u32[]{:S(2)}) collective-permute-start(f32[512,1024]{1,0:T(8,128)S(1)} %copy-done.34), channel_id=1, source_target_pairs={{0,4},{1,5},{2,6},{3,7},{4,0},{5,1},{6,2},{7,3},{8,12},{9,13},{10,... | collective-permute-start | bytes 6291464 | tf_op jit(solution)/shard_map/ppermute | solution.py:39
  75.8 85.7 %collective-permute-start.11 = (f32[128,2048]{1,0:T(8,128)S(1)}, f32[128,2048]{1,0:T(8,128)S(1)}, u32[]{:S(2)}, u32[]{:S(2)}) collective-permute-start(f32[128,2048]{1,0:T(8,128)S(1)} %get-tuple-element.162), channel_id=1, source_target_pairs={{0,16},{1,17},{2,18},{3,19},{4,20},{5,21},{6,22},{7,23},{8,24},{9,... | collective-permute-start | bytes 3145736 | tf_op jit(solution)/shard_map/ppermute | solution.py:1196
  324.0 49.7 %collective-permute-start.32 = (f32[512,1024]{1,0:T(8,128)}, f32[512,1024]{1,0:T(8,128)}, u32[]{:S(2)}, u32[]{:S(2)}) collective-permute-start(f32[512,1024]{1,0:T(8,128)} %get-tuple-element.195.refs_3_), channel_id=1, source_target_pairs={{16,20},{17,21},{18,22},{19,23},{20,16},{21,17},{22,18},{23,19},{2... | collective-permute-start | bytes 6291464 | tf_op jit(solution)/shard_map/ppermute | solution.py:39
  345.9 37.6 %collective-permute-start.28 = (f32[16,256]{1,0:T(8,128)S(1)}, f32[16,256]{1,0:T(8,128)S(1)}, u32[]{:S(2)}, u32[]{:S(2)}) collective-permute-start(f32[16,256]{1,0:T(8,128)S(1)} %slice_bitcast_fusion.5), channel_id=1, source_target_pairs={{20,16},{21,17},{22,18},{23,19},{24,20},{25,21},{26,22},{27,23},{2... | collective-permute-start | bytes 49160 | tf_op jit(solution)/shard_map/ppermute | solution.py:39
  397.3 61.0 %collective-permute-start.34 = (f32[512,1024]{1,0:T(8,128)}, f32[512,1024]{1,0:T(8,128)}, u32[]{:S(2)}, u32[]{:S(2)}) collective-permute-start(f32[512,1024]{1,0:T(8,128)} %get-tuple-element.198.refs_3_), channel_id=1, source_target_pairs={{16,20},{17,21},{18,22},{19,23},{20,16},{21,17},{22,18},{23,19},{2... | collective-permute-start | bytes 6291464 | tf_op jit(solution)/shard_map/ppermute | solution.py:39
  399.3 59.0 %collective-permute-start.38 = (f32[512,1024]{1,0:T(8,128)}, f32[512,1024]{1,0:T(8,128)S(1)}, u32[]{:S(2)}, u32[]{:S(2)}) collective-permute-start(f32[512,1024]{1,0:T(8,128)} %get-tuple-element.204), channel_id=1, source_target_pairs={{16,24},{17,25},{18,26},{19,27},{20,28},{21,29},{22,30},{23,31},{2... | collective-permute-start | bytes 6291464 | tf_op jit(solution)/shard_map/ppermute | solution.py:39
  477.1 50.3 %collective-permute-start.42 = (f32[512,1024]{1,0:T(8,128)}, f32[512,1024]{1,0:T(8,128)S(1)}, u32[]{:S(2)}, u32[]{:S(2)}) collective-permute-start(f32[512,1024]{1,0:T(8,128)} %get-tuple-element.211), channel_id=1, source_target_pairs={{16,24},{17,25},{18,26},{19,27},{20,28},{21,29},{22,30},{23,31},{2... | collective-permute-start | bytes 6291464 | tf_op jit(solution)/shard_map/ppermute | solution.py:39
  496.8 55.6 %collective-permute-start.54 = (f32[2048,128]{1,0:T(8,128)}, f32[2048,128]{1,0:T(8,128)}, u32[]{:S(2)}, u32[]{:S(2)}) collective-permute-start(f32[2048,128]{1,0:T(8,128)} %multiply_add_fusion.1), channel_id=1, source_target_pairs={{8,4},{9,5},{10,6},{11,7}} | collective-permute-start | bytes 3145736 | tf_op jit(solution)/shard_map/ppermute | solution.py:39
  558.1 44.5 %collective-permute-start.60 = (f32[512,1024]{1,0:T(8,128)}, f32[512,1024]{1,0:T(8,128)}, u32[]{:S(2)}, u32[]{:S(2)}) collective-permute-start(f32[512,1024]{1,0:T(8,128)} %get-tuple-element.233.refs_3_), channel_id=1, source_target_pairs={{0,4},{1,5},{2,6},{3,7},{4,0},{5,1},{6,2},{7,3},{8,12},{9,13},{10,... | collective-permute-start | bytes 6291464 | tf_op jit(solution)/shard_map/ppermute | solution.py:39
  572.0 54.2 %collective-permute-start.65 = (f32[512,1024]{1,0:T(8,128)}, f32[512,1024]{1,0:T(8,128)}, u32[]{:S(2)}, u32[]{:S(2)}) collective-permute-start(f32[512,1024]{1,0:T(8,128)} %maximum_convert_fusion.3), channel_id=1, source_target_pairs={{0,4},{1,5},{2,6},{3,7},{4,0},{5,1},{6,2},{7,3},{8,12},{9,13},{10,... | collective-permute-start | bytes 6291464 | tf_op jit(solution)/shard_map/ppermute | solution.py:39
  620.2 51.1 %collective-permute-start.64 = (f32[128,2048]{1,0:T(8,128)}, f32[128,2048]{1,0:T(8,128)}, u32[]{:S(2)}, u32[]{:S(2)}) collective-permute-start(f32[128,2048]{1,0:T(8,128)} %get-tuple-element.240), channel_id=1, source_target_pairs={{0,3},{1,2},{2,1},{3,0},{4,7},{5,6},{6,5},{7,4},{8,11},{9,10},{10,... | collective-permute-start | bytes 3145736 | tf_op jit(solution)/shard_map/ppermute | solution.py:39
  621.8 50.9 %collective-permute-start.62 = (f32[128,2048]{1,0:T(8,128)}, f32[128,2048]{1,0:T(8,128)}, u32[]{:S(2)}, u32[]{:S(2)}) collective-permute-start(f32[128,2048]{1,0:T(8,128)} %get-tuple-element.238), channel_id=1, source_target_pairs={{0,1},{1,0},{2,3},{3,2},{4,5},{5,4},{6,7},{7,6},{8,9},{9,8},{10,11... | collective-permute-start | bytes 3145736 | tf_op jit(solution)/shard_map/ppermute | solution.py:39
  625.3 72.1 %collective-permute-start.70 = (f32[512,1024]{1,0:T(8,128)}, f32[512,1024]{1,0:T(8,128)S(1)}, u32[]{:S(2)}, u32[]{:S(2)}) collective-permute-start(f32[512,1024]{1,0:T(8,128)} %get-tuple-element.251.refs_3_), channel_id=1, source_target_pairs={{0,4},{1,5},{2,6},{3,7},{4,0},{5,1},{6,2},{7,3},{8,12},{9,13},{10,... | collective-permute-start | bytes 6291464 | tf_op jit(solution)/shard_map/ppermute | solution.py:39
  653.1 44.3 %collective-permute-start.69 = (f32[1024,512]{1,0:T(8,128)}, f32[1024,512]{1,0:T(8,128)}, u32[]{:S(2)}, u32[]{:S(2)}) collective-permute-start(f32[1024,512]{1,0:T(8,128)} %get-tuple-element.250), channel_id=1, source_target_pairs={{0,8},{1,9},{2,10},{3,11},{4,12},{5,13},{6,14},{7,15},{8,0},{9,1},... | collective-permute-start | bytes 6291464 | tf_op jit(solution)/shard_map/ppermute | solution.py:39
  676.4 76.9 %collective-permute-start.82 = (f32[512,1024]{1,0:T(8,128)}, f32[512,1024]{1,0:T(8,128)}, u32[]{:S(2)}, u32[]{:S(2)}) collective-permute-start(f32[512,1024]{1,0:T(8,128)} %get-tuple-element.269), channel_id=1, source_target_pairs={{0,8},{1,9},{2,10},{3,11},{4,12},{5,13},{6,14},{7,15},{8,0},{9,1},... | collective-permute-start | bytes 6291464 | tf_op jit(solution)/shard_map/ppermute | solution.py:39
  687.8 84.0 %collective-permute-start.85 = (f32[512,1024]{1,0:T(8,128)}, f32[512,1024]{1,0:T(8,128)}, u32[]{:S(2)}, u32[]{:S(2)}) collective-permute-start(f32[512,1024]{1,0:T(8,128)} %get-tuple-element.273.refs_3_), channel_id=1, source_target_pairs={{16,20},{17,21},{18,22},{19,23},{20,16},{21,17},{22,18},{23,19},{2... | collective-permute-start | bytes 6291464 | tf_op jit(solution)/shard_map/ppermute | solution.py:39
  709.2 173.9 %collective-permute-start.71 = (f32[512,2048]{1,0:T(8,128)}, f32[512,2048]{1,0:T(8,128)}, u32[]{:S(2)}, u32[]{:S(2)}) collective-permute-start(f32[512,2048]{1,0:T(8,128)} %shard_map.316), channel_id=1, source_target_pairs={{16,0},{17,1},{18,2},{19,3},{20,4},{21,5},{22,6},{23,7},{24,8},{25... | collective-permute-start | bytes 12582920 | tf_op jit(solution)/shard_map/ppermute | solution.py:1361
  736.1 168.4 %collective-permute-start.75 = (f32[512,2048]{1,0:T(8,128)}, f32[512,2048]{1,0:T(8,128)}, u32[]{:S(2)}, u32[]{:S(2)}) collective-permute-start(f32[512,2048]{1,0:T(8,128)} %get-tuple-element.255), channel_id=1, source_target_pairs={{0,16},{1,17},{2,18},{3,19},{4,20},{5,21},{6,22},{7,23},{8,24},{9,... | collective-permute-start | bytes 12582920 | tf_op jit(solution)/shard_map/ppermute | solution.py:1363
  738.5 47.4 %collective-permute-start.78 = (f32[592,128]{1,0:T(8,128)}, f32[592,128]{1,0:T(8,128)}, u32[]{:S(2)}, u32[]{:S(2)}) collective-permute-start(f32[592,128]{1,0:T(8,128)} %get-tuple-element.371), channel_id=1, source_target_pairs={{0,12},{4,8},{8,4},{12,0},{1,13},{5,9},{9,5},{13,1},{2,14},{6,10},... | collective-permute-start | bytes 909320 | tf_op jit(solution)/shard_map/ppermute | solution.py:1326
  753.3 39.2 %collective-permute-start.77 = (f32[592,128]{1,0:T(8,128)}, f32[592,128]{1,0:T(8,128)S(1)}, u32[]{:S(2)}, u32[]{:S(2)}) collective-permute-start(f32[592,128]{1,0:T(8,128)} %get-tuple-element.370), channel_id=1, source_target_pairs={{0,8},{4,12},{8,0},{12,4},{1,9},{5,13},{9,1},{13,5},{2,10},{6,14},... | collective-permute-start | bytes 909320 | tf_op jit(solution)/shard_map/ppermute | solution.py:1326
  785.9 95.5 %collective-permute-start.86 = (f32[1024,512]{1,0:T(8,128)}, f32[1024,512]{1,0:T(8,128)}, u32[]{:S(2)}, u32[]{:S(2)}) collective-permute-start(f32[1024,512]{1,0:T(8,128)} %get-tuple-element.275), channel_id=1, source_target_pairs={{16,24},{17,25},{18,26},{19,27},{20,28},{21,29},{22,30},{23,31},{2... | collective-permute-start | bytes 6291464 | tf_op jit(solution)/shard_map/ppermute | solution.py:39
  800.3 110.6 %collective-permute-start.83 = (f32[512,1024]{1,0:T(8,128)}, f32[512,1024]{1,0:T(8,128)}, u32[]{:S(2)}, u32[]{:S(2)}) collective-permute-start(f32[512,1024]{1,0:T(8,128)} %get-tuple-element.270), channel_id=1, source_target_pairs={{0,8},{1,9},{2,10},{3,11},{4,12},{5,13},{6,14},{7,15},{8,0},{9,1},... | collective-permute-start | bytes 6291464 | tf_op jit(solution)/shard_map/ppermute | solution.py:39
  834.6 69.9 %collective-permute-start.72 = (f32[128,2048]{1,0:T(8,128)S(1)}, f32[128,2048]{1,0:T(8,128)}, u32[]{:S(2)}, u32[]{:S(2)}) collective-permute-start(f32[128,2048]{1,0:T(8,128)S(1)} %fusion.3.refs_1_), channel_id=1, source_target_pairs={{0,1},{1,0},{2,3},{3,2},{4,5},{5,4},{6,7},{7,6},{8,9},{9,8},{10,11... | collective-permute-start | bytes 3145736 | tf_op jit(solution)/shard_map/ppermute | solution.py:39
  (149 other events, 2285.6 us)

commit v3 on v2

--- a/solution.py
+++ b/solution.py
@@ -1253,6 +1253,10 @@
         work.value_1 = pair_product(
             1, saved_1.normed, other_1, kept_1.value, after(work.value_other, grad_mid)
         )
+        scaled_other = exchange(1, after(saved_1.scaled, grad_mid))
+        work.scaled_1 = pair_product(
+            1, grad_rows_1, grad_other_1, after(saved_1.scaled, work.value_1[0]), scaled_other, True
+        )
         parts_0[0] = after(parts_0[0], work.value_1[0])
 
     def tell(values):
@@ -1280,7 +1284,7 @@
         work.gate_0 = pair_product(
             0, saved_0.normed, other_0, after(work.kept_gate_0, done), work.gate_other_0, hold=halo
         )
-        return (work.gate_0[0], *work.shown_1)
+        return (work.gate_0[0], work.scaled_1[1], *work.shown_1)
 
     def beside_sum_0(piece, low_value):
         if not pairwise:
@@ -1288,11 +1292,6 @@
         work.value_other_0 = exchange(0, low_value)
         work.scaled_0 = pair_product(
             0, work.low_grad_0, work.grad_other_0, after(saved_0.scaled, piece), scaled_0, True
-        )
-        mark = tell(piece)
-        scaled_other = exchange(1, after(saved_1.scaled, mark))
-        work.scaled_1 = pair_product(
-            1, grad_rows_1, grad_other_1, saved_1.scaled, scaled_other, True, marks=(mark,)
         )
         return (work.scaled_0[0],)
 

time: 928 us -> 904 us (0.974)
  the two profiles are of different devices: /device:TPU:29 before, /device:TPU:0 now
where the time goes in v3:
time: 904 us; the launch traced here: 893 us
  starting transfers between devices  342 us (38%)
  Pallas kernels  234 us (26%)
  waiting for transfers between devices  198 us (22%)
  other arithmetic  54.9 us (6%)
  local copies, waits for them, and re-layouts  46.5 us (5%)
  matrix products  14.8 us (2%)
    ppermute x76, starting transfers between devices, send(): return lax.ppermute(value, AXES, pairs)  305 us
    pallas_call x32, Pallas kernels, call(): pl.pallas_call(guarded, grid_spec=pltpu.PrefetchScalarGridSpec(num_scalar...  234 us
    ppermute x76, waiting for transfers between devices, send(): return lax.ppermute(value, AXES, pairs)  165 us
  transfers between devices with their start and end apart: 86, of which 18 were waited for; matrix products, arithmetic and copies ran while one was open for 10% of the time, Pallas kernels for 22%

profile of v3, /device:TPU:0, one launch (start us, length us, event | category | flops | bytes accessed | tf_op | source)
XLA Modules:
  0.0 892.9 jit_solution(5049739838881233925)
XLA Ops:
  3.1 10.3 %shard_map.288 = (bf16[512,2048]{1,0:T(8,128)(2,1)}, f32[512,1024]{1,0:T(8,128)}, f32[512,256]{1,0:T(8,128)}, f32[512,16]{1,0:T(8,128)}) custom-call(s32[5]{0:T(128)} %stack.30.refs_0_.refs_1_, bf16[512,2048]{1,0:T(8,128)(2,1)} %bitcast.178, f32[1,2048]{1,0:T(1,128)} %refs_5_.1, bf16[2048,1024]{1,0:T(8,128)(2,1)} %bitcast.148, bf16[2048,256]{1,0:T(8,128)(2,1)} %bitcast.162, ...), custom_call_target="tpu_custom_call" | custom-call | flops 2684354560 | bytes 12165120 | tf_op jit(solution)/shard_map/pallas_call | solution.py:101
  22.9 9.5 %shard_map.289 = (f32[512,1280]{1,0:T(8,128)}, f32[512,128]{1,0:T(8,128)}, f32[256,256]{1,0:T(8,128)}, f32[2048,128]{1,0:T(8,128)}) custom-call(s32[2,4]{1,0:T(2,128)} %reduce_window_sum.11.refs_0_, s32[5]{0:T(128)} %stack.30.refs_0_.refs_1_, f32[512,1024]{1,0:T(8,128)} %get-tuple-element.147.refs_2_.refs_4_, f32[512,256]{1,0:T(8,128)} %get-tuple-element.148.refs_3_.refs_7_, ...), custom_call_target="tpu_custom_call" | custom-call | flops 20971520 | bytes 6975488 | tf_op jit(solution)/shard_map/pallas_call | solution.py:101
  38.2 8.2 shard_map.290.refs_1_
  86.6 8.5 shard_map.293
  112.4 10.9 %collective-permute-done.8 = f32[128,2048]{1,0:T(8,128)S(1)} collective-permute-done((f32[128,2048]{1,0:T(8,128)}, f32[128,2048]{1,0:T(8,128)S(1)}, u32[]{:S(2)}, u32[]{:S(2)}) %collective-permute-start.8) | collective-permute-done | bytes 1048608 | tf_op jit(solution)/shard_map/ppermute | solution.py:39
  130.0 17.1 %collective-permute-start.12 = (f32[512,1024]{1,0:T(8,128)}, f32[512,1024]{1,0:T(8,128)S(1)}, u32[]{:S(2)}, u32[]{:S(2)}) collective-permute-start(f32[512,1024]{1,0:T(8,128)} %maximum_convert_fusion.1), channel_id=1, source_target_pairs={{0,4},{1,5},{2,6},{3,7},{4,0},{5,1},{6,2},{7,3},{8,12},{9,13},{10,... | collective-permute-start | bytes 6291464 | tf_op jit(solution)/shard_map/ppermute | solution.py:39
  154.9 16.5 %collective-permute-done.12.refs_2_ = f32[512,1024]{1,0:T(8,128)S(1)} collective-permute-done((f32[512,1024]{1,0:T(8,128)}, f32[512,1024]{1,0:T(8,128)S(1)}, u32[]{:S(2)}, u32[]{:S(2)}) %collective-permute-start.12) | collective-permute-done | bytes 2097184 | tf_op jit(solution)/shard_map/ppermute | solution.py:39
  171.4 22.5 %collective-permute-done.13.refs_4_ = f32[512,1024]{1,0:T(8,128)S(1)} collective-permute-done((f32[512,1024]{1,0:T(8,128)S(1)}, f32[512,1024]{1,0:T(8,128)S(1)}, u32[]{:S(2)}, u32[]{:S(2)}) %collective-permute-start.13) | collective-permute-done | bytes 2097184 | tf_op jit(solution)/shard_map/ppermute | solution.py:39
  197.2 7.5 shard_map.295
  279.8 8.0 shard_map.304
  294.9 140.8 %collective-permute-start.39 = (f32[512,256]{1,0:T(8,128)S(1)}, f32[512,256]{1,0:T(8,128)S(1)}, u32[]{:S(2)}, u32[]{:S(2)}) collective-permute-start(f32[512,256]{1,0:T(8,128)S(1)} %copy-done.52), channel_id=1, source_target_pairs={{16,17},{17,16},{18,19},{19,18},{20,21},{21,20},{22,23},{23,22},{2... | collective-permute-start | bytes 1572872 | tf_op jit(solution)/shard_map/ppermute | solution.py:39
  447.1 17.9 %collective-permute-done.49 = f32[128,2048]{1,0:T(8,128)S(1)} collective-permute-done((f32[128,2048]{1,0:T(8,128)S(1)}, f32[128,2048]{1,0:T(8,128)S(1)}, u32[]{:S(2)}, u32[]{:S(2)}) %collective-permute-start.49) | collective-permute-done | bytes 1048608 | tf_op jit(solution)/shard_map/ppermute | solution.py:1244
  484.2 14.9 %collective-permute-done.51.refs_12_ = f32[128,2176]{1,0:T(8,128)} collective-permute-done((f32[128,2176]{1,0:T(8,128)S(1)}, f32[128,2176]{1,0:T(8,128)}, u32[]{:S(2)}, u32[]{:S(2)}) %collective-permute-start.51) | collective-permute-done | bytes 1114144 | tf_op jit(solution)/shard_map/ppermute | solution.py:39
  499.1 14.5 %shard_map.308 = (f32[512,1024]{1,0:T(8,128)}, f32[512,1024]{1,0:T(8,128)}, f32[2048,128]{1,0:T(8,128)}, f32[16,1024]{1,0:T(8,128)}, bf16[512,2048]{1,0:T(8,128)(2,1)}, /*index=5*/f32[512,2048]{1,0:T(8,128)}) custom-call(s32[5]{0:T(128)} %stack.30.refs_0_.refs_1_, f32[16,256]{1,0:T(8,128)} %get-tuple-element.158.refs_2_.refs_1_, f32[16,256]{1,0:T(8,128)} %copy-done.75, ...), custom_call_target="tpu_custom_call" | custom-call | flops 2147483648 | bytes 27398144 | tf_op jit(solution)/shard_map/pallas_call | solution.py:101
  514.3 17.6 %shard_map.309 = (f32[512,1024]{1,0:T(8,128)}, f32[512,256]{1,0:T(8,128)}, f32[64,256]{1,0:T(8,128)}, f32[32,128]{1,0:T(8,128)}) custom-call(s32[2,4]{1,0:T(2,128)} %reduce_window_sum.11.refs_0_, s32[5]{0:T(128)} %stack.30.refs_0_.refs_1_, f32[512,1280]{1,0:T(8,128)} %get-tuple-element.150.refs_2_.refs_7_.refs_1_, ...), custom_call_target="tpu_custom_call" | custom-call | flops 209715200 | bytes 8998912 | tf_op jit(solution)/shard_map/pallas_call | solution.py:101
  591.2 9.0 %shard_map.310 = (f32[512,1024]{1,0:T(8,128)}, f32[512,256]{1,0:T(8,128)}, f32[512,128]{1,0:T(8,128)}, f32[32,128]{1,0:T(8,128)}) custom-call(s32[5]{0:T(128)} %stack.30.refs_0_.refs_1_, f32[512,1280]{1,0:T(8,128)} %get-tuple-element.150.refs_2_.refs_7_.refs_1_, f32[512,128]{1,0:T(8,128)} %get-tuple-element.151.refs_3_.refs_8_.refs_2_, ...), custom_call_target="tpu_custom_call" | custom-call | flops 31457280 | bytes 10838016 | tf_op jit(solution)/shard_map/pallas_call | solution.py:101
  605.7 18.7 %collective-permute-done.60.refs_4_ = f32[512,1024]{1,0:T(8,128)} collective-permute-done((f32[512,1024]{1,0:T(8,128)}, f32[512,1024]{1,0:T(8,128)}, u32[]{:S(2)}, u32[]{:S(2)}) %collective-permute-start.60) | collective-permute-done | bytes 2097184 | tf_op jit(solution)/shard_map/ppermute | solution.py:39
  625.7 21.3 %collective-permute-done.56 = f32[16,256]{1,0:T(8,128)S(1)} collective-permute-done((f32[16,256]{1,0:T(8,128)S(1)}, f32[16,256]{1,0:T(8,128)S(1)}, u32[]{:S(2)}, u32[]{:S(2)}) %collective-permute-start.56) | collective-permute-done | bytes 16416 | tf_op jit(solution)/shard_map/ppermute | solution.py:39
  648.5 8.3 shard_map.311
  657.4 13.1 %shard_map.313 = (f32[512,1024]{1,0:T(8,128)}, f32[16,1024]{1,0:T(8,128)}, f32[128,2048]{1,0:T(8,128)}, f32[128,2048]{1,0:T(8,128)}, f32[128,2048]{1,0:T(8,128)}, /*index=5*/f32[128,2048]{1,0:T(8,128)}) custom-call(s32[2,4]{1,0:T(2,128)} %reduce_window_sum.11.refs_0_, s32[5]{0:T(128)} %stack.30.refs_0_.refs_1_, f32[512,1024]{1,0:T(8,128)} %get-tuple-element.240.refs_2_, ...), custom_call_target="tpu_custom_call" | custom-call | flops 2147483648 | bytes 19456000 | tf_op jit(solution)/shard_map/pallas_call | solution.py:101
  684.9 8.3 shard_map.314
  729.1 38.2 %collective-permute-done.71 = f32[1024,512]{1,0:T(8,128)} collective-permute-done((f32[1024,512]{1,0:T(8,128)}, f32[1024,512]{1,0:T(8,128)}, u32[]{:S(2)}, u32[]{:S(2)}) %collective-permute-start.71) | collective-permute-done | bytes 2097184 | tf_op jit(solution)/shard_map/ppermute | solution.py:39
  767.3 8.4 shard_map.316
  810.9 13.1 %collective-permute-done.79 = f32[592,128]{1,0:T(8,128)S(1)} collective-permute-done((f32[592,128]{1,0:T(8,128)S(1)}, f32[592,128]{1,0:T(8,128)S(1)}, u32[]{:S(2)}, u32[]{:S(2)}) %collective-permute-start.79) | collective-permute-done | bytes 303136 | tf_op jit(solution)/shard_map/ppermute | solution.py:1325
  (499 shorter events, 427.0 us)
Async XLA Ops:
  61.7 68.3 %collective-permute-start.10 = (f32[512,1024]{1,0:T(8,128)}, f32[512,1024]{1,0:T(8,128)}, u32[]{:S(2)}, u32[]{:S(2)}) collective-permute-start(f32[512,1024]{1,0:T(8,128)} %maximum_convert_fusion), channel_id=1, source_target_pairs={{16,20},{17,21},{18,22},{19,23},{20,16},{21,17},{22,18},{23,19},{2... | collective-permute-start | bytes 6291464 | tf_op jit(solution)/shard_map/ppermute | solution.py:39
  130.0 41.3 %collective-permute-start.12 = (f32[512,1024]{1,0:T(8,128)}, f32[512,1024]{1,0:T(8,128)S(1)}, u32[]{:S(2)}, u32[]{:S(2)}) collective-permute-start(f32[512,1024]{1,0:T(8,128)} %maximum_convert_fusion.1), channel_id=1, source_target_pairs={{0,4},{1,5},{2,6},{3,7},{4,0},{5,1},{6,2},{7,3},{8,12},{9,13},{10,... | collective-permute-start | bytes 6291464 | tf_op jit(solution)/shard_map/ppermute | solution.py:39
  147.2 46.7 %collective-permute-start.13 = (f32[512,1024]{1,0:T(8,128)S(1)}, f32[512,1024]{1,0:T(8,128)S(1)}, u32[]{:S(2)}, u32[]{:S(2)}) collective-permute-start(f32[512,1024]{1,0:T(8,128)S(1)} %copy-done.35), channel_id=1, source_target_pairs={{0,4},{1,5},{2,6},{3,7},{4,0},{5,1},{6,2},{7,3},{8,12},{9,13},{10,... | collective-permute-start | bytes 6291464 | tf_op jit(solution)/shard_map/ppermute | solution.py:39
  152.7 41.2 %collective-permute-start.14 = (f32[128,2048]{1,0:T(8,128)S(1)}, f32[128,2048]{1,0:T(8,128)S(1)}, u32[]{:S(2)}, u32[]{:S(2)}) collective-permute-start(f32[128,2048]{1,0:T(8,128)S(1)} %collective-permute-done.11.refs_1_), channel_id=1, source_target_pairs={{16,17},{17,16},{18,19},{19,18},{20,21},{21,20},{22,23},{23,22},{2... | collective-permute-start | bytes 3145736 | tf_op jit(solution)/shard_map/ppermute | solution.py:39
  153.4 40.5 %collective-permute-start.15 = (f32[128,2048]{1,0:T(8,128)S(1)}, f32[128,2048]{1,0:T(8,128)S(1)}, u32[]{:S(2)}, u32[]{:S(2)}) collective-permute-start(f32[128,2048]{1,0:T(8,128)S(1)} %collective-permute-done.11.refs_1_), channel_id=1, source_target_pairs={{16,18},{17,19},{18,16},{19,17},{20,22},{21,23},{22,20},{23,21},{2... | collective-permute-start | bytes 3145736 | tf_op jit(solution)/shard_map/ppermute | solution.py:39
  154.1 41.0 %collective-permute-start.16 = (f32[128,2048]{1,0:T(8,128)S(1)}, f32[128,2048]{1,0:T(8,128)S(1)}, u32[]{:S(2)}, u32[]{:S(2)}) collective-permute-start(f32[128,2048]{1,0:T(8,128)S(1)} %collective-permute-done.11.refs_1_), channel_id=1, source_target_pairs={{16,19},{17,18},{18,17},{19,16},{20,23},{21,22},{22,21},{23,20},{2... | collective-permute-start | bytes 3145736 | tf_op jit(solution)/shard_map/ppermute | solution.py:39
  287.8 156.2 %collective-permute-start.34 = (f32[512,1024]{1,0:T(8,128)}, f32[512,1024]{1,0:T(8,128)}, u32[]{:S(2)}, u32[]{:S(2)}) collective-permute-start(f32[512,1024]{1,0:T(8,128)} %get-tuple-element.199.refs_3_), channel_id=1, source_target_pairs={{16,20},{17,21},{18,22},{19,23},{20,16},{21,17},{22,18},{23,19},{2... | collective-permute-start | bytes 6291464 | tf_op jit(solution)/shard_map/ppermute | solution.py:39
  290.0 154.0 %collective-permute-start.38 = (f32[512,1024]{1,0:T(8,128)}, f32[512,1024]{1,0:T(8,128)S(1)}, u32[]{:S(2)}, u32[]{:S(2)}) collective-permute-start(f32[512,1024]{1,0:T(8,128)} %get-tuple-element.205), channel_id=1, source_target_pairs={{16,24},{17,25},{18,26},{19,27},{20,28},{21,29},{22,30},{23,31},{2... | collective-permute-start | bytes 6291464 | tf_op jit(solution)/shard_map/ppermute | solution.py:39
  291.5 144.2 %collective-permute-start.37 = (f32[128,2048]{1,0:T(8,128)}, f32[128,2048]{1,0:T(8,128)S(1)}, u32[]{:S(2)}, u32[]{:S(2)}) collective-permute-start(f32[128,2048]{1,0:T(8,128)} %get-tuple-element.203), channel_id=1, source_target_pairs={{16,19},{17,18},{18,17},{19,16},{20,23},{21,22},{22,21},{23,20},{2... | collective-permute-start | bytes 3145736 | tf_op jit(solution)/shard_map/ppermute | solution.py:39
  292.3 144.1 %collective-permute-start.35 = (f32[128,2048]{1,0:T(8,128)}, f32[128,2048]{1,0:T(8,128)S(1)}, u32[]{:S(2)}, u32[]{:S(2)}) collective-permute-start(f32[128,2048]{1,0:T(8,128)} %get-tuple-element.201), channel_id=1, source_target_pairs={{16,17},{17,16},{18,19},{19,18},{20,21},{21,20},{22,23},{23,22},{2... | collective-permute-start | bytes 3145736 | tf_op jit(solution)/shard_map/ppermute | solution.py:39
  294.9 143.3 %collective-permute-start.39 = (f32[512,256]{1,0:T(8,128)S(1)}, f32[512,256]{1,0:T(8,128)S(1)}, u32[]{:S(2)}, u32[]{:S(2)}) collective-permute-start(f32[512,256]{1,0:T(8,128)S(1)} %copy-done.52), channel_id=1, source_target_pairs={{16,17},{17,16},{18,19},{19,18},{20,21},{21,20},{22,23},{23,22},{2... | collective-permute-start | bytes 1572872 | tf_op jit(solution)/shard_map/ppermute | solution.py:39
  481.0 54.0 %collective-permute-start.42 = (f32[512,1024]{1,0:T(8,128)}, f32[512,1024]{1,0:T(8,128)S(1)}, u32[]{:S(2)}, u32[]{:S(2)}) collective-permute-start(f32[512,1024]{1,0:T(8,128)} %get-tuple-element.212), channel_id=1, source_target_pairs={{16,24},{17,25},{18,26},{19,27},{20,28},{21,29},{22,30},{23,31},{2... | collective-permute-start | bytes 6291464 | tf_op jit(solution)/shard_map/ppermute | solution.py:39
  481.8 65.0 %collective-permute-start.61 = (f32[512,1024]{1,0:T(8,128)}, f32[512,1024]{1,0:T(8,128)}, u32[]{:S(2)}, u32[]{:S(2)}) collective-permute-start(f32[512,1024]{1,0:T(8,128)} %get-tuple-element.238.refs_3_), channel_id=1, source_target_pairs={{16,20},{17,21},{18,22},{19,23},{20,16},{21,17},{22,18},{23,19},{2... | collective-permute-start | bytes 6291464 | tf_op jit(solution)/shard_map/ppermute | solution.py:39
  564.8 59.6 %collective-permute-start.60 = (f32[512,1024]{1,0:T(8,128)}, f32[512,1024]{1,0:T(8,128)}, u32[]{:S(2)}, u32[]{:S(2)}) collective-permute-start(f32[512,1024]{1,0:T(8,128)} %get-tuple-element.234.refs_3_), channel_id=1, source_target_pairs={{0,4},{1,5},{2,6},{3,7},{4,0},{5,1},{6,2},{7,3},{8,12},{9,13},{10,... | collective-permute-start | bytes 6291464 | tf_op jit(solution)/shard_map/ppermute | solution.py:39
  580.2 104.7 %collective-permute-start.67 = (f32[512,1024]{1,0:T(8,128)}, f32[512,1024]{1,0:T(8,128)}, u32[]{:S(2)}, u32[]{:S(2)}) collective-permute-start(f32[512,1024]{1,0:T(8,128)} %maximum_convert_fusion.3), channel_id=1, source_target_pairs={{0,4},{1,5},{2,6},{3,7},{4,0},{5,1},{6,2},{7,3},{8,12},{9,13},{10,... | collective-permute-start | bytes 6291464 | tf_op jit(solution)/shard_map/ppermute | solution.py:39
  600.9 46.0 %collective-permute-start.56 = (f32[16,256]{1,0:T(8,128)S(1)}, f32[16,256]{1,0:T(8,128)S(1)}, u32[]{:S(2)}, u32[]{:S(2)}) collective-permute-start(f32[16,256]{1,0:T(8,128)S(1)} %slice_bitcast_fusion.4), channel_id=1, source_target_pairs={{4,0},{5,1},{6,2},{7,3},{8,4},{9,5},{10,6},{11,7},{12,8},{13,9},{1... | collective-permute-start | bytes 49160 | tf_op jit(solution)/shard_map/ppermute | solution.py:39
  603.1 53.6 %collective-permute-start.57 = (f32[16,256]{1,0:T(8,128)S(1)}, f32[16,256]{1,0:T(8,128)S(1)}, u32[]{:S(2)}, u32[]{:S(2)}) collective-permute-start(f32[16,256]{1,0:T(8,128)S(1)} %slice_bitcast_fusion.4), channel_id=1, source_target_pairs={{4,1},{5,0},{6,3},{7,2},{8,5},{9,4},{10,7},{11,6},{12,9},{13,8},{1... | collective-permute-start | bytes 49160 | tf_op jit(solution)/shard_map/ppermute | solution.py:39
  604.4 52.4 %collective-permute-start.58 = (f32[16,256]{1,0:T(8,128)S(1)}, f32[16,256]{1,0:T(8,128)S(1)}, u32[]{:S(2)}, u32[]{:S(2)}) collective-permute-start(f32[16,256]{1,0:T(8,128)S(1)} %slice_bitcast_fusion.4), channel_id=1, source_target_pairs={{4,2},{5,3},{6,0},{7,1},{8,6},{9,7},{10,4},{11,5},{12,10},{13,11},... | collective-permute-start | bytes 49160 | tf_op jit(solution)/shard_map/ppermute | solution.py:39
  680.2 87.1 %collective-permute-start.72 = (f32[512,1024]{1,0:T(8,128)}, f32[512,1024]{1,0:T(8,128)}, u32[]{:S(2)}, u32[]{:S(2)}) collective-permute-start(f32[512,1024]{1,0:T(8,128)} %get-tuple-element.256.refs_3_), channel_id=1, source_target_pairs={{0,4},{1,5},{2,6},{3,7},{4,0},{5,1},{6,2},{7,3},{8,12},{9,13},{10,... | collective-permute-start | bytes 6291464 | tf_op jit(solution)/shard_map/ppermute | solution.py:39
  693.2 74.1 %collective-permute-start.71 = (f32[1024,512]{1,0:T(8,128)}, f32[1024,512]{1,0:T(8,128)}, u32[]{:S(2)}, u32[]{:S(2)}) collective-permute-start(f32[1024,512]{1,0:T(8,128)} %get-tuple-element.255), channel_id=1, source_target_pairs={{0,8},{1,9},{2,10},{3,11},{4,12},{5,13},{6,14},{7,15},{8,0},{9,1},... | collective-permute-start | bytes 6291464 | tf_op jit(solution)/shard_map/ppermute | solution.py:39
  712.7 87.3 %collective-permute-start.84 = (f32[512,1024]{1,0:T(8,128)}, f32[512,1024]{1,0:T(8,128)}, u32[]{:S(2)}, u32[]{:S(2)}) collective-permute-start(f32[512,1024]{1,0:T(8,128)} %get-tuple-element.274), channel_id=1, source_target_pairs={{0,8},{1,9},{2,10},{3,11},{4,12},{5,13},{6,14},{7,15},{8,0},{9,1},... | collective-permute-start | bytes 6291464 | tf_op jit(solution)/shard_map/ppermute | solution.py:39
  780.0 77.2 %collective-permute-start.73 = (f32[512,2048]{1,0:T(8,128)}, f32[512,2048]{1,0:T(8,128)}, u32[]{:S(2)}, u32[]{:S(2)}) collective-permute-start(f32[512,2048]{1,0:T(8,128)} %shard_map.317), channel_id=1, source_target_pairs={{16,0},{17,1},{18,2},{19,3},{20,4},{21,5},{22,6},{23,7},{24,8},{25... | collective-permute-start | bytes 12582920 | tf_op jit(solution)/shard_map/ppermute | solution.py:1360
  785.3 96.8 %collective-permute-start.77 = (f32[512,2048]{1,0:T(8,128)}, f32[512,2048]{1,0:T(8,128)}, u32[]{:S(2)}, u32[]{:S(2)}) collective-permute-start(f32[512,2048]{1,0:T(8,128)} %get-tuple-element.260), channel_id=1, source_target_pairs={{0,16},{1,17},{2,18},{3,19},{4,20},{5,21},{6,22},{7,23},{8,24},{9,... | collective-permute-start | bytes 12582920 | tf_op jit(solution)/shard_map/ppermute | solution.py:1362
  834.4 53.5 %collective-permute-start.85 = (f32[512,1024]{1,0:T(8,128)}, f32[512,1024]{1,0:T(8,128)}, u32[]{:S(2)}, u32[]{:S(2)}) collective-permute-start(f32[512,1024]{1,0:T(8,128)} %get-tuple-element.275), channel_id=1, source_target_pairs={{0,8},{1,9},{2,10},{3,11},{4,12},{5,13},{6,14},{7,15},{8,0},{9,1},... | collective-permute-start | bytes 6291464 | tf_op jit(solution)/shard_map/ppermute | solution.py:39
  (150 other events, 2176.5 us)
